TPU v7x, 32 devices: a whole 2x2x4 slice. The times are simulated.
32 devices in a mesh: rep: 8 (over z, y), shard: 4 (over x, core).
Axes of the slice: x: 2, y: 2, z: 4, core: 2. Of those that a mesh axis runs over, the one named last changes fastest.
Arguments:
- token_ids: int32 [16, 512], P('rep'), may hold values from 0 to 50271
- positions: int32 [16, 512], P('rep'), may hold values from 0 to 510, as said below
- segment_ids: int32 [16, 512], P('rep'), may hold values from 0 to 15, as said below
- pair_index: int32 [16, 8, 2], P('rep'), may hold values from -1 to 15, as said below
- embed_table: bfloat16 [50272, 1024], P('shard'), may hold values from -6 to 6
- pos_table: bfloat16 [2050, 1024], replicated, may hold values from -3 to 3
- base_qkv: bfloat16 [1024, 3072], P('rep'), may hold values from -0.1875 to 0.1875
- base_out: bfloat16 [1024, 1024], P('rep'), may hold values from -0.75 to 0.75
- base_up: bfloat16 [1024, 4096], P('rep'), may hold values from -0.1875 to 0.1875
- base_down: bfloat16 [4096, 1024], P('rep'), may hold values from -0.125 to 0.125
- base_gains: float32 [3, 1024], replicated, may hold values from 0.5 to 1.5
- base_bias: float32 [12288], replicated, may hold values from -1.75 to 1.75
- adapt_d: float32 [4, 1024, 2, 40], P('shard', 'rep'), may hold values from -0.1875 to 0.1875
- adapt_f: float32 [4, 4096, 16], P('shard', 'rep'), may hold values from -0.1875 to 0.1875
- head: float32 [4, 1024], P('shard', 'rep'), may hold values from -0.1875 to 0.1875
- mom_d: float32 [4, 1024, 2, 40], P('shard', 'rep'), may hold values from -7.6293945e-05 to 7.6293945e-05
- mom_f: float32 [4, 4096, 16], P('shard', 'rep'), may hold values from -7.6293945e-05 to 7.6293945e-05
- mom_head: float32 [4, 1024], P('shard', 'rep'), may hold values from -0.00024414062 to 0.00024414062
- err_d: float32 [4, 8, 1024, 2, 40], P('shard', 'rep'), may hold values from -0.046875 to 0.046875
- err_f: float32 [4, 8, 4096, 16], P('shard', 'rep'), may hold values from -0.046875 to 0.046875
- qstart_d: float32 [4, 2, 40, 8], P('shard'), may hold values from -6 to 6
- qstart_f: float32 [4, 16, 8], P('shard'), may hold values from -6 to 6
Outputs:
- loss_sum: float32 [], replicated
- pair_count: float32 [], replicated
- grad_norm: float32 [], replicated
- new_d: float32 [4, 1024, 2, 40], P('shard', 'rep')
- new_f: float32 [4, 4096, 16], P('shard', 'rep')
- new_head: float32 [4, 1024], P('shard', 'rep')
- new_mom_d: float32 [4, 1024, 2, 40], P('shard', 'rep')
- new_mom_f: float32 [4, 4096, 16], P('shard', 'rep')
- new_mom_head: float32 [4, 1024], P('shard', 'rep')
- new_err_d: float32 [4, 8, 1024, 2, 40], P('shard', 'rep')
- new_err_f: float32 [4, 8, 4096, 16], P('shard', 'rep')
- new_q_d: float32 [4, 2, 40, 8], P('shard')
- new_q_f: float32 [4, 16, 8], P('shard')
Inputs may be any that keep to these rules, and one draw needn't show every extreme that they name: `segment_ids`: segment ids start at 0, rise by one at each segment start, every segment holds one token or more; a sequence has an even number of segments. `positions`: positions count from 0 at each segment's first token. `pair_index`: the live slots come first; a live slot names two distinct segments of its own sequence, each segment in exactly one live slot; every sequence has one live slot or more.
All inputs are finite; a program needn't handle non-finite values.
Results may differ from a plain program's by a relative error of at most 0.0033.
Values may be sent and summed in bfloat16 or wider, within the bound.
No kernel may reach another device: no remote copies, remote signals or barrier semaphores. Data moves between devices by JAX's collectives and lax.ppermute only.
A program may use at most 160 MiB of HBM per device.

v0:
```python
import functools
import math

import jax
import jax.numpy as jnp
import numpy as np
from jax import lax
from jax.experimental import pallas as pl
from jax.experimental.pallas import tpu as pltpu
from jax.sharding import PartitionSpec as P

HEAD_DIM = 64
F32 = jnp.float32
BF16 = jnp.bfloat16
EXACT = lax.Precision.HIGHEST
CLIP = 0.01
MOMENTUM = 0.9
RATE = 1000.0
SCALE = 2.0
AXES = ("rep", "shard")


def nn(a, b, precision=None):
    return lax.dot_general(
        a, b, (((1,), (0,)), ((), ())), precision=precision, preferred_element_type=F32
    )


def nt(a, b, precision=None):
    return lax.dot_general(
        a, b, (((1,), (1,)), ((), ())), precision=precision, preferred_element_type=F32
    )


def tn(a, b, precision=None):
    return lax.dot_general(
        a, b, (((0,), (0,)), ((), ())), precision=precision, preferred_element_type=F32
    )


def iota(shape, dim):
    return lax.broadcasted_iota(jnp.int32, shape, dim)


def lanes(x, low, high):
    at = iota(x.shape, x.ndim - 1)
    return jnp.where((at >= low) & (at < high), x, jnp.zeros_like(x))


def norm_parts(x):
    centered = x - jnp.mean(x, -1, keepdims=True)
    rstd = lax.rsqrt(jnp.mean(centered * centered, -1, keepdims=True) + 1e-05)
    return centered * rstd, rstd


def norm_back(grad, gain, unit, rstd):
    g = grad * gain
    return rstd * (
        g - jnp.mean(g, -1, keepdims=True) - unit * jnp.mean(g * unit, -1, keepdims=True)
    )


def load(pieces, spots, target, sems):
    copies = []
    for index, (piece, (row, column)) in enumerate(zip(pieces, spots, strict=True)):
        rows, columns = piece.shape
        if not isinstance(row, int):
            row = pl.multiple_of(row, rows)
        if not isinstance(column, int):
            column = pl.multiple_of(column, columns)
        place = target.at[pl.ds(row, rows), pl.ds(column, columns)]
        copies.append(pltpu.make_async_copy(piece, place, sems.at[index]))
    for copy in copies:
        copy.start()

    def wait():
        for copy in copies:
            copy.wait()

    return wait


def expand_heads(x, heads):
    rows, width = x.shape
    head_of = iota((rows, width), 1) // HEAD_DIM
    return jnp.concatenate(
        [jnp.where(head_of == h, x, jnp.zeros_like(x)) for h in range(heads)], 0
    )


def collapse_heads(x, heads):
    rows, width = x.shape[0] // heads, x.shape[1]
    head_of = iota((rows, width), 1) // HEAD_DIM
    total = jnp.zeros((rows, width), F32)
    for h in range(heads):
        total = total + jnp.where(head_of == h, x[h * rows : (h + 1) * rows], 0.0)
    return total


def column(row):
    return jnp.transpose(jnp.broadcast_to(row, (8, row.shape[1])))[:, :1]


def split_kernel(ready, d_t, f_t, head, live, qkv, out, up, down, left, right, up_part, down_part, sems):
    shard = lax.axis_index("shard")
    core = shard % 2
    rows, width = out.shape
    below = left.shape[0] - rows
    half = down_part.shape[0]
    blocks = up_part.shape[1] // half
    part = width // 2
    copies = []

    def move(piece, to):
        copies.append(pltpu.make_async_copy(piece, to, sems.at[len(copies)]))
        copies[-1].start()

    for j in range(4):
        at = pl.multiple_of(core * part, part)
        piece = out.at[:, pl.ds(at, part)] if j == 3 else qkv.at[:, pl.ds(at + j * width, part)]
        move(piece, (left, right)[j // 2].at[pl.ds(0, rows), pl.ds(j % 2 * part, part)])
    move(down.at[pl.ds(pl.multiple_of(core * half, half), half), :], down_part)
    for b in range(blocks):
        at = pl.multiple_of((2 * b + core) * half, half)
        move(up.at[:, pl.ds(at, half)], up_part.at[:, pl.ds(b * half, half)])
    ready()
    left[rows:, :] = jnp.zeros((below, width), BF16)
    right[rows:, :] = jnp.zeros((below, width), BF16)
    flat = jnp.concatenate([d_t[0], d_t[1]], 0).astype(BF16)
    count = flat.shape[0] // below
    for j in range(count):
        left[rows:, j * rows : (j + 1) * rows] = flat[j * below : (j + 1) * below]
    alive = jnp.sum((live[...] >= 0).astype(F32), keepdims=True)
    two = jnp.where(iota((below, rows), 0) == 0, head[...], alive)
    left[rows:, count * rows : (count + 1) * rows] = two.astype(BF16)
    right[rows:, : f_t.shape[1]] = f_t[...].astype(BF16)
    for copy in copies:
        copy.wait()


def assemble_kernel(ready, source, *refs):
    pieces, (mat, sems) = refs[:-2], refs[-2:]
    rep, core = lax.axis_index("rep"), lax.axis_index("shard") % 2
    n = len(pieces) // 2
    rows, width = mat.shape[0] // n, mat.shape[1] // 2
    tops = [piece.at[pl.ds(0, rows), :] for piece in pieces]
    spots = [(source[rep, core, k % n] * rows, k // n * width) for k in range(2 * n)]
    load(tops, spots, mat, sems)()


def unpack_kernel(rank, rows, ready, source, *refs):
    pieces = refs[:-8]
    wide_d, own, other, head, count, flat, both, sems = refs[-8:]
    rep, core = lax.axis_index("rep"), lax.axis_index("shard") % 2
    n = len(pieces) // 2
    below, hidden = both.shape
    blocks = 10 * rank // below
    copies = []
    for k in range(n):
        r = source[rep, core, k]
        lanes_d = pl.ds(pl.multiple_of(r * rows, rows), rows)
        lanes_f = pl.ds(pl.multiple_of(r * (hidden // n), hidden // n), hidden // n)
        low = pl.ds(rows, below)
        for j in range(blocks + 1):
            place = flat.at[pl.ds(j * below, below), lanes_d]
            copies.append((pieces[k].at[low, pl.ds(j * rows, rows)], place))
        copies.append((pieces[n + k].at[low, pl.ds(0, hidden // n)], both.at[:, lanes_f]))
    copies = [pltpu.make_async_copy(a, b, sems.at[i]) for i, (a, b) in enumerate(copies)]
    for copy in copies:
        copy.start()
    for copy in copies:
        copy.wait()
    ready()
    wide_d[0] = flat[0 : 5 * rank, :]
    wide_d[1] = flat[5 * rank : 10 * rank, :]
    head[...] = flat[10 * rank : 10 * rank + 1, :].astype(F32)
    live = flat[10 * rank + 1 : 10 * rank + 2, :].astype(F32)
    count[...] = jnp.broadcast_to(jnp.sum(live, keepdims=True) / rows, count.shape)
    half = hidden // n // 2
    value = both[...]
    halves = [
        jnp.concatenate([value[:, (2 * r + c) * half : (2 * r + c + 1) * half] for r in range(n)], 1)
        for c in range(2)
    ]
    mine = (core == 0).astype(F32)
    zero, one = halves[0].astype(F32), halves[1].astype(F32)
    own[...] = (zero * mine + one * (1.0 - mine)).astype(BF16)
    other[...] = (zero * (1.0 - mine) + one * mine).astype(BF16)


def factors(ref, rank):
    value = ref[...]
    zero = jnp.zeros((4 * rank, value.shape[1]), value.dtype)
    return jnp.concatenate([zero, value[:rank]], 0), jnp.concatenate([zero, value[rank:]], 0)


def front_kernel(offset, ready, parts, pos_v, seg_v, table, gains, bias, h1, xl, hl, prow, tok):
    tokens, width = h1.shape
    slots = xl.shape[0]
    seq = (lax.axis_index("shard") + offset) % 2
    step = min(128, tokens)
    ready()
    position = pos_v[pl.ds(seq, 1), :]
    total = parts[0][...]
    for part in parts[1:]:
        total = total + part[...]
    tok[...] = total
    for i in range(tokens // step):
        rows = pl.ds(i * step, step)
        place = position[:, i * step : (i + 1) * step]
        onehot = (iota((tokens, step), 0) == place).astype(BF16)
        pos = tn(onehot, table[...])
        prow[rows, :] = pos.astype(BF16)
        unit, _ = norm_parts(tok[rows, :].astype(F32) + pos)
        h1[rows, :] = (unit * gains[0:1, :] + bias[0:1, :]).astype(BF16)
    segment = seg_v[pl.ds(seq, 1), :]
    after = pltpu.roll(jnp.broadcast_to(segment, (8, tokens)), tokens - 1, 1)[0:1]
    final = (segment != after) | (iota((1, tokens), 1) == tokens - 1)
    pick = ((segment == iota((slots, tokens), 0)) & final).astype(BF16)
    xl[...] = nn(pick, tok[...]) + nn(pick, prow[...])
    hl[...] = nn(pick, h1[...]).astype(BF16)


def kv_half(rank, h1, mat, at, u, ad, bias, kv):
    part = mat.shape[1] // 4
    width = 2 * part
    cols = pl.ds(at, part)
    for j in range(2):
        to = pl.ds(pl.multiple_of(at + j * width, part), part)
        for b in range(len(h1)):
            total = nn(h1[b][...], mat[:, (1 + j) * part : (2 + j) * part]) + bias[4 + j : 5 + j, cols]
            total = total + SCALE * nn(lanes(u[b], rank * (1 + j), rank * (2 + j)), ad[1, :, cols])
            kv[b, :, to] = total.astype(BF16)


def rows_kernel(micro, rank, ready, flush, *refs):
    seg_v, refs = refs[0], refs[1:]
    h1, hl, xl = refs[:micro], refs[micro : 2 * micro], refs[2 * micro : 3 * micro]
    ad, gains, bias, mat_own, mat_sib, kv, ukv_t, o, x1, q, p_t, u, w_out, e1, ukv = refs[3 * micro :]
    core = lax.axis_index("shard") % 2
    slots, width = hl[0].shape
    heads = width // HEAD_DIM
    tokens = h1[0].shape[0]
    part = width // 2
    mats = [(mat_own, pl.multiple_of(core * part, part)), (mat_sib, pl.multiple_of((1 - core) * part, part))]
    ready(ad, *h1)
    down, up = ad[0], ad[1]
    for b in range(micro):
        ukv[b] = lanes(nt(h1[b][...], down).astype(BF16), rank, 3 * rank)
        ukv_t[b] = nt(down, h1[b][...]).astype(BF16)
    ready(mat_own, bias)
    kv_half(rank, h1, *mats[0], ukv, ad, bias, kv)
    ready()
    kv_half(rank, h1, *mats[1], ukv, ad, bias, kv)
    flush(0)
    flush(1)
    for mat, at in mats:
        w_out[:, pl.ds(at, part)] = mat[:, 3 * part :]
    flush(7)
    h_last = jnp.concatenate([h[...] for h in hl], 0)
    x_last = jnp.concatenate([x[...] for x in xl], 0)
    u_q = lanes(nt(h_last, down).astype(BF16), 0, rank)
    for mat, at in mats:
        cols = pl.ds(at, part)
        total = nn(h_last, mat[:, :part]) + bias[3:4, cols] + SCALE * nn(u_q, ad[1, :, cols])
        q[:, cols] = total.astype(BF16)
    q_all = q[...]
    parts = []
    for b in range(micro):
        wide_q = expand_heads(q_all[b * slots : (b + 1) * slots], heads)
        scores = HEAD_DIM ** (-0.5) * nt(kv[b, :, :width], wide_q)
        segment = column(seg_v[pl.ds((core + b) % 2, 1), :])
        inside = segment == iota((tokens, heads * slots), 1) % slots
        scores = jnp.where(inside, scores, -1000000000.0)
        e = jnp.exp(scores - jnp.max(scores, 0, keepdims=True))
        probs = e / jnp.sum(e, 0, keepdims=True)
        p_t[b] = probs
        parts.append(collapse_heads(tn(probs.astype(BF16), kv[b, :, width:]), heads))
    flush(5)
    o_all = jnp.concatenate(parts, 0).astype(BF16)
    o[...] = o_all
    u_o = lanes(nt(o_all, down).astype(BF16), 3 * rank, 4 * rank)
    mid = x_last + nn(o_all, w_out[...]) + bias[6:7, :] + SCALE * nn(u_o, up)
    x1[...] = mid
    unit, _ = norm_parts(mid)
    h2 = (unit * gains[1:2, :] + bias[1:2, :]).astype(BF16)
    u_up = lanes(nt(h2, down).astype(BF16), 4 * rank, 5 * rank)
    e1[:, :width] = h2
    e1[:, width:] = jnp.zeros_like(e1[:, width:])
    e1[:, width : width + 5 * rank] = u_up
    u[...] = u_q + u_o + u_up


def up_kernel(rank, ready, source, own, sib, f_own, f_sib, bias, *refs):
    weights = refs[:-4]
    f, a, wide, sems = refs[-4:]
    width = wide.shape[0]
    rep, core = lax.axis_index("rep"), lax.axis_index("shard") % 2
    height = weights[0].shape[0]
    spots = [(source[rep, core, k] * height, 0) for k in range(len(weights))]
    tops = weights
    loaded = load(tops, spots, wide, sems)
    ready()
    h2 = jnp.concatenate([own[:, :width], sib[:, :width]], 0)
    lane = 5 * rank
    extra = jnp.concatenate(
        [
            nn(own[:, width : width + lane], factors(f_own, rank)[1]),
            nn(sib[:, width : width + lane], factors(f_sib, rank)[1]),
        ],
        0,
    )
    loaded()
    total = nn(h2, wide[...]) + bias[...] + SCALE * extra
    f[...] = total
    a[...] = jax.nn.gelu(total, approximate=True).astype(BF16)


def down_kernel(rank, ready, source, a, f_own, f_sib, *refs):
    weights = refs[:-4]
    mine, send, wide, sems = refs[-4:]
    width = wide.shape[1]
    rep, core = lax.axis_index("rep"), lax.axis_index("shard") % 2
    height = weights[0].shape[0]
    spots = [(source[rep, core, k] * height, 0) for k in range(len(weights))]
    ends = weights
    loaded = load(ends, spots, wide, sems)
    ready()
    rows = a.shape[0] // 2
    lane = 5 * rank
    for out, low, factor in ((mine, 0, f_own), (send, rows, f_sib)):
        out[:, width:] = jnp.zeros_like(out[:, width:])
        out[:, width : width + lane] = nt(a[low : low + rows, :], factors(factor, rank)[0])
    loaded()
    y = nn(a[...], wide[...])
    mine[:, :width] = y[:rows]
    send[:, :width] = y[rows:]


def score_kernel(rank, ready, x1, mine, recv, ad, gains, bias, head, x2, u_dn, score):
    ready()
    width = x1.shape[1]
    lane = 5 * rank
    u = (mine[:, width : width + lane] + recv[:, width : width + lane]).astype(BF16)
    u_dn[...] = u
    end = x1[...] + mine[:, :width] + recv[:, :width] + bias[11:12, :] + SCALE * nn(u, ad[1])
    x2[...] = end
    unit, _ = norm_parts(end)
    token = jnp.sum((unit * gains[2:3, :] + bias[2:3, :]) * head[...], -1, keepdims=True)
    score[...] = jnp.broadcast_to(token, score.shape)


def loss_kernel(rank, members, ready, *refs):
    scores = refs[:members]
    x2, u_dn, pairs, count, ad, gains, bias, head = refs[members : members + 8]
    e2, g_end, g_dn, small = refs[members + 8 :]
    ready()
    rows, width = x2.shape
    half = rows // 2

    def value(m):
        if m % 2 == 0:
            return scores[m][...]
        return jnp.concatenate([scores[m][half:, :], scores[m][:half, :]], 0)

    level = [value(m) for m in range(members)]
    while len(level) > 1:
        level = [level[i] + level[i + 1] for i in range(0, len(level), 2)]
    mean_reward = level[0][:, :1] / members
    at = iota((rows, pairs.shape[1]), 0)
    pick = (at == pairs[0:1, :]).astype(F32) - (at == pairs[1:2, :]).astype(F32)
    live = (pairs[0:1, :] >= 0).astype(F32)
    diff = jnp.sum(pick * mean_reward, 0, keepdims=True)
    terms = live * jax.nn.softplus(-diff)
    grad_diff = -live * jax.nn.sigmoid(-diff) / count[:, :1]
    grad_score = jnp.sum(pick * grad_diff, -1, keepdims=True) / members
    unit, rstd = norm_parts(x2[...])
    final = unit * gains[2:3, :] + bias[2:3, :]
    small[...] = jnp.zeros_like(small)
    small[0:1, :] = jnp.sum(final * grad_score, 0, keepdims=True)
    small[1:2, :] = jnp.broadcast_to(jnp.sum(terms, -1, keepdims=True), (1, width))
    end = norm_back(grad_score * head[...], gains[2:3, :], unit, rstd)
    g_end[...] = end
    g_ff = end.astype(BF16)
    left = lanes((SCALE * nt(g_ff, ad[1])).astype(BF16), 4 * rank, 5 * rank)
    g_dn[...] = SCALE * tn(u_dn[...], g_ff)
    e2[:, :width] = g_ff
    e2[:, width:] = jnp.zeros_like(e2[:, width:])
    e2[:, width : width + 5 * rank] = left


def ffn_back_kernel(rank, ready, own, sib, e1_own, e1_sib, f, a, f_own, f_sib, wide_u, wide_d,
                    mine, send, gf_mine, gf_send):
    width = wide_u.shape[0]
    lane = 5 * rank
    ready()
    rows = own.shape[0]
    x = f[...]
    c0, c1 = math.sqrt(2.0 / math.pi), 0.044715
    t = jnp.tanh(c0 * (x + c1 * x * x * x))
    slope = 0.5 * (1.0 + t) + 0.5 * x * (1.0 - t * t) * (c0 * (1.0 + 3.0 * c1 * x * x))
    left_own, left_sib = own[:, width : width + lane], sib[:, width : width + lane]
    u_own, u_sib = e1_own[:, width : width + lane], e1_sib[:, width : width + lane]
    g_ff = jnp.concatenate([own[:, :width], sib[:, :width]], 0)
    pair_own, pair_sib = factors(f_own, rank), factors(f_sib, rank)
    extra = jnp.concatenate([nn(left_own, pair_own[0]), nn(left_sib, pair_sib[0])], 0)
    g_a = (nt(g_ff, wide_d[...]) + extra).astype(BF16)
    g_f = (g_a.astype(F32) * slope).astype(BF16)
    g_h = nt(g_f, wide_u[...])
    parts = (
        (mine, gf_mine, 0, pair_own, left_own, u_own),
        (send, gf_send, rows, pair_sib, left_sib, u_sib),
    )
    for out, _, low, factor, _, _ in parts:
        out[:, :width] = g_h[low : low + rows]
        out[:, width:] = jnp.zeros_like(out[:, width:])
        out[:, width : width + lane] = SCALE * nt(g_f[low : low + rows], factor[1])
    for _, gout, low, _, left, u in parts:
        gout[0:rank, :] = tn(left, a[low : low + rows, :])[4 * rank :]
        gout[rank:, :] = SCALE * tn(u, g_f[low : low + rows])[4 * rank :]


def factor_kernel(rank, half, ready, mine, other, err, start, mat, left):
    ready()
    core = lax.axis_index("shard") % 2
    first = (core == 0).astype(F32)
    even = mine[...] * first + other[...] * (1.0 - first)
    odd = mine[...] * (1.0 - first) + other[...] * first
    parts = []
    for r in range(mine.shape[1] // half):
        cut = slice(r * half, (r + 1) * half)
        parts += [even[:, cut], odd[:, cut]]
    mat[...] = jnp.concatenate(parts, 1) + err[...]
    left[...] = nn(start[...], mat[...], EXACT)


def rows_back_kernel(micro, rank, ready, *refs):
    mine, recv, g_end, g_dn, small, x1, e1, u, o, q, p_t, kv, ukv_t = refs[:13]
    hl = refs[13 : 13 + micro]
    h1 = refs[13 + micro : 13 + 2 * micro]
    ad, gains, err, start, w_out, mat, left = refs[13 + 2 * micro :]
    ready(ad, gains)
    rows, width = x1.shape
    slots = rows // micro
    heads = width // HEAD_DIM
    lane = 5 * rank
    down, up = ad[0], ad[1]
    h2 = e1[:, :width]
    u_rows = u[...]
    g_u = (mine[:, width : width + lane] + recv[:, width : width + lane]).astype(BF16)
    g_h2 = (mine[:, :width] + recv[:, :width] + nn(g_u, down)).astype(BF16)
    grad_in = tn(g_u, h2)
    unit, rstd = norm_parts(x1[...])
    g_mid = g_end[...] + norm_back(g_h2.astype(F32), gains[1:2, :], unit, rstd)
    g_att = g_mid.astype(BF16)
    grad_out = g_dn[...] + SCALE * tn(lanes(u_rows, 3 * rank, 4 * rank), g_att)
    g_ol = lanes((SCALE * nt(g_att, up)).astype(BF16), 3 * rank, 4 * rank)
    grad_in = grad_in + tn(g_ol, o[...])
    g_o = (nt(g_att, w_out[...]) + nn(g_ol, down)).astype(BF16)
    ready()
    scale = HEAD_DIM ** (-0.5)

    def row_part(x, low, high):
        at = iota(x.shape, 0)
        return jnp.where((at >= low) & (at < high), x, jnp.zeros_like(x))

    for b in range(micro):
        pick = slice(b * slots, (b + 1) * slots)
        wide_g = expand_heads(g_o[pick], heads)
        wide_q = expand_heads(q[pick, :], heads)
        probs = p_t[b]
        g_p = nt(kv[b, :, width:], wide_g)
        g_s = (probs * (g_p - jnp.sum(probs * g_p, 0, keepdims=True))).astype(BF16)
        g_q = (scale * collapse_heads(tn(g_s, kv[b, :, :width]), heads)).astype(BF16)
        g_k = (scale * nn(g_s, wide_q)).astype(BF16)
        g_v = nn(probs.astype(BF16), wide_g).astype(BF16)
        u_q = lanes(u_rows[pick], 0, rank)
        u_k = row_part(ukv_t[b], rank, 2 * rank)
        u_v = row_part(ukv_t[b], 2 * rank, 3 * rank)
        grad_out = grad_out + SCALE * (tn(u_q, g_q) + nn(u_k, g_k) + nn(u_v, g_v))
        g_uq = lanes((SCALE * nt(g_q, up)).astype(BF16), 0, rank)
        g_ukv = row_part((SCALE * nt(up, g_k)).astype(BF16), rank, 2 * rank) + row_part(
            (SCALE * nt(up, g_v)).astype(BF16), 2 * rank, 3 * rank
        )
        grad_in = grad_in + tn(g_uq, hl[b][...]) + nn(g_ukv, h1[b][...])
    mat[0] = grad_in + err[0]
    mat[1] = grad_out + err[1]
    first = start.shape[1]
    left[0:first, :] = nn(start[0], mat[0], EXACT)
    left[first : 2 * first, :] = nn(start[1], mat[1], EXACT)
    left[2 * first :, :] = small[...]


def orthonormal_rows(refs):
    count = refs[0].shape[0]
    for k in range(count):
        for ref in refs:
            row = ref[k : k + 1, :]
            row = row * lax.rsqrt(jnp.sum(row * row, -1, keepdims=True) + 1e-06)
            if k + 1 < count:
                block = ref[...]
                at = iota(block.shape, 0)
                dots = jnp.sum(block * row, -1, keepdims=True)
                block = jnp.where(at > k, block - dots * row, block)
                ref[...] = jnp.where(at == k, row, block)
            else:
                ref[k : k + 1, :] = row


def ortho_kernel(rank, ready, d_a, d_b, f_a, f_b, mat_d, mat_f, ph_d, ph_f, head, note):
    count = rank
    for j in range(2):
        part = slice(j * count, (j + 1) * count)
        ph_d[j] = d_a[part, :] + d_b[part, :]
    ph_f[...] = f_a[...] + f_b[...]
    rest = d_a[2 * count :, :] + d_b[2 * count :, :]
    refs = (ph_d.at[0], ph_d.at[1], ph_f)
    orthonormal_rows(refs)
    ready()
    grad = rest[0:1, :]
    head[...] = grad
    parts = []
    for ref, mat in zip(refs, (mat_d.at[0], mat_d.at[1], mat_f), strict=True):
        parts.append(nt(ref[...], mat[...], EXACT))
    for ref in refs:
        parts.append(nt(ref[...], ref[...], EXACT))
    parts.append(jnp.broadcast_to(jnp.sum(grad * grad, keepdims=True), (count, 1)))
    parts.append(jnp.broadcast_to(rest[1:2, :1], (count, 1)))
    used = sum(x.shape[1] for x in parts)
    parts.append(jnp.zeros((count, 128 - used), F32))
    own = jnp.concatenate(parts, 1)

    @pl.loop(0, note.shape[0])
    def _(i):
        note[i] = own


def final_kernel(rank, n, m, ready, notes, ph_d, ph_f, ph_do, ph_fo, ghead, mat_d, mat_f,
                 wd, wf, wh, md, mf, mh,
                 nd, nf, nh, nmd, nmf, nmh, err_d, err_f, q_d, q_f, mean_loss, norm):
    ready()
    shard = lax.axis_index("shard")
    count = rank
    sizes = (5 * rank, 5 * rank, 2 * rank)
    total = jnp.zeros((1, 1), F32)
    loss = jnp.zeros((1, 1), F32)
    own = jnp.zeros((count, 128), F32)
    for s in range(m):
        block = notes[s]
        for r in range(1, n):
            block = block + notes[r * m + s]
        own = jnp.where(shard == s, block, own)
        note = notes[s]
        at, gram = 0, sum(sizes)
        for size in sizes:
            right = block[:, at : at + size]
            inner = note[:, gram : gram + count]
            total = total + jnp.sum(right * nn(inner, right, EXACT), keepdims=True)
            at += size
            gram += count
        total = total + note[0:1, gram : gram + 1]
        loss = loss + note[0:1, gram + 1 : gram + 2]
    grad_norm = jnp.sqrt(total)
    clip = jnp.minimum(1.0, CLIP / (grad_norm + 1e-06))
    mean_loss[...] = loss / m
    norm[...] = grad_norm
    at = 0
    for j in range(2):
        right = own[:, at : at + sizes[j]]
        q_d[j] = right
        at += sizes[j]
        err_d[j] = mat_d[j] - tn(right, ph_d[j], EXACT) * (1.0 / n)
        fresh = MOMENTUM * md[j] + clip * tn(right, ph_do[j], EXACT)
        nmd[j] = fresh
        nd[j] = wd[j] - RATE * fresh
    right = own[:, at : at + sizes[2]]
    q_f[...] = right
    err_f[...] = mat_f[...] - tn(right, ph_f[...], EXACT) * (1.0 / n)
    fresh = MOMENTUM * mf[...] + clip * tn(right, ph_fo[...], EXACT)
    nmf[...] = fresh
    nf[...] = wf[...] - RATE * fresh
    fresh = MOMENTUM * mh[...] + clip * ghead[...]
    nmh[...] = fresh
    nh[...] = wh[...] - RATE * fresh


class Raw:
    def __init__(self, array):
        self.array = array


class Scalars(Raw):
    pass


class Far(Raw):
    pass


class Fresh(Raw):
    pass


class Part:
    def __init__(self, array, rows):
        self.array, self.rows = array, rows


class Kept:
    def __init__(self, shape, dtype):
        self.shape, self.dtype = tuple(shape), dtype


class Placed(Kept):
    pass


def call(body, outs, args, scratch=(), vmem=60, name=None, groups=None, aliases=None, flushes=False):
    arrays, specs, staged = [], [], []
    for arg in args:
        arrays.append(arg.array if isinstance(arg, Raw | Part) else arg)
        space = pl.ANY
        if isinstance(arg, Scalars):
            space = pltpu.SMEM
        elif isinstance(arg, Fresh):
            space = pltpu.VMEM
        elif isinstance(arg, Far):
            space = pltpu.HBM
        specs.append(pl.BlockSpec(memory_space=space))
        if isinstance(arg, Part):
            staged.append(pltpu.VMEM((arg.rows, *arg.array.shape[1:]), arg.array.dtype))
        elif not isinstance(arg, Raw):
            staged.append(pltpu.VMEM(arg.shape, arg.dtype))
    results = [pltpu.VMEM(o.shape, o.dtype) for o in outs if not isinstance(o, Kept)]

    def kernel(*refs):
        ins, refs = refs[: len(args)], refs[len(args) :]
        targets, refs = refs[: len(outs)], refs[len(outs) :]
        held, refs = refs[: len(staged)], refs[len(staged) :]
        buffers, refs = refs[: len(results)], refs[len(results) :]
        extra, sems = refs[:-1], refs[-1]
        copies, given, i = {}, [], 0
        for arg, ref in zip(args, ins, strict=True):
            if isinstance(arg, Raw):
                given.append(ref)
                continue
            origin = ref.at[pl.ds(0, arg.rows)] if isinstance(arg, Part) else ref
            copies[id(held[i])] = pltpu.make_async_copy(origin, held[i], sems.at[i])
            given.append(held[i])
            i += 1
        for copy in copies.values():
            copy.start()

        def ready(*some):
            for key in [id(r) for r in some] or list(copies):
                copies.pop(key).wait()

        local, back, i = [], {}, 0
        for j, out in enumerate(outs):
            if isinstance(out, Kept):
                local.append(targets[j])
                continue
            local.append(buffers[i])
            back[j] = pltpu.make_async_copy(buffers[i], targets[j], sems.at[len(staged) + i])
            i += 1
        def flush(j):
            back[j].start()
            begun.append(j)

        begun = []
        if groups:
            given = [given[:groups], *given[groups:]]
        body(ready, *((flush,) if flushes else ()), *given, *local, *extra)
        for j, copy in back.items():
            if j not in begun:
                copy.start()
        for copy in back.values():
            copy.wait()

    def place(out):
        if type(out) is Kept:
            return pltpu.VMEM
        return pl.ANY if isinstance(out, Kept) else pltpu.HBM

    return pl.pallas_call(
        kernel,
        out_shape=tuple(jax.ShapeDtypeStruct(o.shape, o.dtype) for o in outs),
        in_specs=specs,
        out_specs=tuple(pl.BlockSpec(memory_space=place(o)) for o in outs),
        scratch_shapes=[
            *staged, *results, *scratch, pltpu.SemaphoreType.DMA((max(1, len(staged) + len(results)),)),
        ],
        compiler_params=pltpu.CompilerParams(vmem_limit_bytes=vmem << 20),
        cost_estimate=pl.CostEstimate(flops=0, bytes_accessed=0, transcendentals=0),
        input_output_aliases=aliases or {},
        name=name,
    )(*arrays)


def shaped(shape, dtype):
    return jax.ShapeDtypeStruct(tuple(shape), dtype)


def ring_order(count):
    side = math.isqrt(count // 2)
    if side < 2 or 2 * side * side != count:
        return list(range(count))
    depth = 2 * side
    cells = []
    for z in range(depth):
        ys = range(1, side) if z % 2 == 0 else range(side - 1, 0, -1)
        cells += [(z, y) for y in ys]
    cells += [(z, 0) for z in range(depth - 1, -1, -1)]
    return [z * side + y for z, y in cells]


def pairs_of(n, m, move):
    return [(r * m + s, t[0] * m + t[1]) for r in range(n) for s in range(m) for t in [move(r, s)]]


def on_device(n, m, *args):
    (
        token_ids, positions, segment_ids, pair_index, embed_table, pos_table,
        base_qkv, base_out, base_up, base_down, base_gains, base_bias,
        adapt_d, adapt_f, head, mom_d, mom_f, mom_head, err_d, err_f, qstart_d, qstart_f,
    ) = args
    micro, tokens = token_ids.shape
    held, width = embed_table.shape
    pairs = pair_index.shape[1]
    slots = 2 * pairs
    rows = micro * slots
    hidden = base_up.shape[1]
    rank = adapt_f.shape[2] // 2
    heads = width // HEAD_DIM
    rd, rf = base_up.shape[0], base_down.shape[0]
    half = rf // 2
    own_hidden = hidden // 2
    rep, shard = lax.axis_index("rep"), lax.axis_index("shard")
    core = shard % 2

    order = ring_order(n)
    place = {r: i for i, r in enumerate(order)}
    around = pairs_of(
        n, m, lambda r, s: (order[(place[r] + (1 if s % 2 == 0 else -1)) % n], s)
    )
    turns = [
        [[order[(place[r] + (-k if c == 0 else k)) % n] for k in range(n)] for c in range(2)]
        for r in range(n)
    ]
    source = Scalars(jnp.asarray(np.array(turns, np.int32)))

    def send(x, perm):
        return lax.ppermute(x, AXES, perm)

    def across(x, mask):
        return send(x, pairs_of(n, m, lambda r, s: (r, s ^ mask)))

    def ring(x):
        out = []
        for _ in range(n - 1):
            x = send(x, around)
            out.append(x)
        return out

    def pick(x, index, axis):
        return lax.dynamic_index_in_dim(x, index, axis, keepdims=False)

    d_t = adapt_d[0].transpose(1, 2, 0)
    f_t = adapt_f[0].T
    below = 2 * rank
    live = pair_index[..., 0].reshape(1, micro * pairs)
    whole_blocks = rd % 128 == 0 and half % 128 == 0
    if whole_blocks:
        left, right, up_part, down_part = call(
            split_kernel,
            [shaped((rd + below, width), BF16), shaped((rd + below, width), BF16),
             shaped((rd, own_hidden), BF16), shaped((half, width), BF16)],
            [d_t, f_t, head, live, Raw(base_qkv), Raw(base_out), Raw(base_up), Raw(base_down)],
            [pltpu.SemaphoreType.DMA((n + 5,))],
            vmem=56, name="split",
        )
    else:
        two = jnp.concatenate([head, jnp.broadcast_to(jnp.sum((live >= 0).astype(F32)), (below - 1, rd))], 0)
        flat = [x for x in d_t.reshape(10 * rank // below, below, rd)]
        first = jnp.concatenate([base_qkv, base_out], 1).reshape(rd, 4, 2, width // 2)
        first = pick(first, core, 2).reshape(rd, 2, width)
        sides = []
        for side, extra in enumerate((jnp.concatenate([*flat, two], 1), f_t)):
            extra = jnp.pad(extra.astype(BF16), ((0, 0), (0, width - extra.shape[1])))
            sides.append(jnp.concatenate([first[:, side], extra], 0))
        left, right = sides
        up_part = pick(base_up.reshape(rd, n, 2, half), core, 2).reshape(rd, own_hidden)
        down_part = pick(base_down.reshape(2, half, width), core, 0)

    def after(x, *others):
        return pl.pallas_call(
            lambda *refs: None,
            out_shape=jax.ShapeDtypeStruct(x.shape, x.dtype),
            in_specs=[pl.BlockSpec(memory_space=pl.ANY)] * (1 + len(others)),
            out_specs=pl.BlockSpec(memory_space=pl.ANY),
            input_output_aliases={0: 0},
            cost_estimate=pl.CostEstimate(flops=0, bytes_accessed=0, transcendentals=0),
            name="after",
        )(x, *others)

    def lookup(*start):
        ids = jnp.stack([pick(token_ids, (core + b) % micro, 0) for b in range(micro)])
        ids = after(ids, *start)
        near = ids - shard * held
        inside = (near >= 0) & (near < held)
        found = jnp.take(embed_table, jnp.clip(near, 0, held - 1), axis=0)
        found = jnp.where(inside[..., None], found, jnp.zeros_like(found))
        return found[0], found[1]

    def shared(own, given, *others):
        own = own + across(after(given, *others), 1)
        mask = 2
        while mask < m // 2:
            own = own + across(own, mask)
            mask *= 2
        return own, across(own, mask) if m > 2 else own

    bias = base_bias.reshape(-1, width)
    bias_1 = pick(base_bias[7 * width : 7 * width + hidden].reshape(n, 2, half), core, 1)
    bias_1 = bias_1.reshape(1, own_hidden)
    local = (jnp.arange(micro) + core) % micro * slots
    pair_rows = jnp.where(pair_index >= 0, pair_index + local[:, None, None], -1)
    pair_rows = pair_rows.reshape(micro * pairs, 2).T

    pos_rows = pos_table[:tokens]

    lefts, rights, ups, downs = [left], [right], [up_part], [down_part]
    for k in range(1, n):
        gate = []
        if k == 9:
            gate = [ups[1], downs[1]]
        if k == 4:
            gate = [tok_own]
        if k == 7:
            gate = [tok_far]
        if gate:
            lefts[-1], rights[-1] = after(lefts[-1], *gate), after(rights[-1], *gate)
        lefts.append(send(lefts[-1], around))
        rights.append(send(rights[-1], around))
        if k == 1:
            ups[-1], downs[-1] = after(ups[-1], lefts[1]), after(downs[-1], lefts[1])
            ups.append(send(ups[-1], around))
            downs.append(send(downs[-1], around))
            own, given = lookup(lefts[1], rights[1], bias, bias_1, pos_rows, pair_rows)
        if k == 2:
            tok_own, tok_far = shared(own, given, lefts[2], rights[2], ups[1], downs[1])

    def behind(low, high, *gate):
        for k in range(low, min(high, n)):
            if gate:
                ups[-1], downs[-1] = after(ups[-1], *gate), after(downs[-1], *gate)
            gate = ()
            ups.append(send(ups[-1], around))
            downs.append(send(downs[-1], around))

    behind(2, 4, lefts[5])
    parts = [tok_own, tok_far] if m > 2 else [tok_own]
    both = tok_own + tok_far if m > 2 else tok_own
    toks = [parts, [across(both, 1)]]

    lefts[-1] = after(lefts[-1], ups[2], downs[2])
    step_a = [*lefts, *rights]
    if whole_blocks:
        (mat_own,) = call(
            assemble_kernel,
            [shaped((width, 2 * width), BF16)],
            [source, *[Far(x) for x in step_a]],
            [pltpu.SemaphoreType.DMA((2 * n,))],
            vmem=58, name="assemble",
        )
        wide_d, f_own, f_other, wide_head, count_row = call(
            functools.partial(unpack_kernel, rank, rd),
            [shaped((2, 5 * rank, width), BF16), shaped((2 * rank, own_hidden), BF16),
             Kept((2 * rank, own_hidden), BF16), shaped((1, width), F32), shaped((1, 128), F32)],
            [source, *[Far(x) for x in step_a]],
            [pltpu.VMEM((10 * rank + below, width), BF16), pltpu.VMEM((below, hidden), BF16),
             pltpu.SemaphoreType.DMA((n * (10 * rank // below + 2),))],
            vmem=52, name="unpack",
        )
    else:
        turned = jnp.asarray(np.argsort(np.array(turns, np.int32), -1).astype(np.int32))
        place_at = lax.dynamic_slice(turned, (rep, core, 0), (1, 1, n)).reshape(n)
        steps_l, steps_r = [
            jnp.stack([pick(jnp.stack(x), place_at[r], 0) for r in range(n)]) for x in (lefts, rights)
        ]
        mat_own = jnp.concatenate([steps_l[:, :rd], steps_r[:, :rd]], 2).reshape(width, 2 * width)
        count_d = 10 * rank // below
        wide_d = steps_l[:, rd:, : count_d * rd].reshape(n, below, count_d, rd)
        wide_d = wide_d.transpose(2, 1, 0, 3).reshape(2, 5 * rank, width)
        wide_f = steps_r[:, rd:, :rf].reshape(n, 2 * rank, 2, half)
        wide_f = wide_f.transpose(2, 1, 0, 3).reshape(2, 2 * rank, own_hidden)
        f_own, f_other = pick(wide_f, core, 0), pick(wide_f, 1 - core, 0)
        last = steps_l[:, rd:, count_d * rd : (count_d + 1) * rd].astype(F32)
        wide_head = last[:, 0].reshape(1, width)
        count_row = jnp.broadcast_to(jnp.sum(last[:, 1, 0]), (1, 128))
    count = count_row[0, 0]
    behind(4, 5, mat_own)
    f_sib = across(f_other, 1)
    mat_sib = across(mat_own, 1)

    h1, xl, hl = [], [], []
    for b in range(micro):
        a, x, h = call(
            functools.partial(front_kernel, b),
            [Kept((tokens, width), BF16), Kept((slots, width), F32), Kept((slots, width), BF16)],
            [*toks[b], positions, segment_ids, pos_rows, base_gains, bias],
            [pltpu.VMEM((tokens, width), BF16), pltpu.VMEM((tokens, width), BF16)],
            groups=len(toks[b]), vmem=14, name="front",
        )
        h1.append(a)
        xl.append(x)
        hl.append(h)

    behind(5, 7, *hl, wide_d)
    kv, ukv_t, o, x1, q, p_t, u, w_out, e1 = call(
        functools.partial(rows_kernel, micro, rank),
        [shaped((micro, tokens, 2 * width), BF16), shaped((micro, 5 * rank, tokens), BF16),
         shaped((rows, width), BF16), shaped((rows, width), F32), shaped((rows, width), BF16),
         shaped((micro, tokens, heads * slots), F32), shaped((rows, 5 * rank), BF16),
         shaped((width, width), BF16), shaped((rows, width + 128), BF16)],
        [segment_ids, *h1, *hl, *xl, wide_d, base_gains, bias, mat_own, mat_sib],
        [pltpu.VMEM((micro, tokens, 5 * rank), BF16)],
        vmem=60, flushes=True, name="rows",
    )
    behind(7, n, o)
    ups, downs = [[Far(y) for y in x] for x in (ups, downs)]
    e1_sib = across(e1, 1)
    f, a, w_up = call(
        functools.partial(up_kernel, rank),
        [Kept((2 * rows, own_hidden), F32), Kept((2 * rows, own_hidden), BF16),
         Kept((width, own_hidden), BF16)],
        [source, Fresh(e1), Fresh(e1_sib), f_own, f_sib, bias_1, *ups],
        [pltpu.SemaphoreType.DMA((n,))],
        vmem=10, name="up",
    )
    y_mine, y_send, w_down = call(
        functools.partial(down_kernel, rank),
        [Kept((rows, width + 128), F32)] * 2 + [Kept((own_hidden, width), BF16)],
        [source, Fresh(a), f_own, f_sib, *downs],
        [pltpu.SemaphoreType.DMA((n,))],
        vmem=10, name="down",
    )
    x2, u_dn, score = call(
        functools.partial(score_kernel, rank),
        [Kept((rows, width), F32), Kept((rows, 5 * rank), BF16), Kept((rows, 128), F32)],
        [Fresh(x1), Fresh(y_mine), Fresh(across(y_send, 1)), wide_d, base_gains, bias, wide_head],
        vmem=10, name="score",
    )
    scores = [score] + [across(score, k) for k in range(1, m)]
    e2, g_end, g_dn, small = call(
        functools.partial(loss_kernel, rank, m),
        [Kept((rows, width + 128), BF16), Kept((rows, width), F32), Kept((5 * rank, width), F32),
         Kept((8, width), F32)],
        [*[Fresh(x) for x in scores], Fresh(x2), Fresh(u_dn), pair_rows, count_row, wide_d, base_gains, bias, wide_head],
        vmem=10, name="loss",
    )
    y_mine, y_send, gf_mine, gf_send = call(
        functools.partial(ffn_back_kernel, rank),
        [Kept((rows, width + 128), F32)] * 2 + [Kept((2 * rank, own_hidden), F32)] * 2,
        [Fresh(e2), Fresh(across(e2, 1)), Fresh(e1), Fresh(e1_sib), Fresh(f), Fresh(a), f_own, f_sib,
         Fresh(w_up), Fresh(w_down)],
        vmem=14, name="ffn_back",
    )
    mat_f, left_f = call(
        functools.partial(factor_kernel, rank, half),
        [Kept((2 * rank, hidden), F32), Kept((rank, hidden), F32)],
        [Fresh(gf_mine), Fresh(across(gf_send, 1)), err_f[0, 0].T, qstart_f[0].T],
        vmem=10, name="factor_f",
    )
    mat_d, left_d = call(
        functools.partial(rows_back_kernel, micro, rank),
        [Kept((2, 5 * rank, width), F32), Kept((2 * rank + 8, width), F32)],
        [Fresh(y_mine), Fresh(across(y_send, 1)), Fresh(g_end), Fresh(g_dn), Fresh(small),
         *[Fresh(x) for x in (x1, e1, u, o, q, p_t, kv, ukv_t, *hl, *h1)],
         wide_d, base_gains, err_d[0, 0].transpose(1, 2, 0), qstart_d[0].transpose(0, 2, 1), Fresh(w_out)],
        vmem=26, name="rows_back",
    )

    def rep_parts(x):
        bit, part = 1, jnp.zeros_like(x)
        while bit < n:
            part = send(x, pairs_of(n, m, lambda r, s, bit=bit: (r ^ bit, s)))
            bit *= 2
            if bit < n:
                x = x + part
        return Fresh(x), Fresh(part)

    ph_d, ph_f, total_head, note = call(
        functools.partial(ortho_kernel, rank),
        [Kept((2, rank, width), F32), Kept((rank, hidden), F32), Kept((1, width), F32),
         Kept((n * m, rank, 128), F32)],
        [*rep_parts(left_d), *rep_parts(left_f), Fresh(mat_d), Fresh(mat_f)],
        vmem=10, name="ortho",
    )
    notes = lax.all_to_all(note, AXES, 0, 0)
    own_ph_d = lax.dynamic_slice_in_dim(ph_d, rep * rd, rd, 2)
    own_ph_f = lax.dynamic_slice_in_dim(ph_f, rep * rf, rf, 1)
    own_head = lax.dynamic_slice_in_dim(total_head, rep * rd, rd, 1)
    nd, nf, nh, nmd, nmf, nmh, new_err_d, new_err_f, q_d, q_f, loss_sum, norm = call(
        functools.partial(final_kernel, rank, n, m),
        [shaped((2, 5 * rank, rd), F32), shaped((2 * rank, rf), F32), shaped((1, rd), F32)] * 2
        + [shaped((2, 5 * rank, width), F32), shaped((2 * rank, hidden), F32),
           shaped((2, rank, 5 * rank), F32), shaped((rank, 2 * rank), F32), shaped((1, 1), F32), shaped((1, 1), F32)],
        [Fresh(notes), Fresh(ph_d), Fresh(ph_f), Fresh(own_ph_d), Fresh(own_ph_f), Fresh(own_head),
         Fresh(mat_d), Fresh(mat_f), d_t, f_t, head, mom_d[0].transpose(1, 2, 0), mom_f[0].T, mom_head],
        vmem=16, name="final",
    )
    return (
        loss_sum[0, 0],
        count,
        norm[0, 0],
        nd.transpose(2, 0, 1)[None],
        nf.T[None],
        nh,
        nmd.transpose(2, 0, 1)[None],
        nmf.T[None],
        nmh,
        new_err_d.transpose(2, 0, 1)[None, None],
        new_err_f.T[None, None],
        q_d.transpose(0, 2, 1)[None],
        q_f.T[None],
    )


def solution(mesh):
    n, m = mesh.shape["rep"], mesh.shape["shard"]
    return jax.shard_map(
        functools.partial(on_device, n, m),
        mesh=mesh,
        in_specs=(
            P("rep", None),
            P("rep", None),
            P("rep", None),
            P("rep", None, None),
            P("shard", None),
            P(),
            P("rep", None),
            P("rep", None),
            P("rep", None),
            P("rep", None),
            P(),
            P(),
            P("shard", "rep", None, None),
            P("shard", "rep", None),
            P("shard", "rep"),
            P("shard", "rep", None, None),
            P("shard", "rep", None),
            P("shard", "rep"),
            P("shard", "rep", None, None, None),
            P("shard", "rep", None, None),
            P("shard", None, None, None),
            P("shard", None, None),
        ),
        out_specs=(
            P(),
            P(),
            P(),
            P("shard", "rep", None, None),
            P("shard", "rep", None),
            P("shard", "rep"),
            P("shard", "rep", None, None),
            P("shard", "rep", None),
            P("shard", "rep"),
            P("shard", "rep", None, None, None),
            P("shard", "rep", None, None),
            P("shard", None, None, None),
            P("shard", None, None),
        ),
        check_vma=False,
    )
```

profile of v0, /device:TPU:0, one launch (start us, length us, event | category | flops | bytes accessed | tf_op | source)
XLA Modules:
  0.0 249.3 jit_solution(8699767036422092541)
XLA Ops:
  2.0 2.8 %split.1 = (bf16[144,1024]{1,0:T(8,128)(2,1)}, bf16[144,1024]{1,0:T(8,128)(2,1)}, bf16[128,2048]{1,0:T(8,128)(2,1)}, bf16[256,1024]{1,0:T(8,128)(2,1)}) custom-call(f32[2,40,128]{2,1,0:T(8,128)} %bitcast.68, f32[16,512]{1,0:T(8,128)} %bitcast.70, f32[1,128]{1,0:T(1,128)} %refs_10_.1, s32[1,16]{1,0:T(1,128)} %reshape_squeeze.3.refs_3_, ...), custom_call_target="tpu_custom_call" | custom-call | tf_op jit(solution)/shard_map/split/pallas_call | solution.py:685
  4.8 3.0 %collective-permute-start = (bf16[144,1024]{1,0:T(8,128)(2,1)}, bf16[144,1024]{1,0:T(8,128)(2,1)S(1)}, u32[]{:S(2)}, u32[]{:S(2)}) collective-permute-start(bf16[144,1024]{1,0:T(8,128)(2,1)} %get-tuple-element.74.refs_1_), channel_id=1, source_target_pairs={{0,4},{1,9},{2,6},{3,11},{4,12},{5,1},{6,14},{7,3},{8,0},{9,17},{1... | collective-permute-start | bytes 884744 | tf_op jit(solution)/shard_map/ppermute | solution.py:753
  7.8 1.6 collective-permute-start.1
  10.8 2.3 slice.31.refs_5_.refs_4_.refs_3_
  14.3 1.7 collective-permute-done.1.refs_2_.refs_10_
  18.1 2.0 collective-permute-start.4
  20.2 1.6 collective-permute-start.5
  21.7 17.7 %gather_fusion = bf16[1024,1024]{1,0:T(8,128)(2,1)} fusion(bf16[12568,1024]{1,0:T(8,128)(2,1)} %param.27, s32[1024]{0:T(1024)S(1)} %broadcast_clamp_fusion), kind=kCustom, calls=%fused_computation | custom fusion | bytes 4198400 | tf_op jit(solution)/shard_map/jit(_take)/gather | solution.py:811
  39.4 1.6 collective-permute-start.2
  41.0 1.6 collective-permute-start.3
  42.6 1.8 select_select_fusion
  46.1 3.2 %collective-permute-done.3.refs_2_.refs_11_ = bf16[144,1024]{1,0:T(8,128)(2,1)S(1)} collective-permute-done((bf16[144,1024]{1,0:T(8,128)(2,1)S(1)}, bf16[144,1024]{1,0:T(8,128)(2,1)S(1)}, u32[]{:S(2)}, u32[]{:S(2)}) %collective-permute-start.3) | collective-permute-done | bytes 294944 | tf_op jit(solution)/shard_map/ppermute | solution.py:753
  51.0 1.6 collective-permute-start.16
  52.6 1.6 collective-permute-start.9
  55.5 1.6 collective-permute-start.7
  57.1 4.0 %collective-permute-done.9.refs_0_ = bf16[144,1024]{1,0:T(8,128)(2,1)S(1)} collective-permute-done((bf16[144,1024]{1,0:T(8,128)(2,1)}, bf16[144,1024]{1,0:T(8,128)(2,1)S(1)}, u32[]{:S(2)}, u32[]{:S(2)}) %collective-permute-start.9) | collective-permute-done | bytes 294944 | tf_op jit(solution)/shard_map/ppermute | solution.py:753
  61.8 1.6 collective-permute-start.10
  64.1 1.6 collective-permute-start.17
  65.7 3.0 %collective-permute-done.10.refs_5_ = bf16[144,1024]{1,0:T(8,128)(2,1)S(1)} collective-permute-done((bf16[144,1024]{1,0:T(8,128)(2,1)}, bf16[144,1024]{1,0:T(8,128)(2,1)S(1)}, u32[]{:S(2)}, u32[]{:S(2)}) %collective-permute-start.10) | collective-permute-done | bytes 294944 | tf_op jit(solution)/shard_map/ppermute | solution.py:753
  68.8 1.6 collective-permute-start.11
  70.3 1.6 collective-permute-done.17.refs_13_
  71.9 1.6 collective-permute-start.18
  73.5 2.0 collective-permute-done.11.refs_1_.refs_6_
  75.5 1.6 collective-permute-start.12
  77.1 1.7 collective-permute-done.18.refs_14_
  78.7 1.6 collective-permute-start.19
  80.3 1.6 collective-permute-start.15
  86.4 1.6 collective-permute-start.20
  88.0 3.4 %collective-permute-done.15.refs_2_.refs_6_ = bf16[256,1024]{1,0:T(8,128)(2,1)} collective-permute-done((bf16[256,1024]{1,0:T(8,128)(2,1)}, bf16[256,1024]{1,0:T(8,128)(2,1)}, u32[]{:S(2)}, u32[]{:S(2)}) %collective-permute-start.15) | collective-permute-done | bytes 524320 | tf_op jit(solution)/shard_map/ppermute | solution.py:753
  91.4 5.5 %collective-permute-done.14.refs_1_.refs_8_ = bf16[128,2048]{1,0:T(8,128)(2,1)S(1)} collective-permute-done((bf16[128,2048]{1,0:T(8,128)(2,1)}, bf16[128,2048]{1,0:T(8,128)(2,1)S(1)}, u32[]{:S(2)}, u32[]{:S(2)}) %collective-permute-start.14) | collective-permute-done | bytes 524320 | tf_op jit(solution)/shard_map/ppermute | solution.py:753
  96.9 3.2 %collective-permute-done.13.refs_0_ = bf16[144,1024]{1,0:T(8,128)(2,1)S(1)} collective-permute-done((bf16[144,1024]{1,0:T(8,128)(2,1)}, bf16[144,1024]{1,0:T(8,128)(2,1)S(1)}, u32[]{:S(2)}, u32[]{:S(2)}) %collective-permute-start.13) | collective-permute-done | bytes 294944 | tf_op jit(solution)/shard_map/ppermute | solution.py:753
  100.8 2.4 collective-permute-done.20.refs_16_
  103.9 5.1 %assemble.1.refs_10_.refs_1_ = bf16[1024,2048]{1,0:T(8,128)(2,1)} custom-call(s32[8,2,8]{2,1,0:T(2,128)} %constant.86.clone.refs_0_, bf16[144,1024]{1,0:T(8,128)(2,1)} %get-tuple-element.74.refs_1_, bf16[144,1024]{1,0:T(8,128)(2,1)} %copy-done.5, bf16[144,1024]{1,0:T(8,128)(2,1)} %copy-done.21, bf16[144,1024]{1,0:T(8,128)(2,1)} %after.21.refs_4_, ...), custom_call_target="tpu_custom_call" | custom-call | tf_op jit(solution)/shard_map/assemble/pallas_call | solution.py:685
  111.1 1.6 collective-permute-start.24
  112.7 1.6 collective-permute-start.29
  114.2 6.0 %collective-permute-done.24.refs_0_ = bf16[128,2048]{1,0:T(8,128)(2,1)S(1)} collective-permute-done((bf16[128,2048]{1,0:T(8,128)(2,1)S(1)}, bf16[128,2048]{1,0:T(8,128)(2,1)S(1)}, u32[]{:S(2)}, u32[]{:S(2)}) %collective-permute-start.24) | collective-permute-done | bytes 524320 | tf_op jit(solution)/shard_map/ppermute | solution.py:753
  121.1 1.6 collective-permute-start.25
  122.7 3.3 %collective-permute-done.29.refs_0_ = bf16[256,1024]{1,0:T(8,128)(2,1)} collective-permute-done((bf16[256,1024]{1,0:T(8,128)(2,1)}, bf16[256,1024]{1,0:T(8,128)(2,1)}, u32[]{:S(2)}, u32[]{:S(2)}) %collective-permute-start.29) | collective-permute-done | bytes 524320 | tf_op jit(solution)/shard_map/ppermute | solution.py:753
  126.0 1.8 collective-permute-start.30
  127.8 2.0 front.2
  130.9 3.2 %unpack.1 = (bf16[2,40,1024]{2,1,0:T(8,128)(2,1)S(1)}, bf16[16,2048]{1,0:T(8,128)(2,1)S(1)}, bf16[16,2048]{1,0:T(8,128)(2,1)S(1)}, f32[1,1024]{1,0:T(1,128)S(1)}, f32[1,128]{1,0:T(1,128)}) custom-call(s32[8,2,8]{2,1,0:T(2,128)S(1)} %copy-done.55, bf16[144,1024]{1,0:T(8,128)(2,1)S(1)} %copy-done.37, bf16[144,1024]{1,0:T(8,128)(2,1)S(1)} %copy-done.7, ...), custom_call_target="tpu_custom_call" | custom-call | tf_op jit(solution)/shard_map/unpack/pallas_call | solution.py:685
  134.1 2.9 %front.3 = (bf16[512,1024]{1,0:T(8,128)(2,1)S(1)}, f32[16,1024]{1,0:T(8,128)S(1)}, bf16[16,1024]{1,0:T(8,128)(2,1)S(1)}) custom-call(bf16[512,1024]{1,0:T(8,128)(2,1)} %collective-permute-done.8.refs_0_, s32[2,512]{1,0:T(2,128)S(1)} %copy-done.65, s32[2,512]{1,0:T(2,128)S(1)} %copy-done.63, bf16[512,1024]{1,0:T(8,128)(2,1)S(1)} %copy-done.4, ...), custom_call_target="tpu_custom_call" | custom-call | tf_op jit(solution)/shard_map/front/pallas_call | solution.py:685
  139.2 1.6 collective-permute-start.26
  141.3 7.4 %collective-permute-done.26.refs_11_ = bf16[128,2048]{1,0:T(8,128)(2,1)} collective-permute-done((bf16[128,2048]{1,0:T(8,128)(2,1)}, bf16[128,2048]{1,0:T(8,128)(2,1)}, u32[]{:S(2)}, u32[]{:S(2)}) %collective-permute-start.26) | collective-permute-done | bytes 524320 | tf_op jit(solution)/shard_map/ppermute | solution.py:753
  148.7 1.6 collective-permute-start.27
  150.3 4.0 %collective-permute-done.31.refs_9_ = bf16[256,1024]{1,0:T(8,128)(2,1)} collective-permute-done((bf16[256,1024]{1,0:T(8,128)(2,1)}, bf16[256,1024]{1,0:T(8,128)(2,1)}, u32[]{:S(2)}, u32[]{:S(2)}) %collective-permute-start.31) | collective-permute-done | bytes 524320 | tf_op jit(solution)/shard_map/ppermute | solution.py:753
  154.3 1.6 collective-permute-start.32
  155.9 14.4 %rows.1 = (bf16[2,512,2048]{2,1,0:T(8,128)(2,1)}, bf16[2,40,512]{2,1,0:T(8,128)(2,1)}, bf16[32,1024]{1,0:T(8,128)(2,1)}, f32[32,1024]{1,0:T(8,128)}, bf16[32,102...) custom-call(s32[2,512]{1,0:T(2,128)} %refs_0_.5, ...), custom_call_target="tpu_custom_call" | custom-call | tf_op jit(solution)/shard_map/rows/pallas_call | solution.py:685
  174.3 6.2 %collective-permute-done.28.refs_13_ = bf16[128,2048]{1,0:T(8,128)(2,1)S(1)} collective-permute-done((bf16[128,2048]{1,0:T(8,128)(2,1)}, bf16[128,2048]{1,0:T(8,128)(2,1)S(1)}, u32[]{:S(2)}, u32[]{:S(2)}) %collective-permute-start.28) | collective-permute-done | bytes 524320 | tf_op jit(solution)/shard_map/ppermute | solution.py:753
  183.5 3.3 %up.1 = (f32[64,2048]{1,0:T(8,128)S(1)}, bf16[64,2048]{1,0:T(8,128)(2,1)S(1)}, bf16[1024,2048]{1,0:T(8,128)(2,1)S(1)}) custom-call(s32[8,2,8]{2,1,0:T(2,128)S(1)} %copy-done.55, bf16[32,1152]{1,0:T(8,128)(2,1)S(1)} %copy-done.41, bf16[32,1152]{1,0:T(8,128)(2,1)S(1)} %collective-permute-done.22.refs_2_.refs_3_, ...), custom_call_target="tpu_custom_call" | custom-call | tf_op jit(solution)/shard_map/up/pallas_call | solution.py:685
  186.9 3.4 %down.1 = (f32[32,1152]{1,0:T(8,128)S(1)}, f32[32,1152]{1,0:T(8,128)S(1)}, bf16[2048,1024]{1,0:T(8,128)(2,1)S(1)}) custom-call(s32[8,2,8]{2,1,0:T(2,128)S(1)} %copy-done.55, bf16[64,2048]{1,0:T(8,128)(2,1)S(1)} %get-tuple-element.90.refs_1_.refs_5_, bf16[16,2048]{1,0:T(8,128)(2,1)S(1)} %get-tuple-element.87.refs_3_.refs_2_.refs_6_, ...), custom_call_target="tpu_custom_call" | custom-call | tf_op jit(solution)/shard_map/down/pallas_call | solution.py:685
  192.7 1.5 collective-permute-start.36
  194.4 2.0 collective-permute-done.36.refs_2_
  199.7 3.2 %ffn_back.1 = (f32[32,1152]{1,0:T(8,128)S(1)}, f32[32,1152]{1,0:T(8,128)S(1)}, f32[16,2048]{1,0:T(8,128)S(1)}, f32[16,2048]{1,0:T(8,128)S(1)}) custom-call(bf16[32,1152]{1,0:T(8,128)(2,1)S(1)} %get-tuple-element.98.refs_0_, bf16[32,1152]{1,0:T(8,128)(2,1)S(1)} %collective-permute-done.38.refs_1_, bf16[32,1152]{1,0:T(8,128)(2,1)S(1)} %copy-done.41, ...), custom_call_target="tpu_custom_call" | custom-call | tf_op jit(solution)/shard_map/ffn_back/pallas_call | solution.py:685
  205.5 8.1 %rows_back.1 = (f32[2,40,1024]{2,1,0:T(8,128)S(1)}, f32[24,1024]{1,0:T(8,128)S(1)}) custom-call(f32[32,1152]{1,0:T(8,128)S(1)} %get-tuple-element.102.refs_0_, f32[32,1152]{1,0:T(8,128)S(1)} %collective-permute-done.39.refs_1_, f32[32,1024]{1,0:T(8,128)S(1)} %get-tuple-element.104.refs_2_, f32[40,1024]{1,0:T(8,128)S(1)} %get-tuple-element.105.refs_3_, ...), custom_call_target="tpu_custom_call" | custom-call | tf_op jit(solution)/shard_map/rows_back/pallas_call | solution.py:685
  213.8 1.6 collective-permute-start.40
  215.9 2.6 %collective-permute-done.40 = f32[24,1024]{1,0:T(8,128)S(1)} collective-permute-done((f32[24,1024]{1,0:T(8,128)S(1)}, f32[24,1024]{1,0:T(8,128)S(1)}, u32[]{:S(2)}, u32[]{:S(2)}) %collective-permute-start.40) | collective-permute-done | bytes 98336 | tf_op jit(solution)/shard_map/ppermute | solution.py:753
  219.0 2.1 collective-permute-done.45
  221.5 2.4 collective-permute-done.41
  224.2 7.9 %collective-permute-done.42.refs_1_ = f32[24,1024]{1,0:T(8,128)S(1)} collective-permute-done((f32[24,1024]{1,0:T(8,128)S(1)}, f32[24,1024]{1,0:T(8,128)S(1)}, u32[]{:S(2)}, u32[]{:S(2)}) %collective-permute-start.42) | collective-permute-done | bytes 98336 | tf_op jit(solution)/shard_map/ppermute | solution.py:753
  232.2 3.7 %ortho.1 = (f32[2,8,1024]{2,1,0:T(8,128)S(1)}, f32[8,4096]{1,0:T(8,128)S(1)}, f32[1,1024]{1,0:T(1,128)S(1)}, f32[32,8,128]{2,1,0:T(8,128)}) custom-call(f32[24,1024]{1,0:T(8,128)S(1)} %add.99.refs_0_, f32[24,1024]{1,0:T(8,128)S(1)} %collective-permute-done.42.refs_1_, f32[8,4096]{1,0:T(8,128)S(1)} %add.101.refs_2_, ...), custom_call_target="tpu_custom_call" | custom-call | tf_op jit(solution)/shard_map/ortho/pallas_call | solution.py:685
  235.9 2.6 %all-to-all-start = ((f32[32,8,128]{2,1,0:T(8,128)}), f32[32,8,128]{2,1,0:T(8,128)S(1)}, u32[]{:S(2)}, u32[]{:S(2)}) async-start(f32[32,8,128]{2,1,0:T(8,128)} %get-tuple-element.119), calls=%async_computation | async-start | bytes 262144 | tf_op jit(solution)/shard_map/all_to_all | solution.py:1000
  238.6 8.2 %all-to-all-done.refs_0_ = f32[32,8,128]{2,1,0:T(8,128)S(1)} async-done(((f32[32,8,128]{2,1,0:T(8,128)}), f32[32,8,128]{2,1,0:T(8,128)S(1)}, u32[]{:S(2)}, u32[]{:S(2)}) %all-to-all-start) | async-done | bytes 131104 | tf_op jit(solution)/shard_map/all_to_all | solution.py:1000
  246.8 2.3 final.1
  (266 shorter events, 41.9 us)
Async XLA Ops:
  2.0 11.1 %copy-start.85 = (s32[2,512]{1,0:T(2,128)S(1)}, s32[2,512]{1,0:T(2,128)}, u32[]{:S(2)}) copy-start(s32[2,512]{1,0:T(2,128)} %param.23) | copy-start | bytes 12292
  4.8 9.5 %collective-permute-start = (bf16[144,1024]{1,0:T(8,128)(2,1)}, bf16[144,1024]{1,0:T(8,128)(2,1)S(1)}, u32[]{:S(2)}, u32[]{:S(2)}) collective-permute-start(bf16[144,1024]{1,0:T(8,128)(2,1)} %get-tuple-element.74.refs_1_), channel_id=1, source_target_pairs={{0,4},{1,9},{2,6},{3,11},{4,12},{5,1},{6,14},{7,3},{8,0},{9,17},{1... | collective-permute-start | bytes 884744 | tf_op jit(solution)/shard_map/ppermute | solution.py:753
  7.8 8.1 %collective-permute-start.1 = (bf16[144,1024]{1,0:T(8,128)(2,1)}, bf16[144,1024]{1,0:T(8,128)(2,1)S(1)}, u32[]{:S(2)}, u32[]{:S(2)}) collective-permute-start(bf16[144,1024]{1,0:T(8,128)(2,1)} %get-tuple-element.75.refs_9_), channel_id=1, source_target_pairs={{0,4},{1,9},{2,6},{3,11},{4,12},{5,1},{6,14},{7,3},{8,0},{9,17},{1... | collective-permute-start | bytes 884744 | tf_op jit(solution)/shard_map/ppermute | solution.py:753
  18.1 31.2 %collective-permute-start.4 = (bf16[128,2048]{1,0:T(8,128)(2,1)}, bf16[128,2048]{1,0:T(8,128)(2,1)S(1)}, u32[]{:S(2)}, u32[]{:S(2)}) collective-permute-start(bf16[128,2048]{1,0:T(8,128)(2,1)} %after.18.refs_6_), channel_id=1, source_target_pairs={{0,4},{1,9},{2,6},{3,11},{4,12},{5,1},{6,14},{7,3},{8,0},{9,17},{1... | collective-permute-start | bytes 1572872 | tf_op jit(solution)/shard_map/ppermute | solution.py:753
  20.2 19.3 %copy-start.6 = (bf16[144,1024]{1,0:T(8,128)(2,1)S(1)}, bf16[144,1024]{1,0:T(8,128)(2,1)}, u32[]{:S(2)}) copy-start(bf16[144,1024]{1,0:T(8,128)(2,1)} %copy-done.5) | copy-start | bytes 884740
  20.2 20.8 %copy-start.80 = (bf16[144,1024]{1,0:T(8,128)(2,1)S(1)}, bf16[144,1024]{1,0:T(8,128)(2,1)}, u32[]{:S(2)}) copy-start(bf16[144,1024]{1,0:T(8,128)(2,1)} %copy-done.79) | copy-start | bytes 884740
  20.2 29.2 %collective-permute-start.5 = (bf16[256,1024]{1,0:T(8,128)(2,1)}, bf16[256,1024]{1,0:T(8,128)(2,1)S(1)}, u32[]{:S(2)}, u32[]{:S(2)}) collective-permute-start(bf16[256,1024]{1,0:T(8,128)(2,1)} %after.19.refs_4_), channel_id=1, source_target_pairs={{0,4},{1,9},{2,6},{3,11},{4,12},{5,1},{6,14},{7,3},{8,0},{9,17},{1... | collective-permute-start | bytes 1572872 | tf_op jit(solution)/shard_map/ppermute | solution.py:753
  39.4 6.7 %collective-permute-start.2 = (bf16[144,1024]{1,0:T(8,128)(2,1)S(1)}, bf16[144,1024]{1,0:T(8,128)(2,1)S(1)}, u32[]{:S(2)}, u32[]{:S(2)}) collective-permute-start(bf16[144,1024]{1,0:T(8,128)(2,1)S(1)} %copy-done.6), channel_id=1, source_target_pairs={{0,4},{1,9},{2,6},{3,11},{4,12},{5,1},{6,14},{7,3},{8,0},{9,17},{1... | collective-permute-start | bytes 884744 | tf_op jit(solution)/shard_map/ppermute | solution.py:753
  41.0 8.3 %collective-permute-start.3 = (bf16[144,1024]{1,0:T(8,128)(2,1)S(1)}, bf16[144,1024]{1,0:T(8,128)(2,1)S(1)}, u32[]{:S(2)}, u32[]{:S(2)}) collective-permute-start(bf16[144,1024]{1,0:T(8,128)(2,1)S(1)} %copy-done.80), channel_id=1, source_target_pairs={{0,4},{1,9},{2,6},{3,11},{4,12},{5,1},{6,14},{7,3},{8,0},{9,17},{1... | collective-permute-start | bytes 884744 | tf_op jit(solution)/shard_map/ppermute | solution.py:753
  51.0 3.2 %collective-permute-start.6 = (bf16[512,1024]{1,0:T(8,128)(2,1)}, bf16[512,1024]{1,0:T(8,128)(2,1)S(1)}, u32[]{:S(2)}, u32[]{:S(2)}) collective-permute-start(bf16[512,1024]{1,0:T(8,128)(2,1)} %after.20), channel_id=1, source_target_pairs={{0,1},{1,0},{2,3},{3,2},{4,5},{5,4},{6,7},{7,6},{8,9},{9,8},{10,11... | collective-permute-start | bytes 3145736 | tf_op jit(solution)/shard_map/ppermute | solution.py:753
  51.0 12.4 %collective-permute-start.16 = (bf16[144,1024]{1,0:T(8,128)(2,1)}, bf16[144,1024]{1,0:T(8,128)(2,1)S(1)}, u32[]{:S(2)}, u32[]{:S(2)}) collective-permute-start(bf16[144,1024]{1,0:T(8,128)(2,1)} %copy-done.75), channel_id=1, source_target_pairs={{0,4},{1,9},{2,6},{3,11},{4,12},{5,1},{6,14},{7,3},{8,0},{9,17},{1... | collective-permute-start | bytes 884744 | tf_op jit(solution)/shard_map/ppermute | solution.py:753
  52.6 8.5 %collective-permute-start.9 = (bf16[144,1024]{1,0:T(8,128)(2,1)}, bf16[144,1024]{1,0:T(8,128)(2,1)S(1)}, u32[]{:S(2)}, u32[]{:S(2)}) collective-permute-start(bf16[144,1024]{1,0:T(8,128)(2,1)} %copy-done.21), channel_id=1, source_target_pairs={{0,4},{1,9},{2,6},{3,11},{4,12},{5,1},{6,14},{7,3},{8,0},{9,17},{1... | collective-permute-start | bytes 884744 | tf_op jit(solution)/shard_map/ppermute | solution.py:753
  55.5 26.9 %collective-permute-start.7 = (bf16[512,1024]{1,0:T(8,128)(2,1)S(1)}, bf16[512,1024]{1,0:T(8,128)(2,1)S(1)}, u32[]{:S(2)}, u32[]{:S(2)}) collective-permute-start(bf16[512,1024]{1,0:T(8,128)(2,1)S(1)} %fusion.refs_0_.refs_1_), channel_id=1, source_target_pairs={{0,2},{1,3},{2,0},{3,1},{4,6},{5,7},{6,4},{7,5},{8,10},{9,11},{10,... | collective-permute-start | bytes 3145736 | tf_op jit(solution)/shard_map/ppermute | solution.py:753
  61.8 6.9 %collective-permute-start.10 = (bf16[144,1024]{1,0:T(8,128)(2,1)}, bf16[144,1024]{1,0:T(8,128)(2,1)S(1)}, u32[]{:S(2)}, u32[]{:S(2)}) collective-permute-start(bf16[144,1024]{1,0:T(8,128)(2,1)} %after.21.refs_4_), channel_id=1, source_target_pairs={{0,4},{1,9},{2,6},{3,11},{4,12},{5,1},{6,14},{7,3},{8,0},{9,17},{1... | collective-permute-start | bytes 884744 | tf_op jit(solution)/shard_map/ppermute | solution.py:753
  64.1 7.8 %collective-permute-start.17 = (bf16[144,1024]{1,0:T(8,128)(2,1)}, bf16[144,1024]{1,0:T(8,128)(2,1)S(1)}, u32[]{:S(2)}, u32[]{:S(2)}) collective-permute-start(bf16[144,1024]{1,0:T(8,128)(2,1)} %after.26.refs_12_), channel_id=1, source_target_pairs={{0,4},{1,9},{2,6},{3,11},{4,12},{5,1},{6,14},{7,3},{8,0},{9,17},{1... | collective-permute-start | bytes 884744 | tf_op jit(solution)/shard_map/ppermute | solution.py:753
  68.7 14.7 %copy-start.38 = (bf16[144,1024]{1,0:T(8,128)(2,1)}, bf16[144,1024]{1,0:T(8,128)(2,1)S(1)}, u32[]{:S(2)}) copy-start(bf16[144,1024]{1,0:T(8,128)(2,1)S(1)} %collective-permute-done.10.refs_5_) | copy-start | bytes 884740
  68.8 6.7 %collective-permute-start.11 = (bf16[144,1024]{1,0:T(8,128)(2,1)S(1)}, bf16[144,1024]{1,0:T(8,128)(2,1)S(1)}, u32[]{:S(2)}, u32[]{:S(2)}) collective-permute-start(bf16[144,1024]{1,0:T(8,128)(2,1)S(1)} %collective-permute-done.10.refs_5_), channel_id=1, source_target_pairs={{0,4},{1,9},{2,6},{3,11},{4,12},{5,1},{6,14},{7,3},{8,0},{9,17},{1... | collective-permute-start | bytes 884744 | tf_op jit(solution)/shard_map/ppermute | solution.py:753
  71.9 6.8 %collective-permute-start.18 = (bf16[144,1024]{1,0:T(8,128)(2,1)S(1)}, bf16[144,1024]{1,0:T(8,128)(2,1)}, u32[]{:S(2)}, u32[]{:S(2)}) collective-permute-start(bf16[144,1024]{1,0:T(8,128)(2,1)S(1)} %collective-permute-done.17.refs_13_), channel_id=1, source_target_pairs={{0,4},{1,9},{2,6},{3,11},{4,12},{5,1},{6,14},{7,3},{8,0},{9,17},{1... | collective-permute-start | bytes 884744 | tf_op jit(solution)/shard_map/ppermute | solution.py:753
  75.5 6.9 %collective-permute-start.12 = (bf16[144,1024]{1,0:T(8,128)(2,1)S(1)}, bf16[144,1024]{1,0:T(8,128)(2,1)}, u32[]{:S(2)}, u32[]{:S(2)}) collective-permute-start(bf16[144,1024]{1,0:T(8,128)(2,1)S(1)} %collective-permute-done.11.refs_1_.refs_6_), channel_id=1, source_target_pairs={{0,4},{1,9},{2,6},{3,11},{4,12},{5,1},{6,14},{7,3},{8,0},{9,17},{1... | collective-permute-start | bytes 884744 | tf_op jit(solution)/shard_map/ppermute | solution.py:753
  78.7 6.9 %collective-permute-start.19 = (bf16[144,1024]{1,0:T(8,128)(2,1)}, bf16[144,1024]{1,0:T(8,128)(2,1)S(1)}, u32[]{:S(2)}, u32[]{:S(2)}) collective-permute-start(bf16[144,1024]{1,0:T(8,128)(2,1)} %collective-permute-done.18.refs_14_), channel_id=1, source_target_pairs={{0,4},{1,9},{2,6},{3,11},{4,12},{5,1},{6,14},{7,3},{8,0},{9,17},{1... | collective-permute-start | bytes 884744 | tf_op jit(solution)/shard_map/ppermute | solution.py:753
  80.3 11.1 %collective-permute-start.15 = (bf16[256,1024]{1,0:T(8,128)(2,1)}, bf16[256,1024]{1,0:T(8,128)(2,1)}, u32[]{:S(2)}, u32[]{:S(2)}) collective-permute-start(bf16[256,1024]{1,0:T(8,128)(2,1)} %after.24.refs_5_), channel_id=1, source_target_pairs={{0,4},{1,9},{2,6},{3,11},{4,12},{5,1},{6,14},{7,3},{8,0},{9,17},{1... | collective-permute-start | bytes 1572872 | tf_op jit(solution)/shard_map/ppermute | solution.py:753
  81.9 15.0 %collective-permute-start.14 = (bf16[128,2048]{1,0:T(8,128)(2,1)}, bf16[128,2048]{1,0:T(8,128)(2,1)S(1)}, u32[]{:S(2)}, u32[]{:S(2)}) collective-permute-start(bf16[128,2048]{1,0:T(8,128)(2,1)} %after.23.refs_7_), channel_id=1, source_target_pairs={{0,4},{1,9},{2,6},{3,11},{4,12},{5,1},{6,14},{7,3},{8,0},{9,17},{1... | collective-permute-start | bytes 1572872 | tf_op jit(solution)/shard_map/ppermute | solution.py:753
  83.5 16.6 %collective-permute-start.13 = (bf16[144,1024]{1,0:T(8,128)(2,1)}, bf16[144,1024]{1,0:T(8,128)(2,1)S(1)}, u32[]{:S(2)}, u32[]{:S(2)}) collective-permute-start(bf16[144,1024]{1,0:T(8,128)(2,1)} %after.22.refs_7_), channel_id=1, source_target_pairs={{0,4},{1,9},{2,6},{3,11},{4,12},{5,1},{6,14},{7,3},{8,0},{9,17},{1... | collective-permute-start | bytes 884744 | tf_op jit(solution)/shard_map/ppermute | solution.py:753
  86.4 16.8 %collective-permute-start.20 = (bf16[144,1024]{1,0:T(8,128)(2,1)}, bf16[144,1024]{1,0:T(8,128)(2,1)S(1)}, u32[]{:S(2)}, u32[]{:S(2)}) collective-permute-start(bf16[144,1024]{1,0:T(8,128)(2,1)} %after.27.refs_15_), channel_id=1, source_target_pairs={{0,4},{1,9},{2,6},{3,11},{4,12},{5,1},{6,14},{7,3},{8,0},{9,17},{1... | collective-permute-start | bytes 884744 | tf_op jit(solution)/shard_map/ppermute | solution.py:753
  109.1 46.8 %collective-permute-start.21 = (bf16[1024,2048]{1,0:T(8,128)(2,1)}, bf16[1024,2048]{1,0:T(8,128)(2,1)}, u32[]{:S(2)}, u32[]{:S(2)}) collective-permute-start(bf16[1024,2048]{1,0:T(8,128)(2,1)} %assemble.1.refs_10_.refs_1_), channel_id=1, source_target_pairs={{0,1},{1,0},{2,3},{3,2},{4,5},{5,4},{6,7},{7,6},{8,9},{9,8},{10,11... | collective-permute-start | bytes 12582920 | tf_op jit(solution)/shard_map/ppermute | solution.py:753
  110.6 23.5 %collective-permute-start.8 = (bf16[512,1024]{1,0:T(8,128)(2,1)}, bf16[512,1024]{1,0:T(8,128)(2,1)}, u32[]{:S(2)}, u32[]{:S(2)}) collective-permute-start(bf16[512,1024]{1,0:T(8,128)(2,1)} %add.97), channel_id=1, source_target_pairs={{0,1},{1,0},{2,3},{3,2},{4,5},{5,4},{6,7},{7,6},{8,9},{9,8},{10,11... | collective-permute-start | bytes 3145736 | tf_op jit(solution)/shard_map/ppermute | solution.py:753
  111.1 9.2 %collective-permute-start.24 = (bf16[128,2048]{1,0:T(8,128)(2,1)S(1)}, bf16[128,2048]{1,0:T(8,128)(2,1)S(1)}, u32[]{:S(2)}, u32[]{:S(2)}) collective-permute-start(bf16[128,2048]{1,0:T(8,128)(2,1)S(1)} %copy-done.26), channel_id=1, source_target_pairs={{0,4},{1,9},{2,6},{3,11},{4,12},{5,1},{6,14},{7,3},{8,0},{9,17},{1... | collective-permute-start | bytes 1572872 | tf_op jit(solution)/shard_map/ppermute | solution.py:753
  112.7 13.3 %collective-permute-start.29 = (bf16[256,1024]{1,0:T(8,128)(2,1)}, bf16[256,1024]{1,0:T(8,128)(2,1)}, u32[]{:S(2)}, u32[]{:S(2)}) collective-permute-start(bf16[256,1024]{1,0:T(8,128)(2,1)} %collective-permute-done.15.refs_2_.refs_6_), channel_id=1, source_target_pairs={{0,4},{1,9},{2,6},{3,11},{4,12},{5,1},{6,14},{7,3},{8,0},{9,17},{1... | collective-permute-start | bytes 1572872 | tf_op jit(solution)/shard_map/ppermute | solution.py:753
  121.1 18.1 %collective-permute-start.25 = (bf16[128,2048]{1,0:T(8,128)(2,1)}, bf16[128,2048]{1,0:T(8,128)(2,1)}, u32[]{:S(2)}, u32[]{:S(2)}) collective-permute-start(bf16[128,2048]{1,0:T(8,128)(2,1)} %after.28.refs_9_), channel_id=1, source_target_pairs={{0,4},{1,9},{2,6},{3,11},{4,12},{5,1},{6,14},{7,3},{8,0},{9,17},{1... | collective-permute-start | bytes 1572872 | tf_op jit(solution)/shard_map/ppermute | solution.py:753
  126.0 14.8 %collective-permute-start.30 = (bf16[256,1024]{1,0:T(8,128)(2,1)}, bf16[256,1024]{1,0:T(8,128)(2,1)}, u32[]{:S(2)}, u32[]{:S(2)}) collective-permute-start(bf16[256,1024]{1,0:T(8,128)(2,1)} %after.31.refs_7_), channel_id=1, source_target_pairs={{0,4},{1,9},{2,6},{3,11},{4,12},{5,1},{6,14},{7,3},{8,0},{9,17},{1... | collective-permute-start | bytes 1572872 | tf_op jit(solution)/shard_map/ppermute | solution.py:753
  139.2 9.5 %collective-permute-start.26 = (bf16[128,2048]{1,0:T(8,128)(2,1)}, bf16[128,2048]{1,0:T(8,128)(2,1)}, u32[]{:S(2)}, u32[]{:S(2)}) collective-permute-start(bf16[128,2048]{1,0:T(8,128)(2,1)} %after.29.refs_10_), channel_id=1, source_target_pairs={{0,4},{1,9},{2,6},{3,11},{4,12},{5,1},{6,14},{7,3},{8,0},{9,17},{1... | collective-permute-start | bytes 1572872 | tf_op jit(solution)/shard_map/ppermute | solution.py:753
  140.8 13.5 %collective-permute-start.31 = (bf16[256,1024]{1,0:T(8,128)(2,1)}, bf16[256,1024]{1,0:T(8,128)(2,1)}, u32[]{:S(2)}, u32[]{:S(2)}) collective-permute-start(bf16[256,1024]{1,0:T(8,128)(2,1)} %after.32.refs_8_), channel_id=1, source_target_pairs={{0,4},{1,9},{2,6},{3,11},{4,12},{5,1},{6,14},{7,3},{8,0},{9,17},{1... | collective-permute-start | bytes 1572872 | tf_op jit(solution)/shard_map/ppermute | solution.py:753
  148.7 21.7 %collective-permute-start.27 = (bf16[128,2048]{1,0:T(8,128)(2,1)}, bf16[128,2048]{1,0:T(8,128)(2,1)S(1)}, u32[]{:S(2)}, u32[]{:S(2)}) collective-permute-start(bf16[128,2048]{1,0:T(8,128)(2,1)} %collective-permute-done.26.refs_11_), channel_id=1, source_target_pairs={{0,4},{1,9},{2,6},{3,11},{4,12},{5,1},{6,14},{7,3},{8,0},{9,17},{1... | collective-permute-start | bytes 1572872 | tf_op jit(solution)/shard_map/ppermute | solution.py:753
  154.3 17.4 %collective-permute-start.32 = (bf16[256,1024]{1,0:T(8,128)(2,1)}, bf16[256,1024]{1,0:T(8,128)(2,1)S(1)}, u32[]{:S(2)}, u32[]{:S(2)}) collective-permute-start(bf16[256,1024]{1,0:T(8,128)(2,1)} %collective-permute-done.31.refs_9_), channel_id=1, source_target_pairs={{0,4},{1,9},{2,6},{3,11},{4,12},{5,1},{6,14},{7,3},{8,0},{9,17},{1... | collective-permute-start | bytes 1572872 | tf_op jit(solution)/shard_map/ppermute | solution.py:753
  170.3 11.0 %copy-start.11 = (bf16[128,2048]{1,0:T(8,128)(2,1)S(1)}, bf16[128,2048]{1,0:T(8,128)(2,1)}, u32[]{:S(2)}) copy-start(bf16[128,2048]{1,0:T(8,128)(2,1)} %after.23.refs_7_) | copy-start | bytes 1572868
  170.3 11.0 %copy-start.27 = (bf16[128,2048]{1,0:T(8,128)(2,1)S(1)}, bf16[128,2048]{1,0:T(8,128)(2,1)}, u32[]{:S(2)}) copy-start(bf16[128,2048]{1,0:T(8,128)(2,1)} %copy-done.25) | copy-start | bytes 1572868
  170.3 11.0 %copy-start.29 = (bf16[128,2048]{1,0:T(8,128)(2,1)S(1)}, bf16[128,2048]{1,0:T(8,128)(2,1)}, u32[]{:S(2)}) copy-start(bf16[128,2048]{1,0:T(8,128)(2,1)} %after.28.refs_9_) | copy-start | bytes 1572868
  170.3 11.0 %copy-start.35 = (bf16[128,2048]{1,0:T(8,128)(2,1)S(1)}, bf16[128,2048]{1,0:T(8,128)(2,1)}, u32[]{:S(2)}) copy-start(bf16[128,2048]{1,0:T(8,128)(2,1)} %after.18.refs_6_) | copy-start | bytes 1572868
  171.2 9.4 %collective-permute-start.28 = (bf16[128,2048]{1,0:T(8,128)(2,1)}, bf16[128,2048]{1,0:T(8,128)(2,1)S(1)}, u32[]{:S(2)}, u32[]{:S(2)}) collective-permute-start(bf16[128,2048]{1,0:T(8,128)(2,1)} %after.30.refs_12_), channel_id=1, source_target_pairs={{0,4},{1,9},{2,6},{3,11},{4,12},{5,1},{6,14},{7,3},{8,0},{9,17},{1... | collective-permute-start | bytes 1572872 | tf_op jit(solution)/shard_map/ppermute | solution.py:753
  172.5 14.3 %collective-permute-start.33 = (bf16[256,1024]{1,0:T(8,128)(2,1)}, bf16[256,1024]{1,0:T(8,128)(2,1)S(1)}, u32[]{:S(2)}, u32[]{:S(2)}) collective-permute-start(bf16[256,1024]{1,0:T(8,128)(2,1)} %after.33.refs_10_), channel_id=1, source_target_pairs={{0,4},{1,9},{2,6},{3,11},{4,12},{5,1},{6,14},{7,3},{8,0},{9,17},{1... | collective-permute-start | bytes 1572872 | tf_op jit(solution)/shard_map/ppermute | solution.py:753
  172.9 1.4 collective-permute-start.22
  172.9 1.4 collective-permute-start.23
  186.8 17.6 %copy-start.53 = (f32[1,1,4096,16]{2,3,1,0:T(8,128)S(1)}, f32[1,1,4096,16]{2,3,1,0:T(8,128)}, u32[]{:S(2)}) copy-start(f32[1,1,4096,16]{2,3,1,0:T(8,128)} %param.42) | copy-start | bytes 786436
  186.8 17.5 %copy-start.69 = (f32[1,16,8]{1,2,0:T(8,128)S(1)}, f32[1,16,8]{1,2,0:T(8,128)}, u32[]{:S(2)}) copy-start(f32[1,16,8]{1,2,0:T(8,128)} %param.44) | copy-start | bytes 1540
  190.3 1.4 collective-permute-start.34
  192.5 1.9 collective-permute-start.35
  192.7 3.8 %collective-permute-start.36 = (f32[32,128]{1,0:T(8,128)S(1)}, f32[32,128]{1,0:T(8,128)S(1)}, u32[]{:S(2)}, u32[]{:S(2)}) collective-permute-start(f32[32,128]{1,0:T(8,128)S(1)} %get-tuple-element.94.refs_0_), channel_id=1, source_target_pairs={{0,2},{1,3},{2,0},{3,1},{4,6},{5,7},{6,4},{7,5},{8,10},{9,11},{10,... | collective-permute-start | bytes 49160 | tf_op jit(solution)/shard_map/ppermute | solution.py:753
  194.2 3.2 %collective-permute-start.37 = (f32[32,128]{1,0:T(8,128)S(1)}, f32[32,128]{1,0:T(8,128)S(1)}, u32[]{:S(2)}, u32[]{:S(2)}) collective-permute-start(f32[32,128]{1,0:T(8,128)S(1)} %get-tuple-element.94.refs_0_), channel_id=1, source_target_pairs={{0,3},{1,2},{2,1},{3,0},{4,7},{5,6},{6,5},{7,4},{8,11},{9,10},{10,... | collective-permute-start | bytes 49160 | tf_op jit(solution)/shard_map/ppermute | solution.py:753
  198.3 1.3 collective-permute-start.38
  203.0 1.4 collective-permute-start.43
  203.2 2.2 collective-permute-start.39
  204.8 10.5 %collective-permute-start.44 = (f32[8,4096]{1,0:T(8,128)S(1)}, f32[8,4096]{1,0:T(8,128)S(1)}, u32[]{:S(2)}, u32[]{:S(2)}) collective-permute-start(f32[8,4096]{1,0:T(8,128)S(1)} %get-tuple-element.116), channel_id=1, source_target_pairs={{0,4},{1,5},{2,6},{3,7},{4,0},{5,1},{6,2},{7,3},{8,12},{9,13},{10,... | collective-permute-start | bytes 393224 | tf_op jit(solution)/shard_map/ppermute | solution.py:753
  213.7 33.1 %copy-start.54 = (f32[1,128,2,40]{1,3,2,0:T(8,128)S(1)}, f32[1,128,2,40]{1,3,2,0:T(8,128)}, u32[]{:S(2)}) copy-start(f32[1,128,2,40]{1,3,2,0:T(8,128)} %param.35) | copy-start | bytes 122884
  213.7 33.0 %copy-start.56 = (f32[1,512,16]{1,2,0:T(8,128)S(1)}, f32[1,512,16]{1,2,0:T(8,128)}, u32[]{:S(2)}) copy-start(f32[1,512,16]{1,2,0:T(8,128)} %param.36) | copy-start | bytes 98308
  213.7 33.0 %copy-start.62 = (f32[1,128,2,40]{1,3,2,0:T(8,128)S(1)}, f32[1,128,2,40]{1,3,2,0:T(8,128)}, u32[]{:S(2)}) copy-start(f32[1,128,2,40]{1,3,2,0:T(8,128)} %param.38) | copy-start | bytes 122884
  213.7 33.0 %copy-start.64 = (f32[1,512,16]{1,2,0:T(8,128)S(1)}, f32[1,512,16]{1,2,0:T(8,128)}, u32[]{:S(2)}) copy-start(f32[1,512,16]{1,2,0:T(8,128)} %param.39) | copy-start | bytes 98308
  213.7 33.0 %copy-start.70 = (f32[1,128]{1,0:T(1,128)S(1)}, f32[1,128]{1,0:T(1,128)}, u32[]{:S(2)}) copy-start(f32[1,128]{1,0:T(1,128)} %refs_10_.1) | copy-start | bytes 1540
  213.8 33.0 %copy-start.71 = (f32[1,128]{1,0:T(1,128)S(1)}, f32[1,128]{1,0:T(1,128)}, u32[]{:S(2)}) copy-start(f32[1,128]{1,0:T(1,128)} %refs_13_.1) | copy-start | bytes 1540
  213.8 4.7 %collective-permute-start.40 = (f32[24,1024]{1,0:T(8,128)S(1)}, f32[24,1024]{1,0:T(8,128)S(1)}, u32[]{:S(2)}, u32[]{:S(2)}) collective-permute-start(f32[24,1024]{1,0:T(8,128)S(1)} %get-tuple-element.113), channel_id=1, source_target_pairs={{0,4},{1,5},{2,6},{3,7},{4,0},{5,1},{6,2},{7,3},{8,12},{9,13},{10,... | collective-permute-start | bytes 294920 | tf_op jit(solution)/shard_map/ppermute | solution.py:753
  215.4 5.7 %collective-permute-start.45 = (f32[8,4096]{1,0:T(8,128)S(1)}, f32[8,4096]{1,0:T(8,128)S(1)}, u32[]{:S(2)}, u32[]{:S(2)}) collective-permute-start(f32[8,4096]{1,0:T(8,128)S(1)} %add.100), channel_id=1, source_target_pairs={{0,8},{1,9},{2,10},{3,11},{4,12},{5,13},{6,14},{7,15},{8,0},{9,1},... | collective-permute-start | bytes 393224 | tf_op jit(solution)/shard_map/ppermute | solution.py:753
  218.5 5.4 %collective-permute-start.41 = (f32[24,1024]{1,0:T(8,128)S(1)}, f32[24,1024]{1,0:T(8,128)S(1)}, u32[]{:S(2)}, u32[]{:S(2)}) collective-permute-start(f32[24,1024]{1,0:T(8,128)S(1)} %add.98), channel_id=1, source_target_pairs={{0,8},{1,9},{2,10},{3,11},{4,12},{5,13},{6,14},{7,15},{8,0},{9,1},... | collective-permute-start | bytes 294920 | tf_op jit(solution)/shard_map/ppermute | solution.py:753
  221.1 11.1 %collective-permute-start.46 = (f32[8,4096]{1,0:T(8,128)S(1)}, f32[8,4096]{1,0:T(8,128)S(1)}, u32[]{:S(2)}, u32[]{:S(2)}) collective-permute-start(f32[8,4096]{1,0:T(8,128)S(1)} %add.101.refs_2_), channel_id=1, source_target_pairs={{0,16},{1,17},{2,18},{3,19},{4,20},{5,21},{6,22},{7,23},{8,24},{9,... | collective-permute-start | bytes 393224 | tf_op jit(solution)/shard_map/ppermute | solution.py:753
  223.8 8.3 %collective-permute-start.42 = (f32[24,1024]{1,0:T(8,128)S(1)}, f32[24,1024]{1,0:T(8,128)S(1)}, u32[]{:S(2)}, u32[]{:S(2)}) collective-permute-start(f32[24,1024]{1,0:T(8,128)S(1)} %add.99.refs_0_), channel_id=1, source_target_pairs={{0,16},{1,17},{2,18},{3,19},{4,20},{5,21},{6,22},{7,23},{8,24},{9,... | collective-permute-start | bytes 294920 | tf_op jit(solution)/shard_map/ppermute | solution.py:753
  235.9 10.8 %all-to-all-start = ((f32[32,8,128]{2,1,0:T(8,128)}), f32[32,8,128]{2,1,0:T(8,128)S(1)}, u32[]{:S(2)}, u32[]{:S(2)}) async-start(f32[32,8,128]{2,1,0:T(8,128)} %get-tuple-element.119), calls=%async_computation | async-start | bytes 262144 | tf_op jit(solution)/shard_map/all_to_all | solution.py:1000
  (71 other events, 303.3 us)
where the time goes:
time: 250 us; the launch traced here: 249 us
  waiting for transfers between devices  90.4 us (36%)
  Pallas kernels  56.6 us (23%)
  starting transfers between devices  53.8 us (22%)
  local copies, waits for them, and re-layouts  40.1 us (16%)
  other arithmetic  6.66 us (3%)
    ppermute x47, waiting for transfers between devices, send(): return lax.ppermute(x, AXES, perm)  82.2 us
    pallas_call x15, Pallas kernels, call(): pl.pallas_call(kernel, out_shape=tuple((jax.ShapeDtypeStruct(o.shape, o.d...  56.6 us
    ppermute x47, starting transfers between devices, send(): return lax.ppermute(x, AXES, perm)  51.2 us
    gather x1, local copies, waits for them, and re-layouts, lookup(): found = jnp.take(embed_table, jnp.clip(near, 0, held - 1), axis=0)  17.7 us
    unnamed x173, local copies, waits for them, and re-layouts  15.8 us
    all_to_all x1, waiting for transfers between devices, on_device(): notes = lax.all_to_all(note, AXES, 0, 0)  8.17 us
  transfers between devices with their start and end apart: 48, of which 29 were waited for; matrix products, arithmetic and copies ran while one was open for 11% of the time, Pallas kernels for 14%

commit v1 on v0

--- a/solution.py
+++ b/solution.py
@@ -138,14 +138,12 @@
         copy.wait()
 
 
-def assemble_kernel(ready, source, *refs):
+def assemble_kernel(column, ready, source, *refs):
     pieces, (mat, sems) = refs[:-2], refs[-2:]
     rep, core = lax.axis_index("rep"), lax.axis_index("shard") % 2
-    n = len(pieces) // 2
-    rows, width = mat.shape[0] // n, mat.shape[1] // 2
-    tops = [piece.at[pl.ds(0, rows), :] for piece in pieces]
-    spots = [(source[rep, core, k % n] * rows, k // n * width) for k in range(2 * n)]
-    load(tops, spots, mat, sems)()
+    rows, part = mat.shape[0] // len(pieces), mat.shape[1]
+    tops = [piece.at[pl.ds(0, rows), pl.ds(column * part, part)] for piece in pieces]
+    load(tops, [(source[rep, core, k] * rows, 0) for k in range(len(pieces))], mat, sems)()
 
 
 def unpack_kernel(rank, rows, ready, source, *refs):
@@ -222,13 +220,13 @@
 
 
 def kv_half(rank, h1, mat, at, u, ad, bias, kv):
-    part = mat.shape[1] // 4
+    part = mat[0].shape[1]
     width = 2 * part
     cols = pl.ds(at, part)
     for j in range(2):
         to = pl.ds(pl.multiple_of(at + j * width, part), part)
         for b in range(len(h1)):
-            total = nn(h1[b][...], mat[:, (1 + j) * part : (2 + j) * part]) + bias[4 + j : 5 + j, cols]
+            total = nn(h1[b][...], mat[1 + j][...]) + bias[4 + j : 5 + j, cols]
             total = total + SCALE * nn(lanes(u[b], rank * (1 + j), rank * (2 + j)), ad[1, :, cols])
             kv[b, :, to] = total.astype(BF16)
 
@@ -236,33 +234,36 @@
 def rows_kernel(micro, rank, ready, flush, *refs):
     seg_v, refs = refs[0], refs[1:]
     h1, hl, xl = refs[:micro], refs[micro : 2 * micro], refs[2 * micro : 3 * micro]
-    ad, gains, bias, mat_own, mat_sib, kv, ukv_t, o, x1, q, p_t, u, w_out, e1, ukv = refs[3 * micro :]
+    ad, gains, bias = refs[3 * micro : 3 * micro + 3]
+    mats = refs[3 * micro + 3 : 3 * micro + 11]
+    kv, ukv_t, o, x1, q, p_t, u, w_out, e1, ukv = refs[3 * micro + 11 :]
     core = lax.axis_index("shard") % 2
     slots, width = hl[0].shape
     heads = width // HEAD_DIM
     tokens = h1[0].shape[0]
     part = width // 2
-    mats = [(mat_own, pl.multiple_of(core * part, part)), (mat_sib, pl.multiple_of((1 - core) * part, part))]
+    places = [pl.multiple_of(core * part, part), pl.multiple_of((1 - core) * part, part)]
+    mats = [(mats[:4], places[0]), (mats[4:], places[1])]
     ready(ad, *h1)
     down, up = ad[0], ad[1]
     for b in range(micro):
         ukv[b] = lanes(nt(h1[b][...], down).astype(BF16), rank, 3 * rank)
         ukv_t[b] = nt(down, h1[b][...]).astype(BF16)
-    ready(mat_own, bias)
+    ready(*mats[0][0][1:3], bias)
     kv_half(rank, h1, *mats[0], ukv, ad, bias, kv)
     ready()
     kv_half(rank, h1, *mats[1], ukv, ad, bias, kv)
     flush(0)
     flush(1)
     for mat, at in mats:
-        w_out[:, pl.ds(at, part)] = mat[:, 3 * part :]
+        w_out[:, pl.ds(at, part)] = mat[3][...]
     flush(7)
     h_last = jnp.concatenate([h[...] for h in hl], 0)
     x_last = jnp.concatenate([x[...] for x in xl], 0)
     u_q = lanes(nt(h_last, down).astype(BF16), 0, rank)
     for mat, at in mats:
         cols = pl.ds(at, part)
-        total = nn(h_last, mat[:, :part]) + bias[3:4, cols] + SCALE * nn(u_q, ad[1, :, cols])
+        total = nn(h_last, mat[0][...]) + bias[3:4, cols] + SCALE * nn(u_q, ad[1, :, cols])
         q[:, cols] = total.astype(BF16)
     q_all = q[...]
     parts = []
@@ -291,48 +292,49 @@
     u[...] = u_q + u_o + u_up
 
 
-def up_kernel(rank, ready, source, own, sib, f_own, f_sib, bias, *refs):
-    weights = refs[:-4]
-    f, a, wide, sems = refs[-4:]
-    width = wide.shape[0]
+def preload_kernel(n, ready, source, _, *refs):
+    w_up, w_down, sems = refs[-3:]
     rep, core = lax.axis_index("rep"), lax.axis_index("shard") % 2
-    height = weights[0].shape[0]
-    spots = [(source[rep, core, k] * height, 0) for k in range(len(weights))]
-    tops = weights
-    loaded = load(tops, spots, wide, sems)
-    ready()
+    loads = []
+    for index, wide in enumerate((w_up, w_down)):
+        pieces = refs[index * n : (index + 1) * n]
+        height = pieces[0].shape[0]
+        spots = [(source[rep, core, k] * height, 0) for k in range(n)]
+        loads.append(load(pieces, spots, wide, sems.at[index]))
+    for wait in loads:
+        wait()
+
+
+def ffn_kernel(rank, last, ready, source, own, sib, f_own, f_sib, bias, *refs):
+    up_last, down_last, _, _, f, a, w_up, w_down, mine, send, sems = refs
+    width = w_up.shape[0]
+    rep, core = lax.axis_index("rep"), lax.axis_index("shard") % 2
+    loads = []
+    for index, (piece, wide) in enumerate(((up_last, w_up), (down_last, w_down))):
+        spots = [(source[rep, core, last] * piece.shape[0], 0)]
+        loads.append(load([piece], spots, wide, sems.at[index]))
+    ready()
+    lane = 5 * rank
+    rows = own.shape[0]
     h2 = jnp.concatenate([own[:, :width], sib[:, :width]], 0)
-    lane = 5 * rank
+    pair_own, pair_sib = factors(f_own, rank), factors(f_sib, rank)
     extra = jnp.concatenate(
         [
-            nn(own[:, width : width + lane], factors(f_own, rank)[1]),
-            nn(sib[:, width : width + lane], factors(f_sib, rank)[1]),
+            nn(own[:, width : width + lane], pair_own[1]),
+            nn(sib[:, width : width + lane], pair_sib[1]),
         ],
         0,
     )
-    loaded()
-    total = nn(h2, wide[...]) + bias[...] + SCALE * extra
+    loads[0]()
+    total = nn(h2, w_up[...]) + bias[...] + SCALE * extra
     f[...] = total
-    a[...] = jax.nn.gelu(total, approximate=True).astype(BF16)
-
-
-def down_kernel(rank, ready, source, a, f_own, f_sib, *refs):
-    weights = refs[:-4]
-    mine, send, wide, sems = refs[-4:]
-    width = wide.shape[1]
-    rep, core = lax.axis_index("rep"), lax.axis_index("shard") % 2
-    height = weights[0].shape[0]
-    spots = [(source[rep, core, k] * height, 0) for k in range(len(weights))]
-    ends = weights
-    loaded = load(ends, spots, wide, sems)
-    ready()
-    rows = a.shape[0] // 2
-    lane = 5 * rank
-    for out, low, factor in ((mine, 0, f_own), (send, rows, f_sib)):
+    low = jax.nn.gelu(total, approximate=True).astype(BF16)
+    a[...] = low
+    for out, at, pair in ((mine, 0, pair_own), (send, rows, pair_sib)):
         out[:, width:] = jnp.zeros_like(out[:, width:])
-        out[:, width : width + lane] = nt(a[low : low + rows, :], factors(factor, rank)[0])
-    loaded()
-    y = nn(a[...], wide[...])
+        out[:, width : width + lane] = nt(low[at : at + rows], pair[0])
+    loads[1]()
+    y = nn(low, w_down[...])
     mine[:, :width] = y[:rows]
     send[:, :width] = y[rows:]
 
@@ -389,35 +391,39 @@
     e2[:, width : width + 5 * rank] = left
 
 
-def ffn_back_kernel(rank, ready, own, sib, e1_own, e1_sib, f, a, f_own, f_sib, wide_u, wide_d,
-                    mine, send, gf_mine, gf_send):
-    width = wide_u.shape[0]
-    lane = 5 * rank
-    ready()
-    rows = own.shape[0]
+def slope_kernel(ready, f, _, out):
     x = f[...]
     c0, c1 = math.sqrt(2.0 / math.pi), 0.044715
     t = jnp.tanh(c0 * (x + c1 * x * x * x))
-    slope = 0.5 * (1.0 + t) + 0.5 * x * (1.0 - t * t) * (c0 * (1.0 + 3.0 * c1 * x * x))
+    out[...] = 0.5 * (1.0 + t) + 0.5 * x * (1.0 - t * t) * (c0 * (1.0 + 3.0 * c1 * x * x))
+
+
+def ffn_back_kernel(rank, ready, own, sib, slope, f_own, f_sib, wide_u, wide_d,
+                    mine, send, g_out):
+    width = wide_u.shape[0]
+    lane = 5 * rank
+    ready()
+    rows = own.shape[0]
     left_own, left_sib = own[:, width : width + lane], sib[:, width : width + lane]
-    u_own, u_sib = e1_own[:, width : width + lane], e1_sib[:, width : width + lane]
     g_ff = jnp.concatenate([own[:, :width], sib[:, :width]], 0)
     pair_own, pair_sib = factors(f_own, rank), factors(f_sib, rank)
     extra = jnp.concatenate([nn(left_own, pair_own[0]), nn(left_sib, pair_sib[0])], 0)
     g_a = (nt(g_ff, wide_d[...]) + extra).astype(BF16)
-    g_f = (g_a.astype(F32) * slope).astype(BF16)
+    g_f = (g_a.astype(F32) * slope[...]).astype(BF16)
     g_h = nt(g_f, wide_u[...])
-    parts = (
-        (mine, gf_mine, 0, pair_own, left_own, u_own),
-        (send, gf_send, rows, pair_sib, left_sib, u_sib),
-    )
-    for out, _, low, factor, _, _ in parts:
+    for out, low, factor in ((mine, 0, pair_own), (send, rows, pair_sib)):
         out[:, :width] = g_h[low : low + rows]
         out[:, width:] = jnp.zeros_like(out[:, width:])
         out[:, width : width + lane] = SCALE * nt(g_f[low : low + rows], factor[1])
-    for _, gout, low, _, left, u in parts:
-        gout[0:rank, :] = tn(left, a[low : low + rows, :])[4 * rank :]
-        gout[rank:, :] = SCALE * tn(u, g_f[low : low + rows])[4 * rank :]
+    g_out[...] = g_f
+
+
+def hidden_kernel(rank, ready, own, sib, e1_own, e1_sib, a, g_f, mine, send):
+    rows = own.shape[0]
+    cut = slice(own.shape[1] - 128, own.shape[1] - 128 + 5 * rank)
+    for out, low, left, u in ((mine, 0, own, e1_own), (send, rows, sib, e1_sib)):
+        out[0:rank, :] = tn(left[:, cut], a[low : low + rows, :])[4 * rank :]
+        out[rank:, :] = SCALE * tn(u[:, cut], g_f[low : low + rows, :])[4 * rank :]
 
 
 def factor_kernel(rank, half, ready, mine, other, err, start, mat, left):
@@ -460,9 +466,9 @@
     ready()
     scale = HEAD_DIM ** (-0.5)
 
-    def row_part(x, low, high):
-        at = iota(x.shape, 0)
-        return jnp.where((at >= low) & (at < high), x, jnp.zeros_like(x))
+    both = (lane, 2 * heads * slots)
+    group, side = iota(both, 0) // rank, iota(both, 1) // (heads * slots)
+    keep = jnp.where(group == 1 + side, jnp.where(side == 0, scale, 1.0), 0.0)
 
     for b in range(micro):
         pick = slice(b * slots, (b + 1) * slots)
@@ -472,16 +478,14 @@
         g_p = nt(kv[b, :, width:], wide_g)
         g_s = (probs * (g_p - jnp.sum(probs * g_p, 0, keepdims=True))).astype(BF16)
         g_q = (scale * collapse_heads(tn(g_s, kv[b, :, :width]), heads)).astype(BF16)
-        g_k = (scale * nn(g_s, wide_q)).astype(BF16)
-        g_v = nn(probs.astype(BF16), wide_g).astype(BF16)
         u_q = lanes(u_rows[pick], 0, rank)
-        u_k = row_part(ukv_t[b], rank, 2 * rank)
-        u_v = row_part(ukv_t[b], 2 * rank, 3 * rank)
-        grad_out = grad_out + SCALE * (tn(u_q, g_q) + nn(u_k, g_k) + nn(u_v, g_v))
+        tall = jnp.concatenate([g_s, probs.astype(BF16)], 1)
+        flat = jnp.concatenate([wide_q, wide_g], 0)
+        inner = (nn(ukv_t[b], tall) * keep).astype(BF16)
+        grad_out = grad_out + SCALE * (tn(u_q, g_q) + nn(inner, flat))
         g_uq = lanes((SCALE * nt(g_q, up)).astype(BF16), 0, rank)
-        g_ukv = row_part((SCALE * nt(up, g_k)).astype(BF16), rank, 2 * rank) + row_part(
-            (SCALE * nt(up, g_v)).astype(BF16), 2 * rank, 3 * rank
-        )
+        inner = (nt(up, flat) * keep).astype(BF16)
+        g_ukv = (SCALE * nt(inner, tall)).astype(BF16)
         grad_in = grad_in + tn(g_uq, hl[b][...]) + nn(g_ukv, h1[b][...])
     mat[0] = grad_in + err[0]
     mat[1] = grad_out + err[1]
@@ -495,16 +499,14 @@
     count = refs[0].shape[0]
     for k in range(count):
         for ref in refs:
-            row = ref[k : k + 1, :]
-            row = row * lax.rsqrt(jnp.sum(row * row, -1, keepdims=True) + 1e-06)
-            if k + 1 < count:
-                block = ref[...]
-                at = iota(block.shape, 0)
-                dots = jnp.sum(block * row, -1, keepdims=True)
-                block = jnp.where(at > k, block - dots * row, block)
-                ref[...] = jnp.where(at == k, row, block)
-            else:
-                ref[k : k + 1, :] = row
+            block = ref[...]
+            row = block[k : k + 1, :]
+            dots = jnp.sum(block * row, -1, keepdims=True)
+            scale = lax.rsqrt(dots[k : k + 1] + 1e-06)
+            row = row * scale
+            at = iota(block.shape, 0)
+            later = jnp.where(at > k, block - (dots * scale) * row, block)
+            ref[...] = jnp.where(at == k, row, later)
 
 
 def ortho_kernel(rank, ready, d_a, d_b, f_a, f_b, mat_d, mat_f, ph_d, ph_f, head, note):
@@ -805,10 +807,9 @@
 
     def lookup(*start):
         ids = jnp.stack([pick(token_ids, (core + b) % micro, 0) for b in range(micro)])
-        ids = after(ids, *start)
         near = ids - shard * held
         inside = (near >= 0) & (near < held)
-        found = jnp.take(embed_table, jnp.clip(near, 0, held - 1), axis=0)
+        found = jnp.take(embed_table, after(jnp.clip(near, 0, held - 1), *start), axis=0)
         found = jnp.where(inside[..., None], found, jnp.zeros_like(found))
         return found[0], found[1]
 
@@ -830,6 +831,15 @@
     pos_rows = pos_table[:tokens]
 
     lefts, rights, ups, downs = [left], [right], [up_part], [down_part]
+
+    def behind(low, high, *gate):
+        for k in range(low, min(high, n)):
+            if gate:
+                ups[-1], downs[-1] = after(ups[-1], *gate), after(downs[-1], *gate)
+            gate = ()
+            ups.append(send(ups[-1], around))
+            downs.append(send(downs[-1], around))
+
     for k in range(1, n):
         gate = []
         if k == 9:
@@ -843,36 +853,29 @@
         lefts.append(send(lefts[-1], around))
         rights.append(send(rights[-1], around))
         if k == 1:
-            ups[-1], downs[-1] = after(ups[-1], lefts[1]), after(downs[-1], lefts[1])
+            ups[-1], downs[-1] = ups[-1], downs[-1]
             ups.append(send(ups[-1], around))
             downs.append(send(downs[-1], around))
             own, given = lookup(lefts[1], rights[1], bias, bias_1, pos_rows, pair_rows)
         if k == 2:
             tok_own, tok_far = shared(own, given, lefts[2], rights[2], ups[1], downs[1])
 
-    def behind(low, high, *gate):
-        for k in range(low, min(high, n)):
-            if gate:
-                ups[-1], downs[-1] = after(ups[-1], *gate), after(downs[-1], *gate)
-            gate = ()
-            ups.append(send(ups[-1], around))
-            downs.append(send(downs[-1], around))
-
     behind(2, 4, lefts[5])
     parts = [tok_own, tok_far] if m > 2 else [tok_own]
     both = tok_own + tok_far if m > 2 else tok_own
     toks = [parts, [across(both, 1)]]
 
-    lefts[-1] = after(lefts[-1], ups[2], downs[2])
     step_a = [*lefts, *rights]
     if whole_blocks:
-        (mat_own,) = call(
-            assemble_kernel,
-            [shaped((width, 2 * width), BF16)],
-            [source, *[Far(x) for x in step_a]],
-            [pltpu.SemaphoreType.DMA((2 * n,))],
-            vmem=58, name="assemble",
-        )
+        mats = []
+        for k in range(4):
+            mats += call(
+                functools.partial(assemble_kernel, k % 2),
+                [shaped((width, width // 2), BF16)],
+                [source, *[Far(x) for x in (lefts, rights)[k // 2]]],
+                [pltpu.SemaphoreType.DMA((n,))],
+                vmem=8, name="assemble",
+            )
         wide_d, f_own, f_other, wide_head, count_row = call(
             functools.partial(unpack_kernel, rank, rd),
             [shaped((2, 5 * rank, width), BF16), shaped((2 * rank, own_hidden), BF16),
@@ -888,7 +891,8 @@
         steps_l, steps_r = [
             jnp.stack([pick(jnp.stack(x), place_at[r], 0) for r in range(n)]) for x in (lefts, rights)
         ]
-        mat_own = jnp.concatenate([steps_l[:, :rd], steps_r[:, :rd]], 2).reshape(width, 2 * width)
+        mats = [x[:, :rd].reshape(width, 2, width // 2) for x in (steps_l, steps_r)]
+        mats = [x[:, j] for x in mats for j in range(2)]
         count_d = 10 * rank // below
         wide_d = steps_l[:, rd:, : count_d * rd].reshape(n, below, count_d, rd)
         wide_d = wide_d.transpose(2, 1, 0, 3).reshape(2, 5 * rank, width)
@@ -899,9 +903,9 @@
         wide_head = last[:, 0].reshape(1, width)
         count_row = jnp.broadcast_to(jnp.sum(last[:, 1, 0]), (1, 128))
     count = count_row[0, 0]
-    behind(4, 5, mat_own)
+    behind(4, 5, *mats)
     f_sib = across(f_other, 1)
-    mat_sib = across(mat_own, 1)
+    mats += [across(x, 1) for x in mats]
 
     h1, xl, hl = [], [], []
     for b in range(micro):
@@ -923,27 +927,28 @@
          shaped((rows, width), BF16), shaped((rows, width), F32), shaped((rows, width), BF16),
          shaped((micro, tokens, heads * slots), F32), shaped((rows, 5 * rank), BF16),
          shaped((width, width), BF16), shaped((rows, width + 128), BF16)],
-        [segment_ids, *h1, *hl, *xl, wide_d, base_gains, bias, mat_own, mat_sib],
+        [segment_ids, *h1, *hl, *xl, wide_d, base_gains, bias, *mats],
         [pltpu.VMEM((micro, tokens, 5 * rank), BF16)],
         vmem=60, flushes=True, name="rows",
     )
     behind(7, n, o)
     ups, downs = [[Far(y) for y in x] for x in (ups, downs)]
     e1_sib = across(e1, 1)
-    f, a, w_up = call(
-        functools.partial(up_kernel, rank),
+    w_up, w_down = call(
+        functools.partial(preload_kernel, n - 1),
+        [Kept((width, own_hidden), BF16), Kept((own_hidden, width), BF16)],
+        [source, Raw(o), *ups[:-1], *downs[:-1]],
+        [pltpu.SemaphoreType.DMA((2, n - 1))],
+        vmem=4, name="preload",
+    )
+    f, a, w_up, w_down, y_mine, y_send = call(
+        functools.partial(ffn_kernel, rank, n - 1),
         [Kept((2 * rows, own_hidden), F32), Kept((2 * rows, own_hidden), BF16),
-         Kept((width, own_hidden), BF16)],
-        [source, Fresh(e1), Fresh(e1_sib), f_own, f_sib, bias_1, *ups],
-        [pltpu.SemaphoreType.DMA((n,))],
-        vmem=10, name="up",
-    )
-    y_mine, y_send, w_down = call(
-        functools.partial(down_kernel, rank),
-        [Kept((rows, width + 128), F32)] * 2 + [Kept((own_hidden, width), BF16)],
-        [source, Fresh(a), f_own, f_sib, *downs],
-        [pltpu.SemaphoreType.DMA((n,))],
-        vmem=10, name="down",
+         Kept((width, own_hidden), BF16), Kept((own_hidden, width), BF16)]
+        + [Kept((rows, width + 128), F32)] * 2,
+        [source, Fresh(e1), Fresh(e1_sib), f_own, f_sib, bias_1, ups[-1], downs[-1], Fresh(w_up), Fresh(w_down)],
+        [pltpu.SemaphoreType.DMA((2, 1))],
+        aliases={8: 2, 9: 3}, vmem=10, name="ffn",
     )
     x2, u_dn, score = call(
         functools.partial(score_kernel, rank),
@@ -952,6 +957,12 @@
         vmem=10, name="score",
     )
     scores = [score] + [across(score, k) for k in range(1, m)]
+    (slope,) = call(
+        slope_kernel,
+        [Kept((2 * rows, own_hidden), F32)],
+        [Fresh(f), Fresh(score)],
+        vmem=6, name="slope",
+    )
     e2, g_end, g_dn, small = call(
         functools.partial(loss_kernel, rank, m),
         [Kept((rows, width + 128), BF16), Kept((rows, width), F32), Kept((5 * rank, width), F32),
@@ -959,12 +970,20 @@
         [*[Fresh(x) for x in scores], Fresh(x2), Fresh(u_dn), pair_rows, count_row, wide_d, base_gains, bias, wide_head],
         vmem=10, name="loss",
     )
-    y_mine, y_send, gf_mine, gf_send = call(
+    e2_sib = across(e2, 1)
+    y_mine, y_send, g_f = call(
         functools.partial(ffn_back_kernel, rank),
-        [Kept((rows, width + 128), F32)] * 2 + [Kept((2 * rank, own_hidden), F32)] * 2,
-        [Fresh(e2), Fresh(across(e2, 1)), Fresh(e1), Fresh(e1_sib), Fresh(f), Fresh(a), f_own, f_sib,
+        [Kept((rows, width + 128), F32)] * 2 + [Kept((2 * rows, own_hidden), BF16)],
+        [Fresh(e2), Fresh(e2_sib), Fresh(slope), f_own, f_sib,
          Fresh(w_up), Fresh(w_down)],
         vmem=14, name="ffn_back",
+    )
+    y_other = across(y_send, 1)
+    gf_mine, gf_send = call(
+        functools.partial(hidden_kernel, rank),
+        [Kept((2 * rank, own_hidden), F32)] * 2,
+        [Fresh(x) for x in (e2, e2_sib, e1, e1_sib, a, g_f)],
+        vmem=6, name="hidden",
     )
     mat_f, left_f = call(
         functools.partial(factor_kernel, rank, half),
@@ -975,7 +994,7 @@
     mat_d, left_d = call(
         functools.partial(rows_back_kernel, micro, rank),
         [Kept((2, 5 * rank, width), F32), Kept((2 * rank + 8, width), F32)],
-        [Fresh(y_mine), Fresh(across(y_send, 1)), Fresh(g_end), Fresh(g_dn), Fresh(small),
+        [Fresh(y_mine), Fresh(y_other), Fresh(g_end), Fresh(g_dn), Fresh(small),
          *[Fresh(x) for x in (x1, e1, u, o, q, p_t, kv, ukv_t, *hl, *h1)],
          wide_d, base_gains, err_d[0, 0].transpose(1, 2, 0), qstart_d[0].transpose(0, 2, 1), Fresh(w_out)],
         vmem=26, name="rows_back",

time: 250 us -> 238 us (0.952)
  starting transfers between devices: 53.8 us -> 43.4 us
  waiting for transfers between devices: 90.4 us -> 82.4 us
  other arithmetic: 6.66 us -> 9.2 us
  local copies, waits for them, and re-layouts: 40.1 us -> 42.6 us
    ppermute x47 -> x50, starting transfers between devices: 51.2 us -> 40.9 us  [send(): return lax.ppermute(x, AXES, perm)]
    ppermute x47 -> x50, waiting for transfers between devices: 82.2 us -> 74.3 us  [send(): return lax.ppermute(x, AXES, perm)]
    unnamed x173 -> x195, local copies, waits for them, and re-layouts: 15.8 us -> 18.1 us
    pallas_call x15 -> x20, Pallas kernels: 56.6 us -> 57.5 us  [call(): pl.pallas_call(kernel, out_shape=tuple((jax.ShapeDtypeStruct(o.shape, o.d...]
  transfers between devices with their start and end apart: 48 -> 51, of which waited for: 29 -> 29; matrix products, arithmetic and copies ran while one was open for 11% -> 14% of each run, Pallas kernels for 14% -> 17%
where the time goes in v1:
time: 238 us; the launch traced here: 237 us
  waiting for transfers between devices  82.4 us (35%)
  Pallas kernels  57.5 us (24%)
  starting transfers between devices  43.4 us (18%)
  local copies, waits for them, and re-layouts  42.6 us (18%)
  other arithmetic  9.2 us (4%)
    ppermute x50, waiting for transfers between devices, send(): return lax.ppermute(x, AXES, perm)  74.3 us
    pallas_call x20, Pallas kernels, call(): pl.pallas_call(kernel, out_shape=tuple((jax.ShapeDtypeStruct(o.shape, o.d...  57.5 us
    ppermute x50, starting transfers between devices, send(): return lax.ppermute(x, AXES, perm)  40.9 us
    unnamed x195, local copies, waits for them, and re-layouts  18.1 us
    gather x1, local copies, waits for them, and re-layouts, lookup(): jnp.take(embed_table, after(jnp.clip(near, 0, held - 1), *start), axis=0)  17.7 us
    all_to_all x1, waiting for transfers between devices, on_device(): notes = lax.all_to_all(note, AXES, 0, 0)  8.17 us
  transfers between devices with their start and end apart: 51, of which 29 were waited for; matrix products, arithmetic and copies ran while one was open for 14% of the time, Pallas kernels for 17%

profile of v1, /device:TPU:0, one launch (start us, length us, event | category | flops | bytes accessed | tf_op | source)
XLA Modules:
  0.0 237.2 jit_solution(12312484540874533170)
XLA Ops:
  2.0 2.8 %split.1 = (bf16[144,1024]{1,0:T(8,128)(2,1)}, bf16[144,1024]{1,0:T(8,128)(2,1)}, bf16[128,2048]{1,0:T(8,128)(2,1)}, bf16[256,1024]{1,0:T(8,128)(2,1)}) custom-call(f32[2,40,128]{2,1,0:T(8,128)} %bitcast.68, f32[16,512]{1,0:T(8,128)} %bitcast.70, f32[1,128]{1,0:T(1,128)} %refs_10_.1, s32[1,16]{1,0:T(1,128)} %reshape_squeeze.3.refs_3_, ...), custom_call_target="tpu_custom_call" | custom-call | tf_op jit(solution)/shard_map/split/pallas_call | solution.py:687
  4.8 3.0 %collective-permute-start = (bf16[144,1024]{1,0:T(8,128)(2,1)}, bf16[144,1024]{1,0:T(8,128)(2,1)S(1)}, u32[]{:S(2)}, u32[]{:S(2)}) collective-permute-start(bf16[144,1024]{1,0:T(8,128)(2,1)} %get-tuple-element.77.refs_1_), channel_id=1, source_target_pairs={{0,4},{1,9},{2,6},{3,11},{4,12},{5,1},{6,14},{7,3},{8,0},{9,17},{1... | collective-permute-start | bytes 884744 | tf_op jit(solution)/shard_map/ppermute | solution.py:755
  7.9 1.6 collective-permute-start.1
  9.4 1.6 collective-permute-start.4
  11.0 1.6 collective-permute-start.5
  14.0 2.3 slice.31.refs_5_.refs_4_.refs_3_
  19.8 17.7 %gather_fusion = bf16[1024,1024]{1,0:T(8,128)(2,1)} fusion(bf16[12568,1024]{1,0:T(8,128)(2,1)} %param.27, s32[1024]{0:T(1024)S(1)} %broadcast_clamp_fusion), kind=kCustom, calls=%fused_computation | custom fusion | bytes 4198400 | tf_op jit(solution)/shard_map/jit(_take)/gather | solution.py:812
  38.1 1.4 collective-permute-start.3
  39.4 1.8 select_select_fusion
  41.2 1.2 slice_bitcast_fusion.refs_0_
  42.4 1.9 collective-permute-done.2.refs_1_.refs_3_
  44.3 3.2 %collective-permute-done.3.refs_2_.refs_11_.refs_3_ = bf16[144,1024]{1,0:T(8,128)(2,1)S(1)} collective-permute-done((bf16[144,1024]{1,0:T(8,128)(2,1)S(1)}, bf16[144,1024]{1,0:T(8,128)(2,1)S(1)}, u32[]{:S(2)}, u32[]{:S(2)}) %collective-permute-start.3) | collective-permute-done | bytes 294944 | tf_op jit(solution)/shard_map/ppermute | solution.py:755
  48.7 1.4 collective-permute-start.9
  51.1 2.3 fusion.refs_0_.refs_1_
  53.4 1.5 collective-permute-start.7
  56.3 1.9 collective-permute-done.9.refs_0_
  59.5 3.3 %collective-permute-done.15.refs_13_.refs_5_ = bf16[144,1024]{1,0:T(8,128)(2,1)S(1)} collective-permute-done((bf16[144,1024]{1,0:T(8,128)(2,1)}, bf16[144,1024]{1,0:T(8,128)(2,1)S(1)}, u32[]{:S(2)}, u32[]{:S(2)}) %collective-permute-start.15) | collective-permute-done | bytes 294944 | tf_op jit(solution)/shard_map/ppermute | solution.py:755
  64.0 1.9 collective-permute-done.10.refs_5_
  67.2 2.4 %collective-permute-done.16.refs_14_.refs_6_ = bf16[144,1024]{1,0:T(8,128)(2,1)} collective-permute-done((bf16[144,1024]{1,0:T(8,128)(2,1)S(1)}, bf16[144,1024]{1,0:T(8,128)(2,1)}, u32[]{:S(2)}, u32[]{:S(2)}) %collective-permute-start.16) | collective-permute-done | bytes 294944 | tf_op jit(solution)/shard_map/ppermute | solution.py:755
  70.1 2.6 %collective-permute-done.11.refs_6_.refs_1_ = bf16[144,1024]{1,0:T(8,128)(2,1)S(1)} collective-permute-done((bf16[144,1024]{1,0:T(8,128)(2,1)S(1)}, bf16[144,1024]{1,0:T(8,128)(2,1)S(1)}, u32[]{:S(2)}, u32[]{:S(2)}) %collective-permute-start.11) | collective-permute-done | bytes 294944 | tf_op jit(solution)/shard_map/ppermute | solution.py:755
  73.9 1.5 collective-permute-start.25
  75.4 1.2 collective-permute-done.17.refs_0_
  76.5 2.3 collective-permute-done.7.refs_1_
  80.3 1.4 collective-permute-start.12
  81.6 2.9 %add.97 = bf16[512,1024]{1,0:T(8,128)(2,1)} add(bf16[512,1024]{1,0:T(8,128)(2,1)} %fusion.refs_0_.refs_1_, bf16[512,1024]{1,0:T(8,128)(2,1)} %copy-done.5) | non-fusion elementwise | flops 524288 | bytes 3145728 | tf_op jit(solution)/shard_map/add | solution.py:865
  84.6 1.6 collective-permute-start.32
  86.2 2.4 collective-permute-done.25.refs_4_
  89.0 2.5 %collective-permute-done.18.refs_16_.refs_8_ = bf16[144,1024]{1,0:T(8,128)(2,1)S(1)} collective-permute-done((bf16[144,1024]{1,0:T(8,128)(2,1)}, bf16[144,1024]{1,0:T(8,128)(2,1)S(1)}, u32[]{:S(2)}, u32[]{:S(2)}) %collective-permute-start.18) | collective-permute-done | bytes 294944 | tf_op jit(solution)/shard_map/ppermute | solution.py:755
  92.6 1.8 assemble.7.refs_13_.refs_4_
  99.0 1.8 assemble.6.refs_12_.refs_3_
  101.9 7.3 %collective-permute-done.13.refs_8_ = bf16[144,1024]{1,0:T(8,128)(2,1)S(1)} collective-permute-done((bf16[144,1024]{1,0:T(8,128)(2,1)}, bf16[144,1024]{1,0:T(8,128)(2,1)S(1)}, u32[]{:S(2)}, u32[]{:S(2)}) %collective-permute-start.13) | collective-permute-done | bytes 294944 | tf_op jit(solution)/shard_map/ppermute | solution.py:755
  109.2 1.0 assemble.5.refs_11_.refs_2_
  111.2 1.9 assemble.4.refs_10_.refs_1_
  113.8 1.4 collective-permute-start.27
  115.2 1.2 copy-done.7
  116.4 3.0 %front.2 = (bf16[512,1024]{1,0:T(8,128)(2,1)S(1)}, f32[16,1024]{1,0:T(8,128)S(1)}, bf16[16,1024]{1,0:T(8,128)(2,1)S(1)}) custom-call(bf16[512,1024]{1,0:T(8,128)(2,1)} %fusion.refs_0_.refs_1_, bf16[512,1024]{1,0:T(8,128)(2,1)S(1)} %copy-done.6, s32[2,512]{1,0:T(2,128)S(1)} %copy-done.83, s32[2,512]{1,0:T(2,128)S(1)} %copy-done.81, ...), custom_call_target="tpu_custom_call" | custom-call | tf_op jit(solution)/shard_map/front/pallas_call | solution.py:687
  119.4 1.0 copy-done.36
  120.6 3.2 %unpack.1 = (bf16[2,40,1024]{2,1,0:T(8,128)(2,1)S(1)}, bf16[16,2048]{1,0:T(8,128)(2,1)S(1)}, bf16[16,2048]{1,0:T(8,128)(2,1)S(1)}, f32[1,1024]{1,0:T(1,128)S(1)}, f32[1,128]{1,0:T(1,128)}) custom-call(s32[8,2,8]{2,1,0:T(2,128)S(1)} %copy-done.68, bf16[144,1024]{1,0:T(8,128)(2,1)S(1)} %copy-done.43, bf16[144,1024]{1,0:T(8,128)(2,1)S(1)} %copy-done.32, ...), custom_call_target="tpu_custom_call" | custom-call | tf_op jit(solution)/shard_map/unpack/pallas_call | solution.py:687
  124.9 2.8 %front.3 = (bf16[512,1024]{1,0:T(8,128)(2,1)S(1)}, f32[16,1024]{1,0:T(8,128)S(1)}, bf16[16,1024]{1,0:T(8,128)(2,1)S(1)}) custom-call(bf16[512,1024]{1,0:T(8,128)(2,1)} %collective-permute-done.8.refs_0_, s32[2,512]{1,0:T(2,128)S(1)} %copy-done.83, s32[2,512]{1,0:T(2,128)S(1)} %copy-done.81, bf16[512,1024]{1,0:T(8,128)(2,1)S(1)} %copy-done.8, ...), custom_call_target="tpu_custom_call" | custom-call | tf_op jit(solution)/shard_map/front/pallas_call | solution.py:687
  130.0 1.6 collective-permute-start.34
  131.6 1.6 collective-permute-start.28
  133.2 6.4 %collective-permute-done.34.refs_14_ = bf16[256,1024]{1,0:T(8,128)(2,1)} collective-permute-done((bf16[256,1024]{1,0:T(8,128)(2,1)}, bf16[256,1024]{1,0:T(8,128)(2,1)}, u32[]{:S(2)}, u32[]{:S(2)}) %collective-permute-start.34) | collective-permute-done | bytes 524320 | tf_op jit(solution)/shard_map/ppermute | solution.py:755
  139.6 1.5 collective-permute-start.35
  141.1 4.1 %collective-permute-done.28.refs_7_ = bf16[128,2048]{1,0:T(8,128)(2,1)} collective-permute-done((bf16[128,2048]{1,0:T(8,128)(2,1)}, bf16[128,2048]{1,0:T(8,128)(2,1)}, u32[]{:S(2)}, u32[]{:S(2)}) %collective-permute-start.28) | collective-permute-done | bytes 524320 | tf_op jit(solution)/shard_map/ppermute | solution.py:755
  145.2 1.5 collective-permute-start.29
  146.7 14.3 %rows.1 = (bf16[2,512,2048]{2,1,0:T(8,128)(2,1)}, bf16[2,40,512]{2,1,0:T(8,128)(2,1)}, bf16[32,1024]{1,0:T(8,128)(2,1)}, f32[32,1024]{1,0:T(8,128)}, bf16[32,102...) custom-call(s32[2,512]{1,0:T(2,128)} %refs_0_.8, ...), custom_call_target="tpu_custom_call" | custom-call | tf_op jit(solution)/shard_map/rows/pallas_call | solution.py:687
  161.1 1.6 collective-permute-start.36
  163.8 3.4 %preload.1 = (bf16[1024,2048]{1,0:T(8,128)(2,1)S(1)}, bf16[2048,1024]{1,0:T(8,128)(2,1)S(1)}) custom-call(s32[8,2,8]{2,1,0:T(2,128)S(1)} %copy-done.68, bf16[32,1024]{1,0:T(8,128)(2,1)S(1)} %copy-done.56, bf16[128,2048]{1,0:T(8,128)(2,1)S(1)} %copy-done.66, bf16[128,2048]{1,0:T(8,128)(2,1)S(1)} %copy-done.19, ...), custom_call_target="tpu_custom_call" | custom-call | tf_op jit(solution)/shard_map/preload/pallas_call | solution.py:687
  167.2 3.3 %collective-permute-done.36.refs_7_ = bf16[256,1024]{1,0:T(8,128)(2,1)S(1)} collective-permute-done((bf16[256,1024]{1,0:T(8,128)(2,1)}, bf16[256,1024]{1,0:T(8,128)(2,1)S(1)}, u32[]{:S(2)}, u32[]{:S(2)}) %collective-permute-start.36) | collective-permute-done | bytes 524320 | tf_op jit(solution)/shard_map/ppermute | solution.py:755
  170.6 5.6 %collective-permute-done.30.refs_6_ = bf16[128,2048]{1,0:T(8,128)(2,1)S(1)} collective-permute-done((bf16[128,2048]{1,0:T(8,128)(2,1)}, bf16[128,2048]{1,0:T(8,128)(2,1)S(1)}, u32[]{:S(2)}, u32[]{:S(2)}) %collective-permute-start.30) | collective-permute-done | bytes 524320 | tf_op jit(solution)/shard_map/ppermute | solution.py:755
  176.2 3.1 %ffn.1 = (f32[64,2048]{1,0:T(8,128)S(1)}, bf16[64,2048]{1,0:T(8,128)(2,1)S(1)}, bf16[1024,2048]{1,0:T(8,128)(2,1)S(1)}, bf16[2048,1024]{1,0:T(8,128)(2,1)S(1)}, ...) custom-call(s32[8,2,8]{2,1,0:T(2,128)S(1)} %copy-done.68, ...), custom_call_target="tpu_custom_call", output_to_operand_aliasing={{2}: (8, {}), {3}: (9, {})} | custom-call | tf_op jit(solution)/shard_map/ffn/pallas_call | solution.py:687
  179.4 1.4 collective-permute-done.37.refs_2_
  181.8 1.5 collective-permute-start.39
  183.5 2.0 collective-permute-done.39.refs_2_
  188.8 3.0 %ffn_back.1 = (f32[32,1152]{1,0:T(8,128)S(1)}, f32[32,1152]{1,0:T(8,128)S(1)}, bf16[64,2048]{1,0:T(8,128)(2,1)S(1)}) custom-call(bf16[32,1152]{1,0:T(8,128)(2,1)S(1)} %get-tuple-element.102.refs_0_, bf16[32,1152]{1,0:T(8,128)(2,1)S(1)} %collective-permute-done.41.refs_1_, f32[64,2048]{1,0:T(8,128)S(1)} %slope.1.refs_2_, bf16[16,2048]{1,0:T(8,128)(2,1)S(1)} %copy-done.71, ...), custom_call_target="tpu_custom_call" | custom-call | tf_op jit(solution)/shard_map/ffn_back/pallas_call | solution.py:687
  194.1 1.6 collective-permute-start.47
  195.9 7.1 %rows_back.1 = (f32[2,40,1024]{2,1,0:T(8,128)S(1)}, f32[24,1024]{1,0:T(8,128)S(1)}) custom-call(f32[32,1152]{1,0:T(8,128)S(1)} %get-tuple-element.106.refs_0_, f32[32,1152]{1,0:T(8,128)S(1)} %collective-permute-done.42.refs_1_, f32[32,1024]{1,0:T(8,128)S(1)} %get-tuple-element.108.refs_2_, f32[40,1024]{1,0:T(8,128)S(1)} %get-tuple-element.109.refs_3_, ...), custom_call_target="tpu_custom_call" | custom-call | tf_op jit(solution)/shard_map/rows_back/pallas_call | solution.py:687
  204.1 3.6 %collective-permute-done.43 = f32[24,1024]{1,0:T(8,128)S(1)} collective-permute-done((f32[24,1024]{1,0:T(8,128)S(1)}, f32[24,1024]{1,0:T(8,128)S(1)}, u32[]{:S(2)}, u32[]{:S(2)}) %collective-permute-start.43) | collective-permute-done | bytes 98336 | tf_op jit(solution)/shard_map/ppermute | solution.py:755
  209.3 4.1 %collective-permute-done.44 = f32[24,1024]{1,0:T(8,128)S(1)} collective-permute-done((f32[24,1024]{1,0:T(8,128)S(1)}, f32[24,1024]{1,0:T(8,128)S(1)}, u32[]{:S(2)}, u32[]{:S(2)}) %collective-permute-start.44) | collective-permute-done | bytes 98336 | tf_op jit(solution)/shard_map/ppermute | solution.py:755
  214.1 6.7 %collective-permute-done.45.refs_1_ = f32[24,1024]{1,0:T(8,128)S(1)} collective-permute-done((f32[24,1024]{1,0:T(8,128)S(1)}, f32[24,1024]{1,0:T(8,128)S(1)}, u32[]{:S(2)}, u32[]{:S(2)}) %collective-permute-start.45) | collective-permute-done | bytes 98336 | tf_op jit(solution)/shard_map/ppermute | solution.py:755
  220.8 3.1 %ortho.1 = (f32[2,8,1024]{2,1,0:T(8,128)S(1)}, f32[8,4096]{1,0:T(8,128)S(1)}, f32[1,1024]{1,0:T(1,128)S(1)}, f32[32,8,128]{2,1,0:T(8,128)}) custom-call(f32[24,1024]{1,0:T(8,128)S(1)} %add.99.refs_0_, f32[24,1024]{1,0:T(8,128)S(1)} %collective-permute-done.45.refs_1_, f32[8,4096]{1,0:T(8,128)S(1)} %add.101.refs_2_, ...), custom_call_target="tpu_custom_call" | custom-call | tf_op jit(solution)/shard_map/ortho/pallas_call | solution.py:687
  223.8 2.6 %all-to-all-start = ((f32[32,8,128]{2,1,0:T(8,128)}), f32[32,8,128]{2,1,0:T(8,128)S(1)}, u32[]{:S(2)}, u32[]{:S(2)}) async-start(f32[32,8,128]{2,1,0:T(8,128)} %get-tuple-element.125), calls=%async_computation | async-start | bytes 262144 | tf_op jit(solution)/shard_map/all_to_all | solution.py:1019
  226.5 8.2 %all-to-all-done.refs_0_ = f32[32,8,128]{2,1,0:T(8,128)S(1)} async-done(((f32[32,8,128]{2,1,0:T(8,128)}), f32[32,8,128]{2,1,0:T(8,128)S(1)}, u32[]{:S(2)}, u32[]{:S(2)}) %all-to-all-start) | async-done | bytes 131104 | tf_op jit(solution)/shard_map/all_to_all | solution.py:1019
  234.7 2.3 final.1
  (297 shorter events, 40.7 us)
Async XLA Ops:
  4.8 12.7 %collective-permute-start = (bf16[144,1024]{1,0:T(8,128)(2,1)}, bf16[144,1024]{1,0:T(8,128)(2,1)S(1)}, u32[]{:S(2)}, u32[]{:S(2)}) collective-permute-start(bf16[144,1024]{1,0:T(8,128)(2,1)} %get-tuple-element.77.refs_1_), channel_id=1, source_target_pairs={{0,4},{1,9},{2,6},{3,11},{4,12},{5,1},{6,14},{7,3},{8,0},{9,17},{1... | collective-permute-start | bytes 884744 | tf_op jit(solution)/shard_map/ppermute | solution.py:755
  7.9 9.7 %collective-permute-start.1 = (bf16[144,1024]{1,0:T(8,128)(2,1)}, bf16[144,1024]{1,0:T(8,128)(2,1)S(1)}, u32[]{:S(2)}, u32[]{:S(2)}) collective-permute-start(bf16[144,1024]{1,0:T(8,128)(2,1)} %get-tuple-element.78.refs_9_.refs_1_), channel_id=1, source_target_pairs={{0,4},{1,9},{2,6},{3,11},{4,12},{5,1},{6,14},{7,3},{8,0},{9,17},{1... | collective-permute-start | bytes 884744 | tf_op jit(solution)/shard_map/ppermute | solution.py:755
  9.4 32.9 %collective-permute-start.4 = (bf16[128,2048]{1,0:T(8,128)(2,1)}, bf16[128,2048]{1,0:T(8,128)(2,1)S(1)}, u32[]{:S(2)}, u32[]{:S(2)}) collective-permute-start(bf16[128,2048]{1,0:T(8,128)(2,1)} %get-tuple-element.79.refs_2_), channel_id=1, source_target_pairs={{0,4},{1,9},{2,6},{3,11},{4,12},{5,1},{6,14},{7,3},{8,0},{9,17},{1... | collective-permute-start | bytes 1572872 | tf_op jit(solution)/shard_map/ppermute | solution.py:755
  11.0 31.4 %collective-permute-start.5 = (bf16[256,1024]{1,0:T(8,128)(2,1)}, bf16[256,1024]{1,0:T(8,128)(2,1)S(1)}, u32[]{:S(2)}, u32[]{:S(2)}) collective-permute-start(bf16[256,1024]{1,0:T(8,128)(2,1)} %get-tuple-element.80.refs_9_), channel_id=1, source_target_pairs={{0,4},{1,9},{2,6},{3,11},{4,12},{5,1},{6,14},{7,3},{8,0},{9,17},{1... | collective-permute-start | bytes 1572872 | tf_op jit(solution)/shard_map/ppermute | solution.py:755
  19.8 17.8 %copy-start.31 = (bf16[144,1024]{1,0:T(8,128)(2,1)S(1)}, bf16[144,1024]{1,0:T(8,128)(2,1)}, u32[]{:S(2)}) copy-start(bf16[144,1024]{1,0:T(8,128)(2,1)} %copy-done.30) | copy-start | bytes 884740
  19.8 18.3 %copy-start.34 = (bf16[144,1024]{1,0:T(8,128)(2,1)S(1)}, bf16[144,1024]{1,0:T(8,128)(2,1)}, u32[]{:S(2)}) copy-start(bf16[144,1024]{1,0:T(8,128)(2,1)} %copy-done.33) | copy-start | bytes 884740
  37.5 6.7 %collective-permute-start.2 = (bf16[144,1024]{1,0:T(8,128)(2,1)S(1)}, bf16[144,1024]{1,0:T(8,128)(2,1)S(1)}, u32[]{:S(2)}, u32[]{:S(2)}) collective-permute-start(bf16[144,1024]{1,0:T(8,128)(2,1)S(1)} %copy-done.31), channel_id=1, source_target_pairs={{0,4},{1,9},{2,6},{3,11},{4,12},{5,1},{6,14},{7,3},{8,0},{9,17},{1... | collective-permute-start | bytes 884744 | tf_op jit(solution)/shard_map/ppermute | solution.py:755
  38.1 9.4 %collective-permute-start.3 = (bf16[144,1024]{1,0:T(8,128)(2,1)S(1)}, bf16[144,1024]{1,0:T(8,128)(2,1)S(1)}, u32[]{:S(2)}, u32[]{:S(2)}) collective-permute-start(bf16[144,1024]{1,0:T(8,128)(2,1)S(1)} %copy-done.34), channel_id=1, source_target_pairs={{0,4},{1,9},{2,6},{3,11},{4,12},{5,1},{6,14},{7,3},{8,0},{9,17},{1... | collective-permute-start | bytes 884744 | tf_op jit(solution)/shard_map/ppermute | solution.py:755
  48.2 2.9 %collective-permute-start.6 = (bf16[512,1024]{1,0:T(8,128)(2,1)}, bf16[512,1024]{1,0:T(8,128)(2,1)S(1)}, u32[]{:S(2)}, u32[]{:S(2)}) collective-permute-start(bf16[512,1024]{1,0:T(8,128)(2,1)} %after.15), channel_id=1, source_target_pairs={{0,1},{1,0},{2,3},{3,2},{4,5},{5,4},{6,7},{7,6},{8,9},{9,8},{10,11... | collective-permute-start | bytes 3145736 | tf_op jit(solution)/shard_map/ppermute | solution.py:755
  48.2 6.9 %collective-permute-start.14 = (bf16[144,1024]{1,0:T(8,128)(2,1)}, bf16[144,1024]{1,0:T(8,128)(2,1)S(1)}, u32[]{:S(2)}, u32[]{:S(2)}) collective-permute-start(bf16[144,1024]{1,0:T(8,128)(2,1)} %copy-done.16), channel_id=1, source_target_pairs={{0,4},{1,9},{2,6},{3,11},{4,12},{5,1},{6,14},{7,3},{8,0},{9,17},{1... | collective-permute-start | bytes 884744 | tf_op jit(solution)/shard_map/ppermute | solution.py:755
  48.7 9.6 %collective-permute-start.9 = (bf16[144,1024]{1,0:T(8,128)(2,1)}, bf16[144,1024]{1,0:T(8,128)(2,1)S(1)}, u32[]{:S(2)}, u32[]{:S(2)}) collective-permute-start(bf16[144,1024]{1,0:T(8,128)(2,1)} %copy-done.13), channel_id=1, source_target_pairs={{0,4},{1,9},{2,6},{3,11},{4,12},{5,1},{6,14},{7,3},{8,0},{9,17},{1... | collective-permute-start | bytes 884744 | tf_op jit(solution)/shard_map/ppermute | solution.py:755
  53.4 25.4 %collective-permute-start.7 = (bf16[512,1024]{1,0:T(8,128)(2,1)}, bf16[512,1024]{1,0:T(8,128)(2,1)S(1)}, u32[]{:S(2)}, u32[]{:S(2)}) collective-permute-start(bf16[512,1024]{1,0:T(8,128)(2,1)} %fusion.refs_0_.refs_1_), channel_id=1, source_target_pairs={{0,2},{1,3},{2,0},{3,1},{4,6},{5,7},{6,4},{7,5},{8,10},{9,11},{10,... | collective-permute-start | bytes 3145736 | tf_op jit(solution)/shard_map/ppermute | solution.py:755
  55.8 6.9 %collective-permute-start.15 = (bf16[144,1024]{1,0:T(8,128)(2,1)}, bf16[144,1024]{1,0:T(8,128)(2,1)S(1)}, u32[]{:S(2)}, u32[]{:S(2)}) collective-permute-start(bf16[144,1024]{1,0:T(8,128)(2,1)} %after.18.refs_12_.refs_4_), channel_id=1, source_target_pairs={{0,4},{1,9},{2,6},{3,11},{4,12},{5,1},{6,14},{7,3},{8,0},{9,17},{1... | collective-permute-start | bytes 884744 | tf_op jit(solution)/shard_map/ppermute | solution.py:755
  59.0 6.9 %collective-permute-start.10 = (bf16[144,1024]{1,0:T(8,128)(2,1)}, bf16[144,1024]{1,0:T(8,128)(2,1)S(1)}, u32[]{:S(2)}, u32[]{:S(2)}) collective-permute-start(bf16[144,1024]{1,0:T(8,128)(2,1)} %after.16.refs_4_), channel_id=1, source_target_pairs={{0,4},{1,9},{2,6},{3,11},{4,12},{5,1},{6,14},{7,3},{8,0},{9,17},{1... | collective-permute-start | bytes 884744 | tf_op jit(solution)/shard_map/ppermute | solution.py:755
  62.8 6.8 %collective-permute-start.16 = (bf16[144,1024]{1,0:T(8,128)(2,1)S(1)}, bf16[144,1024]{1,0:T(8,128)(2,1)}, u32[]{:S(2)}, u32[]{:S(2)}) collective-permute-start(bf16[144,1024]{1,0:T(8,128)(2,1)S(1)} %collective-permute-done.15.refs_13_.refs_5_), channel_id=1, source_target_pairs={{0,4},{1,9},{2,6},{3,11},{4,12},{5,1},{6,14},{7,3},{8,0},{9,17},{1... | collective-permute-start | bytes 884744 | tf_op jit(solution)/shard_map/ppermute | solution.py:755
  65.9 6.7 %collective-permute-start.11 = (bf16[144,1024]{1,0:T(8,128)(2,1)S(1)}, bf16[144,1024]{1,0:T(8,128)(2,1)S(1)}, u32[]{:S(2)}, u32[]{:S(2)}) collective-permute-start(bf16[144,1024]{1,0:T(8,128)(2,1)S(1)} %collective-permute-done.10.refs_5_), channel_id=1, source_target_pairs={{0,4},{1,9},{2,6},{3,11},{4,12},{5,1},{6,14},{7,3},{8,0},{9,17},{1... | collective-permute-start | bytes 884744 | tf_op jit(solution)/shard_map/ppermute | solution.py:755
  69.6 6.9 %collective-permute-start.17 = (bf16[144,1024]{1,0:T(8,128)(2,1)}, bf16[144,1024]{1,0:T(8,128)(2,1)S(1)}, u32[]{:S(2)}, u32[]{:S(2)}) collective-permute-start(bf16[144,1024]{1,0:T(8,128)(2,1)} %collective-permute-done.16.refs_14_.refs_6_), channel_id=1, source_target_pairs={{0,4},{1,9},{2,6},{3,11},{4,12},{5,1},{6,14},{7,3},{8,0},{9,17},{1... | collective-permute-start | bytes 884744 | tf_op jit(solution)/shard_map/ppermute | solution.py:755
  73.4 11.2 %collective-permute-start.31 = (bf16[256,1024]{1,0:T(8,128)(2,1)}, bf16[256,1024]{1,0:T(8,128)(2,1)}, u32[]{:S(2)}, u32[]{:S(2)}) collective-permute-start(bf16[256,1024]{1,0:T(8,128)(2,1)} %after.24.refs_10_), channel_id=1, source_target_pairs={{0,4},{1,9},{2,6},{3,11},{4,12},{5,1},{6,14},{7,3},{8,0},{9,17},{1... | collective-permute-start | bytes 1572872 | tf_op jit(solution)/shard_map/ppermute | solution.py:755
  73.9 17.7 %copy-start.17 = (bf16[144,1024]{1,0:T(8,128)(2,1)S(1)}, bf16[144,1024]{1,0:T(8,128)(2,1)}, u32[]{:S(2)}) copy-start(bf16[144,1024]{1,0:T(8,128)(2,1)} %copy-done.16) | copy-start | bytes 884740
  73.9 17.7 %copy-start.29 = (bf16[144,1024]{1,0:T(8,128)(2,1)S(1)}, bf16[144,1024]{1,0:T(8,128)(2,1)}, u32[]{:S(2)}) copy-start(bf16[144,1024]{1,0:T(8,128)(2,1)} %after.18.refs_12_.refs_4_) | copy-start | bytes 884740
  73.9 17.7 %copy-start.44 = (bf16[144,1024]{1,0:T(8,128)(2,1)S(1)}, bf16[144,1024]{1,0:T(8,128)(2,1)}, u32[]{:S(2)}) copy-start(bf16[144,1024]{1,0:T(8,128)(2,1)} %get-tuple-element.78.refs_9_.refs_1_) | copy-start | bytes 884740
  73.9 17.7 %copy-start.68 = (s32[8,2,8]{2,1,0:T(2,128)S(1)}, s32[8,2,8]{2,1,0:T(2,128)}, u32[]{:S(2)}) copy-start(s32[8,2,8]{2,1,0:T(2,128)} %constant.86.clone.refs_0_) | copy-start | bytes 1540
  73.9 14.6 %collective-permute-start.25 = (bf16[128,2048]{1,0:T(8,128)(2,1)}, bf16[128,2048]{1,0:T(8,128)(2,1)}, u32[]{:S(2)}, u32[]{:S(2)}) collective-permute-start(bf16[128,2048]{1,0:T(8,128)(2,1)} %after.20.refs_3_), channel_id=1, source_target_pairs={{0,4},{1,9},{2,6},{3,11},{4,12},{5,1},{6,14},{7,3},{8,0},{9,17},{1... | collective-permute-start | bytes 1572872 | tf_op jit(solution)/shard_map/ppermute | solution.py:755
  79.8 11.8 %collective-permute-start.18 = (bf16[144,1024]{1,0:T(8,128)(2,1)}, bf16[144,1024]{1,0:T(8,128)(2,1)S(1)}, u32[]{:S(2)}, u32[]{:S(2)}) collective-permute-start(bf16[144,1024]{1,0:T(8,128)(2,1)} %after.19.refs_15_.refs_7_), channel_id=1, source_target_pairs={{0,4},{1,9},{2,6},{3,11},{4,12},{5,1},{6,14},{7,3},{8,0},{9,17},{1... | collective-permute-start | bytes 884744 | tf_op jit(solution)/shard_map/ppermute | solution.py:755
  80.3 14.4 %collective-permute-start.12 = (bf16[144,1024]{1,0:T(8,128)(2,1)S(1)}, bf16[144,1024]{1,0:T(8,128)(2,1)S(1)}, u32[]{:S(2)}, u32[]{:S(2)}) collective-permute-start(bf16[144,1024]{1,0:T(8,128)(2,1)S(1)} %copy-done.10), channel_id=1, source_target_pairs={{0,4},{1,9},{2,6},{3,11},{4,12},{5,1},{6,14},{7,3},{8,0},{9,17},{1... | collective-permute-start | bytes 884744 | tf_op jit(solution)/shard_map/ppermute | solution.py:755
  84.6 39.8 %collective-permute-start.8 = (bf16[512,1024]{1,0:T(8,128)(2,1)}, bf16[512,1024]{1,0:T(8,128)(2,1)}, u32[]{:S(2)}, u32[]{:S(2)}) collective-permute-start(bf16[512,1024]{1,0:T(8,128)(2,1)} %add.97), channel_id=1, source_target_pairs={{0,1},{1,0},{2,3},{3,2},{4,5},{5,4},{6,7},{7,6},{8,9},{9,8},{10,11... | collective-permute-start | bytes 3145736 | tf_op jit(solution)/shard_map/ppermute | solution.py:755
  84.6 28.5 %collective-permute-start.32 = (bf16[256,1024]{1,0:T(8,128)(2,1)}, bf16[256,1024]{1,0:T(8,128)(2,1)}, u32[]{:S(2)}, u32[]{:S(2)}) collective-permute-start(bf16[256,1024]{1,0:T(8,128)(2,1)} %collective-permute-done.31.refs_11_), channel_id=1, source_target_pairs={{0,4},{1,9},{2,6},{3,11},{4,12},{5,1},{6,14},{7,3},{8,0},{9,17},{1... | collective-permute-start | bytes 1572872 | tf_op jit(solution)/shard_map/ppermute | solution.py:755
  88.5 25.2 %collective-permute-start.26 = (bf16[128,2048]{1,0:T(8,128)(2,1)}, bf16[128,2048]{1,0:T(8,128)(2,1)}, u32[]{:S(2)}, u32[]{:S(2)}) collective-permute-start(bf16[128,2048]{1,0:T(8,128)(2,1)} %collective-permute-done.25.refs_4_), channel_id=1, source_target_pairs={{0,4},{1,9},{2,6},{3,11},{4,12},{5,1},{6,14},{7,3},{8,0},{9,17},{1... | collective-permute-start | bytes 1572872 | tf_op jit(solution)/shard_map/ppermute | solution.py:755
  94.4 37.2 %collective-permute-start.22 = (bf16[1024,512]{1,0:T(8,128)(2,1)S(1)}, bf16[1024,512]{1,0:T(8,128)(2,1)}, u32[]{:S(2)}, u32[]{:S(2)}) collective-permute-start(bf16[1024,512]{1,0:T(8,128)(2,1)S(1)} %assemble.7.refs_13_.refs_4_), channel_id=1, source_target_pairs={{0,1},{1,0},{2,3},{3,2},{4,5},{5,4},{6,7},{7,6},{8,9},{9,8},{10,11... | collective-permute-start | bytes 3145736 | tf_op jit(solution)/shard_map/ppermute | solution.py:755
  95.5 13.6 %collective-permute-start.13 = (bf16[144,1024]{1,0:T(8,128)(2,1)}, bf16[144,1024]{1,0:T(8,128)(2,1)S(1)}, u32[]{:S(2)}, u32[]{:S(2)}) collective-permute-start(bf16[144,1024]{1,0:T(8,128)(2,1)} %after.17.refs_7_), channel_id=1, source_target_pairs={{0,4},{1,9},{2,6},{3,11},{4,12},{5,1},{6,14},{7,3},{8,0},{9,17},{1... | collective-permute-start | bytes 884744 | tf_op jit(solution)/shard_map/ppermute | solution.py:755
  113.2 16.8 %collective-permute-start.33 = (bf16[256,1024]{1,0:T(8,128)(2,1)}, bf16[256,1024]{1,0:T(8,128)(2,1)}, u32[]{:S(2)}, u32[]{:S(2)}) collective-permute-start(bf16[256,1024]{1,0:T(8,128)(2,1)} %after.25.refs_12_), channel_id=1, source_target_pairs={{0,4},{1,9},{2,6},{3,11},{4,12},{5,1},{6,14},{7,3},{8,0},{9,17},{1... | collective-permute-start | bytes 1572872 | tf_op jit(solution)/shard_map/ppermute | solution.py:755
  113.8 16.3 %collective-permute-start.27 = (bf16[128,2048]{1,0:T(8,128)(2,1)}, bf16[128,2048]{1,0:T(8,128)(2,1)}, u32[]{:S(2)}, u32[]{:S(2)}) collective-permute-start(bf16[128,2048]{1,0:T(8,128)(2,1)} %after.21.refs_5_), channel_id=1, source_target_pairs={{0,4},{1,9},{2,6},{3,11},{4,12},{5,1},{6,14},{7,3},{8,0},{9,17},{1... | collective-permute-start | bytes 1572872 | tf_op jit(solution)/shard_map/ppermute | solution.py:755
  120.4 26.3 %collective-permute-start.21 = (bf16[1024,512]{1,0:T(8,128)(2,1)S(1)}, bf16[1024,512]{1,0:T(8,128)(2,1)}, u32[]{:S(2)}, u32[]{:S(2)}) collective-permute-start(bf16[1024,512]{1,0:T(8,128)(2,1)S(1)} %copy-done.2), channel_id=1, source_target_pairs={{0,1},{1,0},{2,3},{3,2},{4,5},{5,4},{6,7},{7,6},{8,9},{9,8},{10,11... | collective-permute-start | bytes 3145736 | tf_op jit(solution)/shard_map/ppermute | solution.py:755
  124.4 22.3 %collective-permute-start.20 = (bf16[1024,512]{1,0:T(8,128)(2,1)S(1)}, bf16[1024,512]{1,0:T(8,128)(2,1)}, u32[]{:S(2)}, u32[]{:S(2)}) collective-permute-start(bf16[1024,512]{1,0:T(8,128)(2,1)S(1)} %copy-done.4), channel_id=1, source_target_pairs={{0,1},{1,0},{2,3},{3,2},{4,5},{5,4},{6,7},{7,6},{8,9},{9,8},{10,11... | collective-permute-start | bytes 3145736 | tf_op jit(solution)/shard_map/ppermute | solution.py:755
  130.0 16.7 %collective-permute-start.19 = (bf16[1024,512]{1,0:T(8,128)(2,1)}, bf16[1024,512]{1,0:T(8,128)(2,1)}, u32[]{:S(2)}, u32[]{:S(2)}) collective-permute-start(bf16[1024,512]{1,0:T(8,128)(2,1)} %assemble.4.refs_10_.refs_1_), channel_id=1, source_target_pairs={{0,1},{1,0},{2,3},{3,2},{4,5},{5,4},{6,7},{7,6},{8,9},{9,8},{10,11... | collective-permute-start | bytes 3145736 | tf_op jit(solution)/shard_map/ppermute | solution.py:755
  130.0 9.5 %collective-permute-start.34 = (bf16[256,1024]{1,0:T(8,128)(2,1)}, bf16[256,1024]{1,0:T(8,128)(2,1)}, u32[]{:S(2)}, u32[]{:S(2)}) collective-permute-start(bf16[256,1024]{1,0:T(8,128)(2,1)} %after.26.refs_13_), channel_id=1, source_target_pairs={{0,4},{1,9},{2,6},{3,11},{4,12},{5,1},{6,14},{7,3},{8,0},{9,17},{1... | collective-permute-start | bytes 1572872 | tf_op jit(solution)/shard_map/ppermute | solution.py:755
  131.6 13.6 %collective-permute-start.28 = (bf16[128,2048]{1,0:T(8,128)(2,1)}, bf16[128,2048]{1,0:T(8,128)(2,1)}, u32[]{:S(2)}, u32[]{:S(2)}) collective-permute-start(bf16[128,2048]{1,0:T(8,128)(2,1)} %after.22.refs_6_), channel_id=1, source_target_pairs={{0,4},{1,9},{2,6},{3,11},{4,12},{5,1},{6,14},{7,3},{8,0},{9,17},{1... | collective-permute-start | bytes 1572872 | tf_op jit(solution)/shard_map/ppermute | solution.py:755
  139.6 21.5 %collective-permute-start.35 = (bf16[256,1024]{1,0:T(8,128)(2,1)}, bf16[256,1024]{1,0:T(8,128)(2,1)}, u32[]{:S(2)}, u32[]{:S(2)}) collective-permute-start(bf16[256,1024]{1,0:T(8,128)(2,1)} %collective-permute-done.34.refs_14_), channel_id=1, source_target_pairs={{0,4},{1,9},{2,6},{3,11},{4,12},{5,1},{6,14},{7,3},{8,0},{9,17},{1... | collective-permute-start | bytes 1572872 | tf_op jit(solution)/shard_map/ppermute | solution.py:755
  145.2 17.6 %collective-permute-start.29 = (bf16[128,2048]{1,0:T(8,128)(2,1)}, bf16[128,2048]{1,0:T(8,128)(2,1)}, u32[]{:S(2)}, u32[]{:S(2)}) collective-permute-start(bf16[128,2048]{1,0:T(8,128)(2,1)} %collective-permute-done.28.refs_7_), channel_id=1, source_target_pairs={{0,4},{1,9},{2,6},{3,11},{4,12},{5,1},{6,14},{7,3},{8,0},{9,17},{1... | collective-permute-start | bytes 1572872 | tf_op jit(solution)/shard_map/ppermute | solution.py:755
  146.7 17.0 %copy-start.67 = (bf16[256,1024]{1,0:T(8,128)(2,1)S(1)}, bf16[256,1024]{1,0:T(8,128)(2,1)}, u32[]{:S(2)}) copy-start(bf16[256,1024]{1,0:T(8,128)(2,1)} %get-tuple-element.80.refs_9_) | copy-start | bytes 1572868
  161.1 9.4 %collective-permute-start.36 = (bf16[256,1024]{1,0:T(8,128)(2,1)}, bf16[256,1024]{1,0:T(8,128)(2,1)S(1)}, u32[]{:S(2)}, u32[]{:S(2)}) collective-permute-start(bf16[256,1024]{1,0:T(8,128)(2,1)} %after.27.refs_15_), channel_id=1, source_target_pairs={{0,4},{1,9},{2,6},{3,11},{4,12},{5,1},{6,14},{7,3},{8,0},{9,17},{1... | collective-permute-start | bytes 1572872 | tf_op jit(solution)/shard_map/ppermute | solution.py:755
  162.7 13.4 %collective-permute-start.30 = (bf16[128,2048]{1,0:T(8,128)(2,1)}, bf16[128,2048]{1,0:T(8,128)(2,1)S(1)}, u32[]{:S(2)}, u32[]{:S(2)}) collective-permute-start(bf16[128,2048]{1,0:T(8,128)(2,1)} %after.23.refs_8_), channel_id=1, source_target_pairs={{0,4},{1,9},{2,6},{3,11},{4,12},{5,1},{6,14},{7,3},{8,0},{9,17},{1... | collective-permute-start | bytes 1572872 | tf_op jit(solution)/shard_map/ppermute | solution.py:755
  163.3 3.9 %collective-permute-start.23 = (bf16[32,1152]{1,0:T(8,128)(2,1)S(1)}, bf16[32,1152]{1,0:T(8,128)(2,1)S(1)}, u32[]{:S(2)}, u32[]{:S(2)}) collective-permute-start(bf16[32,1152]{1,0:T(8,128)(2,1)S(1)} %copy-done.58), channel_id=1, source_target_pairs={{0,1},{1,0},{2,3},{3,2},{4,5},{5,4},{6,7},{7,6},{8,9},{9,8},{10,11... | collective-permute-start | bytes 221192 | tf_op jit(solution)/shard_map/ppermute | solution.py:755
  163.3 3.9 %collective-permute-start.24 = (bf16[16,2048]{1,0:T(8,128)(2,1)S(1)}, bf16[16,2048]{1,0:T(8,128)(2,1)S(1)}, u32[]{:S(2)}, u32[]{:S(2)}) collective-permute-start(bf16[16,2048]{1,0:T(8,128)(2,1)S(1)} %copy-done.92), channel_id=1, source_target_pairs={{0,1},{1,0},{2,3},{3,2},{4,5},{5,4},{6,7},{7,6},{8,9},{9,8},{10,11... | collective-permute-start | bytes 196616 | tf_op jit(solution)/shard_map/ppermute | solution.py:755
  179.4 1.4 collective-permute-start.37
  181.6 1.9 collective-permute-start.38
  181.8 3.8 %collective-permute-start.39 = (f32[32,128]{1,0:T(8,128)S(1)}, f32[32,128]{1,0:T(8,128)S(1)}, u32[]{:S(2)}, u32[]{:S(2)}) collective-permute-start(f32[32,128]{1,0:T(8,128)S(1)} %get-tuple-element.98.refs_0_.refs_1_), channel_id=1, source_target_pairs={{0,2},{1,3},{2,0},{3,1},{4,6},{5,7},{6,4},{7,5},{8,10},{9,11},{10,... | collective-permute-start | bytes 49160 | tf_op jit(solution)/shard_map/ppermute | solution.py:755
  183.3 3.2 %collective-permute-start.40 = (f32[32,128]{1,0:T(8,128)S(1)}, f32[32,128]{1,0:T(8,128)S(1)}, u32[]{:S(2)}, u32[]{:S(2)}) collective-permute-start(f32[32,128]{1,0:T(8,128)S(1)} %get-tuple-element.98.refs_0_.refs_1_), channel_id=1, source_target_pairs={{0,3},{1,2},{2,1},{3,0},{4,7},{5,6},{6,5},{7,4},{8,11},{9,10},{10,... | collective-permute-start | bytes 49160 | tf_op jit(solution)/shard_map/ppermute | solution.py:755
  187.4 1.3 collective-permute-start.41
  192.3 1.4 collective-permute-start.46
  192.5 3.3 %collective-permute-start.42 = (f32[32,1152]{1,0:T(8,128)S(1)}, f32[32,1152]{1,0:T(8,128)S(1)}, u32[]{:S(2)}, u32[]{:S(2)}) collective-permute-start(f32[32,1152]{1,0:T(8,128)S(1)} %get-tuple-element.107), channel_id=1, source_target_pairs={{0,1},{1,0},{2,3},{3,2},{4,5},{5,4},{6,7},{7,6},{8,9},{9,8},{10,11... | collective-permute-start | bytes 442376 | tf_op jit(solution)/shard_map/ppermute | solution.py:755
  194.1 9.4 %collective-permute-start.47 = (f32[8,4096]{1,0:T(8,128)S(1)}, f32[8,4096]{1,0:T(8,128)S(1)}, u32[]{:S(2)}, u32[]{:S(2)}) collective-permute-start(f32[8,4096]{1,0:T(8,128)S(1)} %get-tuple-element.122), channel_id=1, source_target_pairs={{0,4},{1,5},{2,6},{3,7},{4,0},{5,1},{6,2},{7,3},{8,12},{9,13},{10,... | collective-permute-start | bytes 393224 | tf_op jit(solution)/shard_map/ppermute | solution.py:755
  203.0 31.7 %copy-start.73 = (f32[1,128,2,40]{1,3,2,0:T(8,128)S(1)}, f32[1,128,2,40]{1,3,2,0:T(8,128)}, u32[]{:S(2)}) copy-start(f32[1,128,2,40]{1,3,2,0:T(8,128)} %param.35) | copy-start | bytes 122884
  203.0 31.7 %copy-start.74 = (f32[1,512,16]{1,2,0:T(8,128)S(1)}, f32[1,512,16]{1,2,0:T(8,128)}, u32[]{:S(2)}) copy-start(f32[1,512,16]{1,2,0:T(8,128)} %param.36) | copy-start | bytes 98308
  203.0 31.7 %copy-start.80 = (f32[1,128,2,40]{1,3,2,0:T(8,128)S(1)}, f32[1,128,2,40]{1,3,2,0:T(8,128)}, u32[]{:S(2)}) copy-start(f32[1,128,2,40]{1,3,2,0:T(8,128)} %param.38) | copy-start | bytes 122884
  203.0 31.7 %copy-start.82 = (f32[1,512,16]{1,2,0:T(8,128)S(1)}, f32[1,512,16]{1,2,0:T(8,128)}, u32[]{:S(2)}) copy-start(f32[1,512,16]{1,2,0:T(8,128)} %param.39) | copy-start | bytes 98308
  203.0 31.7 %copy-start.88 = (f32[1,128]{1,0:T(1,128)S(1)}, f32[1,128]{1,0:T(1,128)}, u32[]{:S(2)}) copy-start(f32[1,128]{1,0:T(1,128)} %refs_10_.1) | copy-start | bytes 1540
  203.0 31.7 %copy-start.89 = (f32[1,128]{1,0:T(1,128)S(1)}, f32[1,128]{1,0:T(1,128)}, u32[]{:S(2)}) copy-start(f32[1,128]{1,0:T(1,128)} %refs_13_.1) | copy-start | bytes 1540
  203.1 4.7 %collective-permute-start.43 = (f32[24,1024]{1,0:T(8,128)S(1)}, f32[24,1024]{1,0:T(8,128)S(1)}, u32[]{:S(2)}, u32[]{:S(2)}) collective-permute-start(f32[24,1024]{1,0:T(8,128)S(1)} %get-tuple-element.117), channel_id=1, source_target_pairs={{0,4},{1,5},{2,6},{3,7},{4,0},{5,1},{6,2},{7,3},{8,12},{9,13},{10,... | collective-permute-start | bytes 294920 | tf_op jit(solution)/shard_map/ppermute | solution.py:755
  203.6 5.1 %collective-permute-start.48 = (f32[8,4096]{1,0:T(8,128)S(1)}, f32[8,4096]{1,0:T(8,128)S(1)}, u32[]{:S(2)}, u32[]{:S(2)}) collective-permute-start(f32[8,4096]{1,0:T(8,128)S(1)} %add.100), channel_id=1, source_target_pairs={{0,8},{1,9},{2,10},{3,11},{4,12},{5,13},{6,14},{7,15},{8,0},{9,1},... | collective-permute-start | bytes 393224 | tf_op jit(solution)/shard_map/ppermute | solution.py:755
  207.8 5.6 %collective-permute-start.44 = (f32[24,1024]{1,0:T(8,128)S(1)}, f32[24,1024]{1,0:T(8,128)S(1)}, u32[]{:S(2)}, u32[]{:S(2)}) collective-permute-start(f32[24,1024]{1,0:T(8,128)S(1)} %add.98), channel_id=1, source_target_pairs={{0,8},{1,9},{2,10},{3,11},{4,12},{5,13},{6,14},{7,15},{8,0},{9,1},... | collective-permute-start | bytes 294920 | tf_op jit(solution)/shard_map/ppermute | solution.py:755
  208.7 12.1 %collective-permute-start.49 = (f32[8,4096]{1,0:T(8,128)S(1)}, f32[8,4096]{1,0:T(8,128)S(1)}, u32[]{:S(2)}, u32[]{:S(2)}) collective-permute-start(f32[8,4096]{1,0:T(8,128)S(1)} %add.101.refs_2_), channel_id=1, source_target_pairs={{0,16},{1,17},{2,18},{3,19},{4,20},{5,21},{6,22},{7,23},{8,24},{9,... | collective-permute-start | bytes 393224 | tf_op jit(solution)/shard_map/ppermute | solution.py:755
  213.4 7.4 %collective-permute-start.45 = (f32[24,1024]{1,0:T(8,128)S(1)}, f32[24,1024]{1,0:T(8,128)S(1)}, u32[]{:S(2)}, u32[]{:S(2)}) collective-permute-start(f32[24,1024]{1,0:T(8,128)S(1)} %add.99.refs_0_), channel_id=1, source_target_pairs={{0,16},{1,17},{2,18},{3,19},{4,20},{5,21},{6,22},{7,23},{8,24},{9,... | collective-permute-start | bytes 294920 | tf_op jit(solution)/shard_map/ppermute | solution.py:755
  223.8 10.8 %all-to-all-start = ((f32[32,8,128]{2,1,0:T(8,128)}), f32[32,8,128]{2,1,0:T(8,128)S(1)}, u32[]{:S(2)}, u32[]{:S(2)}) async-start(f32[32,8,128]{2,1,0:T(8,128)} %get-tuple-element.125), calls=%async_computation | async-start | bytes 262144 | tf_op jit(solution)/shard_map/all_to_all | solution.py:1019
  (85 other events, 413.4 us)

commit v2 on v1

--- a/solution.py
+++ b/solution.py
@@ -845,8 +845,8 @@
         if k == 9:
             gate = [ups[1], downs[1]]
         if k == 4:
-            gate = [tok_own]
-        if k == 7:
+            gate = [tok_own, bias, bias_1, pos_rows, pair_rows]
+        if k == 9:
             gate = [tok_far]
         if gate:
             lefts[-1], rights[-1] = after(lefts[-1], *gate), after(rights[-1], *gate)
@@ -856,11 +856,10 @@
             ups[-1], downs[-1] = ups[-1], downs[-1]
             ups.append(send(ups[-1], around))
             downs.append(send(downs[-1], around))
-            own, given = lookup(lefts[1], rights[1], bias, bias_1, pos_rows, pair_rows)
-        if k == 2:
-            tok_own, tok_far = shared(own, given, lefts[2], rights[2], ups[1], downs[1])
-
-    behind(2, 4, lefts[5])
+            own, given = lookup(left)
+        if k == 1:
+            tok_own, tok_far = shared(own, given, lefts[1], rights[1], ups[1], downs[1])
+
     parts = [tok_own, tok_far] if m > 2 else [tok_own]
     both = tok_own + tok_far if m > 2 else tok_own
     toks = [parts, [across(both, 1)]]
@@ -903,7 +902,6 @@
         wide_head = last[:, 0].reshape(1, width)
         count_row = jnp.broadcast_to(jnp.sum(last[:, 1, 0]), (1, 128))
     count = count_row[0, 0]
-    behind(4, 5, *mats)
     f_sib = across(f_other, 1)
     mats += [across(x, 1) for x in mats]
 
@@ -920,7 +918,11 @@
         xl.append(x)
         hl.append(h)
 
-    behind(5, 7, *hl, wide_d)
+    behind(2, 3, lefts[5])
+    behind(3, 4, *mats[:2])
+    behind(4, 5, *mats[2:4], hl[0])
+    behind(5, 6, hl[1], wide_d)
+    behind(6, 7)
     kv, ukv_t, o, x1, q, p_t, u, w_out, e1 = call(
         functools.partial(rows_kernel, micro, rank),
         [shaped((micro, tokens, 2 * width), BF16), shaped((micro, 5 * rank, tokens), BF16),
@@ -1000,12 +1002,12 @@
         vmem=26, name="rows_back",
     )
 
-    def rep_parts(x):
-        bit, part = 1, jnp.zeros_like(x)
-        while bit < n:
+    def rep_parts(x, order):
+        part = jnp.zeros_like(x)
+        bits = [1 << k for k in range(n.bit_length() - 1)][::order]
+        for bit in bits:
             part = send(x, pairs_of(n, m, lambda r, s, bit=bit: (r ^ bit, s)))
-            bit *= 2
-            if bit < n:
+            if bit != bits[-1]:
                 x = x + part
         return Fresh(x), Fresh(part)
 
@@ -1013,7 +1015,7 @@
         functools.partial(ortho_kernel, rank),
         [Kept((2, rank, width), F32), Kept((rank, hidden), F32), Kept((1, width), F32),
          Kept((n * m, rank, 128), F32)],
-        [*rep_parts(left_d), *rep_parts(left_f), Fresh(mat_d), Fresh(mat_f)],
+        [*rep_parts(left_d, 1), *rep_parts(left_f, -1), Fresh(mat_d), Fresh(mat_f)],
         vmem=10, name="ortho",
     )
     notes = lax.all_to_all(note, AXES, 0, 0)

time: 238 us -> 230 us (0.966)
  starting transfers between devices: 43.4 us -> 37.3 us
  other arithmetic: 9.2 us -> 6.48 us
    ppermute x50, starting transfers between devices: 40.9 us -> 34.4 us  [send(): return lax.ppermute(x, AXES, perm)]
    unnamed x195 -> x185, local copies, waits for them, and re-layouts: 18.1 us -> 19.4 us
  transfers between devices with their start and end apart: 51 -> 51, of which waited for: 29 -> 26; matrix products, arithmetic and copies ran while one was open for 14% -> 13% of each run, Pallas kernels for 17% -> 19%
where the time goes in v2:
time: 230 us; the launch traced here: 229 us
  waiting for transfers between devices  80.6 us (35%)
  Pallas kernels  59.1 us (26%)
  local copies, waits for them, and re-layouts  43.9 us (19%)
  starting transfers between devices  37.3 us (16%)
  other arithmetic  6.48 us (3%)
    ppermute x50, waiting for transfers between devices, send(): return lax.ppermute(x, AXES, perm)  72.4 us
    pallas_call x20, Pallas kernels, call(): pl.pallas_call(kernel, out_shape=tuple((jax.ShapeDtypeStruct(o.shape, o.d...  59.1 us
    ppermute x50, starting transfers between devices, send(): return lax.ppermute(x, AXES, perm)  34.4 us
    unnamed x185, local copies, waits for them, and re-layouts  19.4 us
    gather x1, local copies, waits for them, and re-layouts, lookup(): jnp.take(embed_table, after(jnp.clip(near, 0, held - 1), *start), axis=0)  17.7 us
    all_to_all x1, waiting for transfers between devices, on_device(): notes = lax.all_to_all(note, AXES, 0, 0)  8.17 us
  transfers between devices with their start and end apart: 51, of which 26 were waited for; matrix products, arithmetic and copies ran while one was open for 13% of the time, Pallas kernels for 19%

profile of v2, /device:TPU:0, one launch (start us, length us, event | category | flops | bytes accessed | tf_op | source)
XLA Modules:
  0.0 229.3 jit_solution(15923648625624139037)
XLA Ops:
  2.0 2.8 %split.1 = (bf16[144,1024]{1,0:T(8,128)(2,1)}, bf16[144,1024]{1,0:T(8,128)(2,1)}, bf16[128,2048]{1,0:T(8,128)(2,1)}, bf16[256,1024]{1,0:T(8,128)(2,1)}) custom-call(f32[2,40,128]{2,1,0:T(8,128)} %bitcast.68, f32[16,512]{1,0:T(8,128)} %bitcast.73, f32[1,128]{1,0:T(1,128)} %refs_10_.1, s32[1,16]{1,0:T(1,128)} %reshape_squeeze.3.refs_3_, ...), custom_call_target="tpu_custom_call" | custom-call | tf_op jit(solution)/shard_map/split/pallas_call | solution.py:687
  4.8 3.0 %collective-permute-start = (bf16[144,1024]{1,0:T(8,128)(2,1)}, bf16[144,1024]{1,0:T(8,128)(2,1)S(1)}, u32[]{:S(2)}, u32[]{:S(2)}) collective-permute-start(bf16[144,1024]{1,0:T(8,128)(2,1)} %get-tuple-element.77.refs_1_), channel_id=1, source_target_pairs={{0,4},{1,9},{2,6},{3,11},{4,12},{5,1},{6,14},{7,3},{8,0},{9,17},{1... | collective-permute-start | bytes 884744 | tf_op jit(solution)/shard_map/ppermute | solution.py:755
  7.8 1.6 collective-permute-start.1
  9.3 1.6 collective-permute-start.2
  10.9 1.6 collective-permute-start.3
  14.5 17.7 %gather_fusion = bf16[1024,1024]{1,0:T(8,128)(2,1)} fusion(bf16[12568,1024]{1,0:T(8,128)(2,1)} %param.27, s32[1024]{0:T(1024)S(1)} %broadcast_clamp_fusion), kind=kCustom, calls=%fused_computation | custom fusion | bytes 4198400 | tf_op jit(solution)/shard_map/jit(_take)/gather | solution.py:812
  32.2 1.8 select_select_fusion
  34.0 1.2 slice_bitcast_fusion.refs_0_
  39.7 2.5 %slice.31.refs_4_.refs_3_ = bf16[512,1024]{1,0:T(8,128)(2,1)} slice(bf16[2050,1024]{1,0:T(8,128)(2,1)} %param.28), slice={[0:512], [0:1024]} | slice | bytes 2097152 | tf_op jit(solution)/shard_map/slice | solution.py:831
  42.8 2.2 collective-permute-done.7.refs_3_
  45.4 2.7 %collective-permute-done.13.refs_11_.refs_3_ = bf16[144,1024]{1,0:T(8,128)(2,1)S(1)} collective-permute-done((bf16[144,1024]{1,0:T(8,128)(2,1)}, bf16[144,1024]{1,0:T(8,128)(2,1)S(1)}, u32[]{:S(2)}, u32[]{:S(2)}) %collective-permute-start.13) | collective-permute-done | bytes 294944 | tf_op jit(solution)/shard_map/ppermute | solution.py:755
  48.6 1.1 fusion.refs_0_.refs_1_
  49.8 1.9 collective-permute-done.8.refs_0_
  52.9 1.9 collective-permute-done.14.refs_0_
  56.1 1.5 collective-permute-start.5
  57.6 1.8 collective-permute-done.9.refs_5_
  60.5 2.0 collective-permute-done.15.refs_13_.refs_5_
  63.7 2.4 %collective-permute-done.10.refs_6_.refs_1_ = bf16[144,1024]{1,0:T(8,128)(2,1)} collective-permute-done((bf16[144,1024]{1,0:T(8,128)(2,1)S(1)}, bf16[144,1024]{1,0:T(8,128)(2,1)}, u32[]{:S(2)}, u32[]{:S(2)}) %collective-permute-start.10) | collective-permute-done | bytes 294944 | tf_op jit(solution)/shard_map/ppermute | solution.py:755
  66.7 2.7 %collective-permute-done.16.refs_14_.refs_6_ = bf16[144,1024]{1,0:T(8,128)(2,1)} collective-permute-done((bf16[144,1024]{1,0:T(8,128)(2,1)S(1)}, bf16[144,1024]{1,0:T(8,128)(2,1)}, u32[]{:S(2)}, u32[]{:S(2)}) %collective-permute-start.16) | collective-permute-done | bytes 294944 | tf_op jit(solution)/shard_map/ppermute | solution.py:755
  70.8 2.4 %collective-permute-done.11.refs_7_ = bf16[144,1024]{1,0:T(8,128)(2,1)} collective-permute-done((bf16[144,1024]{1,0:T(8,128)(2,1)}, bf16[144,1024]{1,0:T(8,128)(2,1)}, u32[]{:S(2)}, u32[]{:S(2)}) %collective-permute-start.11) | collective-permute-done | bytes 294944 | tf_op jit(solution)/shard_map/ppermute | solution.py:755
  73.7 2.7 %collective-permute-done.17.refs_15_.refs_7_ = bf16[144,1024]{1,0:T(8,128)(2,1)} collective-permute-done((bf16[144,1024]{1,0:T(8,128)(2,1)}, bf16[144,1024]{1,0:T(8,128)(2,1)}, u32[]{:S(2)}, u32[]{:S(2)}) %collective-permute-start.17) | collective-permute-done | bytes 294944 | tf_op jit(solution)/shard_map/ppermute | solution.py:755
  76.9 3.2 %collective-permute-done.5.refs_1_ = bf16[512,1024]{1,0:T(8,128)(2,1)S(1)} collective-permute-done((bf16[512,1024]{1,0:T(8,128)(2,1)S(1)}, bf16[512,1024]{1,0:T(8,128)(2,1)S(1)}, u32[]{:S(2)}, u32[]{:S(2)}) %collective-permute-start.5) | collective-permute-done | bytes 1048608 | tf_op jit(solution)/shard_map/ppermute | solution.py:755
  80.1 1.4 add.91
  81.5 9.2 %collective-permute-done.12.refs_8_ = bf16[144,1024]{1,0:T(8,128)(2,1)S(1)} collective-permute-done((bf16[144,1024]{1,0:T(8,128)(2,1)}, bf16[144,1024]{1,0:T(8,128)(2,1)S(1)}, u32[]{:S(2)}, u32[]{:S(2)}) %collective-permute-start.12) | collective-permute-done | bytes 294944 | tf_op jit(solution)/shard_map/ppermute | solution.py:755
  90.7 1.9 assemble.5.refs_11_.refs_2_
  92.6 1.0 copy-done.2
  93.6 1.9 assemble.4.refs_10_.refs_1_
  95.5 1.0 copy-done.4
  97.7 1.1 copy-done.31
  98.8 1.0 copy-done.36
  99.7 1.0 copy-done.42
  100.7 2.9 %assemble.7.refs_13_.refs_2_ = bf16[1024,512]{1,0:T(8,128)(2,1)} custom-call(s32[8,2,8]{2,1,0:T(2,128)S(1)} %copy-done.62, bf16[144,1024]{1,0:T(8,128)(2,1)S(1)} %copy-done.31, bf16[144,1024]{1,0:T(8,128)(2,1)S(1)} %copy-done.11, bf16[144,1024]{1,0:T(8,128)(2,1)S(1)} %copy-done.36, bf16[144,1024]{1,0:T(8,128)(2,1)S(1)} %copy-done.13, ...), custom_call_target="tpu_custom_call" | custom-call | tf_op jit(solution)/shard_map/assemble/pallas_call | solution.py:687
  103.8 2.0 front.2
  105.8 2.9 %assemble.6.refs_12_.refs_1_ = bf16[1024,512]{1,0:T(8,128)(2,1)} custom-call(s32[8,2,8]{2,1,0:T(2,128)S(1)} %copy-done.62, bf16[144,1024]{1,0:T(8,128)(2,1)S(1)} %copy-done.32, bf16[144,1024]{1,0:T(8,128)(2,1)S(1)} %copy-done.11, bf16[144,1024]{1,0:T(8,128)(2,1)S(1)} %copy-done.37, bf16[144,1024]{1,0:T(8,128)(2,1)S(1)} %copy-done.13, ...), custom_call_target="tpu_custom_call" | custom-call | tf_op jit(solution)/shard_map/assemble/pallas_call | solution.py:687
  109.3 2.4 %collective-permute-done.26.refs_0_ = bf16[128,2048]{1,0:T(8,128)(2,1)} collective-permute-done((bf16[128,2048]{1,0:T(8,128)(2,1)}, bf16[128,2048]{1,0:T(8,128)(2,1)}, u32[]{:S(2)}, u32[]{:S(2)}) %collective-permute-start.26) | collective-permute-done | bytes 524320 | tf_op jit(solution)/shard_map/ppermute | solution.py:755
  113.2 3.1 %unpack.1 = (bf16[2,40,1024]{2,1,0:T(8,128)(2,1)S(1)}, bf16[16,2048]{1,0:T(8,128)(2,1)S(1)}, bf16[16,2048]{1,0:T(8,128)(2,1)S(1)}, f32[1,1024]{1,0:T(1,128)S(1)}, f32[1,128]{1,0:T(1,128)}) custom-call(s32[8,2,8]{2,1,0:T(2,128)S(1)} %copy-done.62, bf16[144,1024]{1,0:T(8,128)(2,1)S(1)} %copy-done.21, bf16[144,1024]{1,0:T(8,128)(2,1)S(1)} %copy-done.9, ...), custom_call_target="tpu_custom_call" | custom-call | tf_op jit(solution)/shard_map/unpack/pallas_call | solution.py:687
  118.2 2.8 %front.3 = (bf16[512,1024]{1,0:T(8,128)(2,1)S(1)}, f32[16,1024]{1,0:T(8,128)S(1)}, bf16[16,1024]{1,0:T(8,128)(2,1)S(1)}) custom-call(bf16[512,1024]{1,0:T(8,128)(2,1)} %collective-permute-done.6.refs_0_, s32[2,512]{1,0:T(2,128)S(1)} %copy-done.78, s32[2,512]{1,0:T(2,128)S(1)} %copy-done.75, bf16[512,1024]{1,0:T(8,128)(2,1)S(1)} %copy-done.1, ...), custom_call_target="tpu_custom_call" | custom-call | tf_op jit(solution)/shard_map/front/pallas_call | solution.py:687
  121.0 1.0 copy-done.27
  124.9 8.6 %collective-permute-done.34.refs_14_ = bf16[256,1024]{1,0:T(8,128)(2,1)} collective-permute-done((bf16[256,1024]{1,0:T(8,128)(2,1)}, bf16[256,1024]{1,0:T(8,128)(2,1)}, u32[]{:S(2)}, u32[]{:S(2)}) %collective-permute-start.34) | collective-permute-done | bytes 524320 | tf_op jit(solution)/shard_map/ppermute | solution.py:755
  133.9 5.2 %collective-permute-done.28.refs_7_ = bf16[128,2048]{1,0:T(8,128)(2,1)} collective-permute-done((bf16[128,2048]{1,0:T(8,128)(2,1)}, bf16[128,2048]{1,0:T(8,128)(2,1)}, u32[]{:S(2)}, u32[]{:S(2)}) %collective-permute-start.28) | collective-permute-done | bytes 524320 | tf_op jit(solution)/shard_map/ppermute | solution.py:755
  139.6 14.2 %rows.1 = (bf16[2,512,2048]{2,1,0:T(8,128)(2,1)}, bf16[2,40,512]{2,1,0:T(8,128)(2,1)}, bf16[32,1024]{1,0:T(8,128)(2,1)}, f32[32,1024]{1,0:T(8,128)}, bf16[32,102...) custom-call(s32[2,512]{1,0:T(2,128)} %refs_0_.8, ...), custom_call_target="tpu_custom_call" | custom-call | tf_op jit(solution)/shard_map/rows/pallas_call | solution.py:687
  155.9 1.4 collective-permute-start.30
  157.9 1.0 copy-done.46
  158.9 1.0 copy-done.48
  160.0 1.0 copy-done.61
  161.0 3.1 %preload.1 = (bf16[1024,2048]{1,0:T(8,128)(2,1)S(1)}, bf16[2048,1024]{1,0:T(8,128)(2,1)S(1)}) custom-call(s32[8,2,8]{2,1,0:T(2,128)S(1)} %copy-done.62, bf16[32,1024]{1,0:T(8,128)(2,1)S(1)} %copy-done.50, bf16[128,2048]{1,0:T(8,128)(2,1)S(1)} %copy-done.60, bf16[128,2048]{1,0:T(8,128)(2,1)S(1)} %copy-done.17, bf16[128,2048]{1,0:T(8,128)(2,1)} %after.19.refs_4_, ...), custom_call_target="tpu_custom_call" | custom-call | tf_op jit(solution)/shard_map/preload/pallas_call | solution.py:687
  164.1 5.6 %collective-permute-done.30.refs_6_ = bf16[128,2048]{1,0:T(8,128)(2,1)S(1)} collective-permute-done((bf16[128,2048]{1,0:T(8,128)(2,1)}, bf16[128,2048]{1,0:T(8,128)(2,1)S(1)}, u32[]{:S(2)}, u32[]{:S(2)}) %collective-permute-start.30) | collective-permute-done | bytes 524320 | tf_op jit(solution)/shard_map/ppermute | solution.py:755
  169.8 3.1 %ffn.1 = (f32[64,2048]{1,0:T(8,128)S(1)}, bf16[64,2048]{1,0:T(8,128)(2,1)S(1)}, bf16[1024,2048]{1,0:T(8,128)(2,1)S(1)}, bf16[2048,1024]{1,0:T(8,128)(2,1)S(1)}, ...) custom-call(s32[8,2,8]{2,1,0:T(2,128)S(1)} %copy-done.62, ...), custom_call_target="tpu_custom_call", output_to_operand_aliasing={{2}: (8, {}), {3}: (9, {})} | custom-call | tf_op jit(solution)/shard_map/ffn/pallas_call | solution.py:687
  173.0 1.4 collective-permute-done.37.refs_2_
  175.3 1.5 collective-permute-start.39
  177.1 2.0 collective-permute-done.39.refs_2_
  182.4 3.0 %ffn_back.1 = (f32[32,1152]{1,0:T(8,128)S(1)}, f32[32,1152]{1,0:T(8,128)S(1)}, bf16[64,2048]{1,0:T(8,128)(2,1)S(1)}) custom-call(bf16[32,1152]{1,0:T(8,128)(2,1)S(1)} %get-tuple-element.102.refs_0_, bf16[32,1152]{1,0:T(8,128)(2,1)S(1)} %collective-permute-done.41.refs_1_, f32[64,2048]{1,0:T(8,128)S(1)} %slope.1.refs_2_, bf16[16,2048]{1,0:T(8,128)(2,1)S(1)} %copy-done.65, ...), custom_call_target="tpu_custom_call" | custom-call | tf_op jit(solution)/shard_map/ffn_back/pallas_call | solution.py:687
  187.7 2.6 %collective-permute-start.47 = (f32[8,4096]{1,0:T(8,128)S(1)}, f32[8,4096]{1,0:T(8,128)S(1)}, u32[]{:S(2)}, u32[]{:S(2)}) collective-permute-start(f32[8,4096]{1,0:T(8,128)S(1)} %get-tuple-element.122), channel_id=1, source_target_pairs={{0,16},{1,17},{2,18},{3,19},{4,20},{5,21},{6,22},{7,23},{8,24},{9,... | collective-permute-start | bytes 393224 | tf_op jit(solution)/shard_map/ppermute | solution.py:755
  190.4 7.1 %rows_back.1 = (f32[2,40,1024]{2,1,0:T(8,128)S(1)}, f32[24,1024]{1,0:T(8,128)S(1)}) custom-call(f32[32,1152]{1,0:T(8,128)S(1)} %get-tuple-element.106.refs_0_, f32[32,1152]{1,0:T(8,128)S(1)} %collective-permute-done.42.refs_1_, f32[32,1024]{1,0:T(8,128)S(1)} %get-tuple-element.108.refs_2_, f32[40,1024]{1,0:T(8,128)S(1)} %get-tuple-element.109.refs_3_, ...), custom_call_target="tpu_custom_call" | custom-call | tf_op jit(solution)/shard_map/rows_back/pallas_call | solution.py:687
  198.0 1.6 collective-permute-start.48
  199.6 2.6 %collective-permute-done.43 = f32[24,1024]{1,0:T(8,128)S(1)} collective-permute-done((f32[24,1024]{1,0:T(8,128)S(1)}, f32[24,1024]{1,0:T(8,128)S(1)}, u32[]{:S(2)}, u32[]{:S(2)}) %collective-permute-start.43) | collective-permute-done | bytes 98336 | tf_op jit(solution)/shard_map/ppermute | solution.py:755
  202.3 1.5 collective-permute-start.44
  203.8 1.8 collective-permute-start.49
  205.6 1.3 collective-permute-done.44
  207.4 5.1 %collective-permute-done.45.refs_1_ = f32[24,1024]{1,0:T(8,128)S(1)} collective-permute-done((f32[24,1024]{1,0:T(8,128)S(1)}, f32[24,1024]{1,0:T(8,128)S(1)}, u32[]{:S(2)}, u32[]{:S(2)}) %collective-permute-start.45) | collective-permute-done | bytes 98336 | tf_op jit(solution)/shard_map/ppermute | solution.py:755
  212.6 3.1 %ortho.1 = (f32[2,8,1024]{2,1,0:T(8,128)S(1)}, f32[8,4096]{1,0:T(8,128)S(1)}, f32[1,1024]{1,0:T(1,128)S(1)}, f32[32,8,128]{2,1,0:T(8,128)}) custom-call(f32[24,1024]{1,0:T(8,128)S(1)} %add.99.refs_0_, f32[24,1024]{1,0:T(8,128)S(1)} %collective-permute-done.45.refs_1_, f32[8,4096]{1,0:T(8,128)S(1)} %add.101.refs_2_, ...), custom_call_target="tpu_custom_call" | custom-call | tf_op jit(solution)/shard_map/ortho/pallas_call | solution.py:687
  215.6 2.9 %all-to-all-start = ((f32[32,8,128]{2,1,0:T(8,128)}), f32[32,8,128]{2,1,0:T(8,128)S(1)}, u32[]{:S(2)}, u32[]{:S(2)}) async-start(f32[32,8,128]{2,1,0:T(8,128)} %get-tuple-element.125), calls=%async_computation | async-start | bytes 262144 | tf_op jit(solution)/shard_map/all_to_all | solution.py:1021
  218.5 8.2 %all-to-all-done.refs_0_ = f32[32,8,128]{2,1,0:T(8,128)S(1)} async-done(((f32[32,8,128]{2,1,0:T(8,128)}), f32[32,8,128]{2,1,0:T(8,128)S(1)}, u32[]{:S(2)}, u32[]{:S(2)}) %all-to-all-start) | async-done | bytes 131104 | tf_op jit(solution)/shard_map/all_to_all | solution.py:1021
  226.8 2.3 %final.1 = (f32[2,40,128]{2,1,0:T(8,128)}, f32[16,512]{1,0:T(8,128)}, f32[1,128]{1,0:T(1,128)}, f32[2,40,128]{2,1,0:T(8,128)}, f32[16,512]{1,0:T(8,128)}, /*inde...) custom-call(f32[32,8,128]{2,1,0:T(8,128)S(1)} %all-to-all-done.refs_, ...), custom_call_target="tpu_custom_call" | custom-call | tf_op jit(solution)/shard_map/final/pallas_call | solution.py:687
  (287 shorter events, 36.5 us)
Async XLA Ops:
  4.8 30.4 %collective-permute-start = (bf16[144,1024]{1,0:T(8,128)(2,1)}, bf16[144,1024]{1,0:T(8,128)(2,1)S(1)}, u32[]{:S(2)}, u32[]{:S(2)}) collective-permute-start(bf16[144,1024]{1,0:T(8,128)(2,1)} %get-tuple-element.77.refs_1_), channel_id=1, source_target_pairs={{0,4},{1,9},{2,6},{3,11},{4,12},{5,1},{6,14},{7,3},{8,0},{9,17},{1... | collective-permute-start | bytes 884744 | tf_op jit(solution)/shard_map/ppermute | solution.py:755
  7.8 27.4 %collective-permute-start.1 = (bf16[144,1024]{1,0:T(8,128)(2,1)}, bf16[144,1024]{1,0:T(8,128)(2,1)S(1)}, u32[]{:S(2)}, u32[]{:S(2)}) collective-permute-start(bf16[144,1024]{1,0:T(8,128)(2,1)} %get-tuple-element.78.refs_9_.refs_1_), channel_id=1, source_target_pairs={{0,4},{1,9},{2,6},{3,11},{4,12},{5,1},{6,14},{7,3},{8,0},{9,17},{1... | collective-permute-start | bytes 884744 | tf_op jit(solution)/shard_map/ppermute | solution.py:755
  9.3 25.9 %collective-permute-start.2 = (bf16[128,2048]{1,0:T(8,128)(2,1)}, bf16[128,2048]{1,0:T(8,128)(2,1)S(1)}, u32[]{:S(2)}, u32[]{:S(2)}) collective-permute-start(bf16[128,2048]{1,0:T(8,128)(2,1)} %get-tuple-element.79.refs_2_), channel_id=1, source_target_pairs={{0,4},{1,9},{2,6},{3,11},{4,12},{5,1},{6,14},{7,3},{8,0},{9,17},{1... | collective-permute-start | bytes 1572872 | tf_op jit(solution)/shard_map/ppermute | solution.py:755
  10.9 24.7 %collective-permute-start.3 = (bf16[256,1024]{1,0:T(8,128)(2,1)}, bf16[256,1024]{1,0:T(8,128)(2,1)S(1)}, u32[]{:S(2)}, u32[]{:S(2)}) collective-permute-start(bf16[256,1024]{1,0:T(8,128)(2,1)} %get-tuple-element.80.refs_9_), channel_id=1, source_target_pairs={{0,4},{1,9},{2,6},{3,11},{4,12},{5,1},{6,14},{7,3},{8,0},{9,17},{1... | collective-permute-start | bytes 1572872 | tf_op jit(solution)/shard_map/ppermute | solution.py:755
  37.3 11.3 %collective-permute-start.4 = (bf16[512,1024]{1,0:T(8,128)(2,1)}, bf16[512,1024]{1,0:T(8,128)(2,1)S(1)}, u32[]{:S(2)}, u32[]{:S(2)}) collective-permute-start(bf16[512,1024]{1,0:T(8,128)(2,1)} %after.15), channel_id=1, source_target_pairs={{0,1},{1,0},{2,3},{3,2},{4,5},{5,4},{6,7},{7,6},{8,9},{9,8},{10,11... | collective-permute-start | bytes 3145736 | tf_op jit(solution)/shard_map/ppermute | solution.py:755
  37.9 7.0 %collective-permute-start.7 = (bf16[144,1024]{1,0:T(8,128)(2,1)}, bf16[144,1024]{1,0:T(8,128)(2,1)S(1)}, u32[]{:S(2)}, u32[]{:S(2)}) collective-permute-start(bf16[144,1024]{1,0:T(8,128)(2,1)} %copy-done.8), channel_id=1, source_target_pairs={{0,4},{1,9},{2,6},{3,11},{4,12},{5,1},{6,14},{7,3},{8,0},{9,17},{1... | collective-permute-start | bytes 884744 | tf_op jit(solution)/shard_map/ppermute | solution.py:755
  38.5 9.6 %collective-permute-start.13 = (bf16[144,1024]{1,0:T(8,128)(2,1)}, bf16[144,1024]{1,0:T(8,128)(2,1)S(1)}, u32[]{:S(2)}, u32[]{:S(2)}) collective-permute-start(bf16[144,1024]{1,0:T(8,128)(2,1)} %copy-done.10), channel_id=1, source_target_pairs={{0,4},{1,9},{2,6},{3,11},{4,12},{5,1},{6,14},{7,3},{8,0},{9,17},{1... | collective-permute-start | bytes 884744 | tf_op jit(solution)/shard_map/ppermute | solution.py:755
  44.9 47.7 %copy-start.33 = (bf16[144,1024]{1,0:T(8,128)(2,1)}, bf16[144,1024]{1,0:T(8,128)(2,1)S(1)}, u32[]{:S(2)}) copy-start(bf16[144,1024]{1,0:T(8,128)(2,1)S(1)} %collective-permute-done.7.refs_3_) | copy-start | bytes 884740
  44.9 6.7 %collective-permute-start.8 = (bf16[144,1024]{1,0:T(8,128)(2,1)S(1)}, bf16[144,1024]{1,0:T(8,128)(2,1)S(1)}, u32[]{:S(2)}, u32[]{:S(2)}) collective-permute-start(bf16[144,1024]{1,0:T(8,128)(2,1)S(1)} %collective-permute-done.7.refs_3_), channel_id=1, source_target_pairs={{0,4},{1,9},{2,6},{3,11},{4,12},{5,1},{6,14},{7,3},{8,0},{9,17},{1... | collective-permute-start | bytes 884744 | tf_op jit(solution)/shard_map/ppermute | solution.py:755
  48.1 6.7 %collective-permute-start.14 = (bf16[144,1024]{1,0:T(8,128)(2,1)S(1)}, bf16[144,1024]{1,0:T(8,128)(2,1)S(1)}, u32[]{:S(2)}, u32[]{:S(2)}) collective-permute-start(bf16[144,1024]{1,0:T(8,128)(2,1)S(1)} %collective-permute-done.13.refs_11_.refs_3_), channel_id=1, source_target_pairs={{0,4},{1,9},{2,6},{3,11},{4,12},{5,1},{6,14},{7,3},{8,0},{9,17},{1... | collective-permute-start | bytes 884744 | tf_op jit(solution)/shard_map/ppermute | solution.py:755
  52.4 6.9 %collective-permute-start.9 = (bf16[144,1024]{1,0:T(8,128)(2,1)}, bf16[144,1024]{1,0:T(8,128)(2,1)S(1)}, u32[]{:S(2)}, u32[]{:S(2)}) collective-permute-start(bf16[144,1024]{1,0:T(8,128)(2,1)} %after.16.refs_4_), channel_id=1, source_target_pairs={{0,4},{1,9},{2,6},{3,11},{4,12},{5,1},{6,14},{7,3},{8,0},{9,17},{1... | collective-permute-start | bytes 884744 | tf_op jit(solution)/shard_map/ppermute | solution.py:755
  55.6 6.9 %collective-permute-start.15 = (bf16[144,1024]{1,0:T(8,128)(2,1)}, bf16[144,1024]{1,0:T(8,128)(2,1)S(1)}, u32[]{:S(2)}, u32[]{:S(2)}) collective-permute-start(bf16[144,1024]{1,0:T(8,128)(2,1)} %after.17.refs_12_.refs_4_), channel_id=1, source_target_pairs={{0,4},{1,9},{2,6},{3,11},{4,12},{5,1},{6,14},{7,3},{8,0},{9,17},{1... | collective-permute-start | bytes 884744 | tf_op jit(solution)/shard_map/ppermute | solution.py:755
  56.1 24.0 %collective-permute-start.5 = (bf16[512,1024]{1,0:T(8,128)(2,1)S(1)}, bf16[512,1024]{1,0:T(8,128)(2,1)S(1)}, u32[]{:S(2)}, u32[]{:S(2)}) collective-permute-start(bf16[512,1024]{1,0:T(8,128)(2,1)S(1)} %copy-done), channel_id=1, source_target_pairs={{0,2},{1,3},{2,0},{3,1},{4,6},{5,7},{6,4},{7,5},{8,10},{9,11},{10,... | collective-permute-start | bytes 3145736 | tf_op jit(solution)/shard_map/ppermute | solution.py:755
  59.3 6.8 %collective-permute-start.10 = (bf16[144,1024]{1,0:T(8,128)(2,1)S(1)}, bf16[144,1024]{1,0:T(8,128)(2,1)}, u32[]{:S(2)}, u32[]{:S(2)}) collective-permute-start(bf16[144,1024]{1,0:T(8,128)(2,1)S(1)} %collective-permute-done.9.refs_5_), channel_id=1, source_target_pairs={{0,4},{1,9},{2,6},{3,11},{4,12},{5,1},{6,14},{7,3},{8,0},{9,17},{1... | collective-permute-start | bytes 884744 | tf_op jit(solution)/shard_map/ppermute | solution.py:755
  62.5 6.8 %collective-permute-start.16 = (bf16[144,1024]{1,0:T(8,128)(2,1)S(1)}, bf16[144,1024]{1,0:T(8,128)(2,1)}, u32[]{:S(2)}, u32[]{:S(2)}) collective-permute-start(bf16[144,1024]{1,0:T(8,128)(2,1)S(1)} %collective-permute-done.15.refs_13_.refs_5_), channel_id=1, source_target_pairs={{0,4},{1,9},{2,6},{3,11},{4,12},{5,1},{6,14},{7,3},{8,0},{9,17},{1... | collective-permute-start | bytes 884744 | tf_op jit(solution)/shard_map/ppermute | solution.py:755
  66.2 7.0 %collective-permute-start.11 = (bf16[144,1024]{1,0:T(8,128)(2,1)}, bf16[144,1024]{1,0:T(8,128)(2,1)}, u32[]{:S(2)}, u32[]{:S(2)}) collective-permute-start(bf16[144,1024]{1,0:T(8,128)(2,1)} %collective-permute-done.10.refs_6_.refs_1_), channel_id=1, source_target_pairs={{0,4},{1,9},{2,6},{3,11},{4,12},{5,1},{6,14},{7,3},{8,0},{9,17},{1... | collective-permute-start | bytes 884744 | tf_op jit(solution)/shard_map/ppermute | solution.py:755
  69.3 7.0 %collective-permute-start.17 = (bf16[144,1024]{1,0:T(8,128)(2,1)}, bf16[144,1024]{1,0:T(8,128)(2,1)}, u32[]{:S(2)}, u32[]{:S(2)}) collective-permute-start(bf16[144,1024]{1,0:T(8,128)(2,1)} %collective-permute-done.16.refs_14_.refs_6_), channel_id=1, source_target_pairs={{0,4},{1,9},{2,6},{3,11},{4,12},{5,1},{6,14},{7,3},{8,0},{9,17},{1... | collective-permute-start | bytes 884744 | tf_op jit(solution)/shard_map/ppermute | solution.py:755
  69.8 20.8 %copy-start.9 = (bf16[144,1024]{1,0:T(8,128)(2,1)S(1)}, bf16[144,1024]{1,0:T(8,128)(2,1)}, u32[]{:S(2)}) copy-start(bf16[144,1024]{1,0:T(8,128)(2,1)} %copy-done.8) | copy-start | bytes 884740
  69.8 20.8 %copy-start.15 = (bf16[144,1024]{1,0:T(8,128)(2,1)S(1)}, bf16[144,1024]{1,0:T(8,128)(2,1)}, u32[]{:S(2)}) copy-start(bf16[144,1024]{1,0:T(8,128)(2,1)} %after.16.refs_4_) | copy-start | bytes 884740
  69.8 20.8 %copy-start.20 = (bf16[144,1024]{1,0:T(8,128)(2,1)S(1)}, bf16[144,1024]{1,0:T(8,128)(2,1)}, u32[]{:S(2)}) copy-start(bf16[144,1024]{1,0:T(8,128)(2,1)} %get-tuple-element.77.refs_1_) | copy-start | bytes 884740
  69.8 20.8 %copy-start.62 = (s32[8,2,8]{2,1,0:T(2,128)S(1)}, s32[8,2,8]{2,1,0:T(2,128)}, u32[]{:S(2)}) copy-start(s32[8,2,8]{2,1,0:T(2,128)} %constant.86.clone.refs_0_) | copy-start | bytes 1540
  69.9 26.7 %collective-permute-start.31 = (bf16[256,1024]{1,0:T(8,128)(2,1)}, bf16[256,1024]{1,0:T(8,128)(2,1)}, u32[]{:S(2)}, u32[]{:S(2)}) collective-permute-start(bf16[256,1024]{1,0:T(8,128)(2,1)} %after.23.refs_10_), channel_id=1, source_target_pairs={{0,4},{1,9},{2,6},{3,11},{4,12},{5,1},{6,14},{7,3},{8,0},{9,17},{1... | collective-permute-start | bytes 1572872 | tf_op jit(solution)/shard_map/ppermute | solution.py:755
  70.4 20.3 %copy-start.39 = (bf16[144,1024]{1,0:T(8,128)(2,1)S(1)}, bf16[144,1024]{1,0:T(8,128)(2,1)}, u32[]{:S(2)}) copy-start(bf16[144,1024]{1,0:T(8,128)(2,1)} %copy-done.38) | copy-start | bytes 884740
  70.4 26.8 %collective-permute-start.25 = (bf16[128,2048]{1,0:T(8,128)(2,1)}, bf16[128,2048]{1,0:T(8,128)(2,1)}, u32[]{:S(2)}, u32[]{:S(2)}) collective-permute-start(bf16[128,2048]{1,0:T(8,128)(2,1)} %after.18.refs_3_), channel_id=1, source_target_pairs={{0,4},{1,9},{2,6},{3,11},{4,12},{5,1},{6,14},{7,3},{8,0},{9,17},{1... | collective-permute-start | bytes 1572872 | tf_op jit(solution)/shard_map/ppermute | solution.py:755
  73.2 17.5 %collective-permute-start.12 = (bf16[144,1024]{1,0:T(8,128)(2,1)}, bf16[144,1024]{1,0:T(8,128)(2,1)S(1)}, u32[]{:S(2)}, u32[]{:S(2)}) collective-permute-start(bf16[144,1024]{1,0:T(8,128)(2,1)} %collective-permute-done.11.refs_7_), channel_id=1, source_target_pairs={{0,4},{1,9},{2,6},{3,11},{4,12},{5,1},{6,14},{7,3},{8,0},{9,17},{1... | collective-permute-start | bytes 884744 | tf_op jit(solution)/shard_map/ppermute | solution.py:755
  76.4 21.3 %collective-permute-start.18 = (bf16[144,1024]{1,0:T(8,128)(2,1)}, bf16[144,1024]{1,0:T(8,128)(2,1)}, u32[]{:S(2)}, u32[]{:S(2)}) collective-permute-start(bf16[144,1024]{1,0:T(8,128)(2,1)} %collective-permute-done.17.refs_15_.refs_7_), channel_id=1, source_target_pairs={{0,4},{1,9},{2,6},{3,11},{4,12},{5,1},{6,14},{7,3},{8,0},{9,17},{1... | collective-permute-start | bytes 884744 | tf_op jit(solution)/shard_map/ppermute | solution.py:755
  80.0 12.6 %copy-start.29 = (bf16[512,1024]{1,0:T(8,128)(2,1)}, bf16[512,1024]{1,0:T(8,128)(2,1)S(1)}, u32[]{:S(2)}) copy-start(bf16[512,1024]{1,0:T(8,128)(2,1)S(1)} %collective-permute-done.5.refs_1_) | copy-start | bytes 3145732
  81.5 36.2 %collective-permute-start.6 = (bf16[512,1024]{1,0:T(8,128)(2,1)}, bf16[512,1024]{1,0:T(8,128)(2,1)}, u32[]{:S(2)}, u32[]{:S(2)}) collective-permute-start(bf16[512,1024]{1,0:T(8,128)(2,1)} %add.91), channel_id=1, source_target_pairs={{0,1},{1,0},{2,3},{3,2},{4,5},{5,4},{6,7},{7,6},{8,9},{9,8},{10,11... | collective-permute-start | bytes 3145736 | tf_op jit(solution)/shard_map/ppermute | solution.py:755
  96.6 12.2 %collective-permute-start.32 = (bf16[256,1024]{1,0:T(8,128)(2,1)}, bf16[256,1024]{1,0:T(8,128)(2,1)}, u32[]{:S(2)}, u32[]{:S(2)}) collective-permute-start(bf16[256,1024]{1,0:T(8,128)(2,1)} %after.24.refs_11_), channel_id=1, source_target_pairs={{0,4},{1,9},{2,6},{3,11},{4,12},{5,1},{6,14},{7,3},{8,0},{9,17},{1... | collective-permute-start | bytes 1572872 | tf_op jit(solution)/shard_map/ppermute | solution.py:755
  97.2 14.6 %collective-permute-start.26 = (bf16[128,2048]{1,0:T(8,128)(2,1)}, bf16[128,2048]{1,0:T(8,128)(2,1)}, u32[]{:S(2)}, u32[]{:S(2)}) collective-permute-start(bf16[128,2048]{1,0:T(8,128)(2,1)} %after.19.refs_4_), channel_id=1, source_target_pairs={{0,4},{1,9},{2,6},{3,11},{4,12},{5,1},{6,14},{7,3},{8,0},{9,17},{1... | collective-permute-start | bytes 1572872 | tf_op jit(solution)/shard_map/ppermute | solution.py:755
  103.6 20.8 %collective-permute-start.22 = (bf16[1024,512]{1,0:T(8,128)(2,1)}, bf16[1024,512]{1,0:T(8,128)(2,1)}, u32[]{:S(2)}, u32[]{:S(2)}) collective-permute-start(bf16[1024,512]{1,0:T(8,128)(2,1)} %assemble.7.refs_13_.refs_2_), channel_id=1, source_target_pairs={{0,1},{1,0},{2,3},{3,2},{4,5},{5,4},{6,7},{7,6},{8,9},{9,8},{10,11... | collective-permute-start | bytes 3145736 | tf_op jit(solution)/shard_map/ppermute | solution.py:755
  108.8 14.4 %collective-permute-start.33 = (bf16[256,1024]{1,0:T(8,128)(2,1)}, bf16[256,1024]{1,0:T(8,128)(2,1)}, u32[]{:S(2)}, u32[]{:S(2)}) collective-permute-start(bf16[256,1024]{1,0:T(8,128)(2,1)} %after.25.refs_12_), channel_id=1, source_target_pairs={{0,4},{1,9},{2,6},{3,11},{4,12},{5,1},{6,14},{7,3},{8,0},{9,17},{1... | collective-permute-start | bytes 1572872 | tf_op jit(solution)/shard_map/ppermute | solution.py:755
  111.7 12.3 %collective-permute-start.27 = (bf16[128,2048]{1,0:T(8,128)(2,1)}, bf16[128,2048]{1,0:T(8,128)(2,1)}, u32[]{:S(2)}, u32[]{:S(2)}) collective-permute-start(bf16[128,2048]{1,0:T(8,128)(2,1)} %after.20.refs_5_), channel_id=1, source_target_pairs={{0,4},{1,9},{2,6},{3,11},{4,12},{5,1},{6,14},{7,3},{8,0},{9,17},{1... | collective-permute-start | bytes 1572872 | tf_op jit(solution)/shard_map/ppermute | solution.py:755
  112.2 27.3 %collective-permute-start.21 = (bf16[1024,512]{1,0:T(8,128)(2,1)}, bf16[1024,512]{1,0:T(8,128)(2,1)}, u32[]{:S(2)}, u32[]{:S(2)}) collective-permute-start(bf16[1024,512]{1,0:T(8,128)(2,1)} %assemble.6.refs_12_.refs_1_), channel_id=1, source_target_pairs={{0,1},{1,0},{2,3},{3,2},{4,5},{5,4},{6,7},{7,6},{8,9},{9,8},{10,11... | collective-permute-start | bytes 3145736 | tf_op jit(solution)/shard_map/ppermute | solution.py:755
  117.6 21.9 %collective-permute-start.20 = (bf16[1024,512]{1,0:T(8,128)(2,1)S(1)}, bf16[1024,512]{1,0:T(8,128)(2,1)}, u32[]{:S(2)}, u32[]{:S(2)}) collective-permute-start(bf16[1024,512]{1,0:T(8,128)(2,1)S(1)} %copy-done.3), channel_id=1, source_target_pairs={{0,1},{1,0},{2,3},{3,2},{4,5},{5,4},{6,7},{7,6},{8,9},{9,8},{10,11... | collective-permute-start | bytes 3145736 | tf_op jit(solution)/shard_map/ppermute | solution.py:755
  123.2 16.3 %collective-permute-start.19 = (bf16[1024,512]{1,0:T(8,128)(2,1)S(1)}, bf16[1024,512]{1,0:T(8,128)(2,1)}, u32[]{:S(2)}, u32[]{:S(2)}) collective-permute-start(bf16[1024,512]{1,0:T(8,128)(2,1)S(1)} %copy-done.5), channel_id=1, source_target_pairs={{0,1},{1,0},{2,3},{3,2},{4,5},{5,4},{6,7},{7,6},{8,9},{9,8},{10,11... | collective-permute-start | bytes 3145736 | tf_op jit(solution)/shard_map/ppermute | solution.py:755
  124.0 9.5 %collective-permute-start.34 = (bf16[256,1024]{1,0:T(8,128)(2,1)}, bf16[256,1024]{1,0:T(8,128)(2,1)}, u32[]{:S(2)}, u32[]{:S(2)}) collective-permute-start(bf16[256,1024]{1,0:T(8,128)(2,1)} %after.26.refs_13_), channel_id=1, source_target_pairs={{0,4},{1,9},{2,6},{3,11},{4,12},{5,1},{6,14},{7,3},{8,0},{9,17},{1... | collective-permute-start | bytes 1572872 | tf_op jit(solution)/shard_map/ppermute | solution.py:755
  124.4 14.7 %collective-permute-start.28 = (bf16[128,2048]{1,0:T(8,128)(2,1)}, bf16[128,2048]{1,0:T(8,128)(2,1)}, u32[]{:S(2)}, u32[]{:S(2)}) collective-permute-start(bf16[128,2048]{1,0:T(8,128)(2,1)} %after.21.refs_6_), channel_id=1, source_target_pairs={{0,4},{1,9},{2,6},{3,11},{4,12},{5,1},{6,14},{7,3},{8,0},{9,17},{1... | collective-permute-start | bytes 1572872 | tf_op jit(solution)/shard_map/ppermute | solution.py:755
  133.5 20.4 %collective-permute-start.35 = (bf16[256,1024]{1,0:T(8,128)(2,1)}, bf16[256,1024]{1,0:T(8,128)(2,1)S(1)}, u32[]{:S(2)}, u32[]{:S(2)}) collective-permute-start(bf16[256,1024]{1,0:T(8,128)(2,1)} %collective-permute-done.34.refs_14_), channel_id=1, source_target_pairs={{0,4},{1,9},{2,6},{3,11},{4,12},{5,1},{6,14},{7,3},{8,0},{9,17},{1... | collective-permute-start | bytes 1572872 | tf_op jit(solution)/shard_map/ppermute | solution.py:755
  139.1 16.0 %collective-permute-start.29 = (bf16[128,2048]{1,0:T(8,128)(2,1)}, bf16[128,2048]{1,0:T(8,128)(2,1)S(1)}, u32[]{:S(2)}, u32[]{:S(2)}) collective-permute-start(bf16[128,2048]{1,0:T(8,128)(2,1)} %collective-permute-done.28.refs_7_), channel_id=1, source_target_pairs={{0,4},{1,9},{2,6},{3,11},{4,12},{5,1},{6,14},{7,3},{8,0},{9,17},{1... | collective-permute-start | bytes 1572872 | tf_op jit(solution)/shard_map/ppermute | solution.py:755
  154.7 9.4 %collective-permute-start.36 = (bf16[256,1024]{1,0:T(8,128)(2,1)}, bf16[256,1024]{1,0:T(8,128)(2,1)S(1)}, u32[]{:S(2)}, u32[]{:S(2)}) collective-permute-start(bf16[256,1024]{1,0:T(8,128)(2,1)} %after.27.refs_15_), channel_id=1, source_target_pairs={{0,4},{1,9},{2,6},{3,11},{4,12},{5,1},{6,14},{7,3},{8,0},{9,17},{1... | collective-permute-start | bytes 1572872 | tf_op jit(solution)/shard_map/ppermute | solution.py:755
  155.9 13.8 %collective-permute-start.30 = (bf16[128,2048]{1,0:T(8,128)(2,1)}, bf16[128,2048]{1,0:T(8,128)(2,1)S(1)}, u32[]{:S(2)}, u32[]{:S(2)}) collective-permute-start(bf16[128,2048]{1,0:T(8,128)(2,1)} %after.22.refs_8_), channel_id=1, source_target_pairs={{0,4},{1,9},{2,6},{3,11},{4,12},{5,1},{6,14},{7,3},{8,0},{9,17},{1... | collective-permute-start | bytes 1572872 | tf_op jit(solution)/shard_map/ppermute | solution.py:755
  157.4 6.7 %collective-permute-start.23 = (bf16[32,1152]{1,0:T(8,128)(2,1)S(1)}, bf16[32,1152]{1,0:T(8,128)(2,1)S(1)}, u32[]{:S(2)}, u32[]{:S(2)}) collective-permute-start(bf16[32,1152]{1,0:T(8,128)(2,1)S(1)} %copy-done.52), channel_id=1, source_target_pairs={{0,1},{1,0},{2,3},{3,2},{4,5},{5,4},{6,7},{7,6},{8,9},{9,8},{10,11... | collective-permute-start | bytes 221192 | tf_op jit(solution)/shard_map/ppermute | solution.py:755
  157.4 6.7 %collective-permute-start.24 = (bf16[16,2048]{1,0:T(8,128)(2,1)S(1)}, bf16[16,2048]{1,0:T(8,128)(2,1)S(1)}, u32[]{:S(2)}, u32[]{:S(2)}) collective-permute-start(bf16[16,2048]{1,0:T(8,128)(2,1)S(1)} %copy-done.86), channel_id=1, source_target_pairs={{0,1},{1,0},{2,3},{3,2},{4,5},{5,4},{6,7},{7,6},{8,9},{9,8},{10,11... | collective-permute-start | bytes 196616 | tf_op jit(solution)/shard_map/ppermute | solution.py:755
  172.9 1.4 collective-permute-start.37
  175.1 1.9 collective-permute-start.38
  175.3 3.8 %collective-permute-start.39 = (f32[32,128]{1,0:T(8,128)S(1)}, f32[32,128]{1,0:T(8,128)S(1)}, u32[]{:S(2)}, u32[]{:S(2)}) collective-permute-start(f32[32,128]{1,0:T(8,128)S(1)} %get-tuple-element.98.refs_0_.refs_1_), channel_id=1, source_target_pairs={{0,2},{1,3},{2,0},{3,1},{4,6},{5,7},{6,4},{7,5},{8,10},{9,11},{10,... | collective-permute-start | bytes 49160 | tf_op jit(solution)/shard_map/ppermute | solution.py:755
  176.9 3.2 %collective-permute-start.40 = (f32[32,128]{1,0:T(8,128)S(1)}, f32[32,128]{1,0:T(8,128)S(1)}, u32[]{:S(2)}, u32[]{:S(2)}) collective-permute-start(f32[32,128]{1,0:T(8,128)S(1)} %get-tuple-element.98.refs_0_.refs_1_), channel_id=1, source_target_pairs={{0,3},{1,2},{2,1},{3,0},{4,7},{5,6},{6,5},{7,4},{8,11},{9,10},{10,... | collective-permute-start | bytes 49160 | tf_op jit(solution)/shard_map/ppermute | solution.py:755
  180.9 1.3 collective-permute-start.41
  185.8 1.4 collective-permute-start.46
  186.0 4.3 %collective-permute-start.42 = (f32[32,1152]{1,0:T(8,128)S(1)}, f32[32,1152]{1,0:T(8,128)S(1)}, u32[]{:S(2)}, u32[]{:S(2)}) collective-permute-start(f32[32,1152]{1,0:T(8,128)S(1)} %get-tuple-element.107), channel_id=1, source_target_pairs={{0,1},{1,0},{2,3},{3,2},{4,5},{5,4},{6,7},{7,6},{8,9},{9,8},{10,11... | collective-permute-start | bytes 442376 | tf_op jit(solution)/shard_map/ppermute | solution.py:755
  187.7 10.3 %collective-permute-start.47 = (f32[8,4096]{1,0:T(8,128)S(1)}, f32[8,4096]{1,0:T(8,128)S(1)}, u32[]{:S(2)}, u32[]{:S(2)}) collective-permute-start(f32[8,4096]{1,0:T(8,128)S(1)} %get-tuple-element.122), channel_id=1, source_target_pairs={{0,16},{1,17},{2,18},{3,19},{4,20},{5,21},{6,22},{7,23},{8,24},{9,... | collective-permute-start | bytes 393224 | tf_op jit(solution)/shard_map/ppermute | solution.py:755
  197.5 29.2 %copy-start.67 = (f32[1,128,2,40]{1,3,2,0:T(8,128)S(1)}, f32[1,128,2,40]{1,3,2,0:T(8,128)}, u32[]{:S(2)}) copy-start(f32[1,128,2,40]{1,3,2,0:T(8,128)} %param.35) | copy-start | bytes 122884
  197.5 29.2 %copy-start.69 = (f32[1,512,16]{1,2,0:T(8,128)S(1)}, f32[1,512,16]{1,2,0:T(8,128)}, u32[]{:S(2)}) copy-start(f32[1,512,16]{1,2,0:T(8,128)} %param.36) | copy-start | bytes 98308
  197.5 29.2 %copy-start.74 = (f32[1,128,2,40]{1,3,2,0:T(8,128)S(1)}, f32[1,128,2,40]{1,3,2,0:T(8,128)}, u32[]{:S(2)}) copy-start(f32[1,128,2,40]{1,3,2,0:T(8,128)} %param.38) | copy-start | bytes 122884
  197.5 29.2 %copy-start.76 = (f32[1,512,16]{1,2,0:T(8,128)S(1)}, f32[1,512,16]{1,2,0:T(8,128)}, u32[]{:S(2)}) copy-start(f32[1,512,16]{1,2,0:T(8,128)} %param.39) | copy-start | bytes 98308
  197.5 29.2 %copy-start.82 = (f32[1,128]{1,0:T(1,128)S(1)}, f32[1,128]{1,0:T(1,128)}, u32[]{:S(2)}) copy-start(f32[1,128]{1,0:T(1,128)} %refs_10_.1) | copy-start | bytes 1540
  197.5 29.2 %copy-start.83 = (f32[1,128]{1,0:T(1,128)S(1)}, f32[1,128]{1,0:T(1,128)}, u32[]{:S(2)}) copy-start(f32[1,128]{1,0:T(1,128)} %refs_13_.1) | copy-start | bytes 1540
  197.6 4.7 %collective-permute-start.43 = (f32[24,1024]{1,0:T(8,128)S(1)}, f32[24,1024]{1,0:T(8,128)S(1)}, u32[]{:S(2)}, u32[]{:S(2)}) collective-permute-start(f32[24,1024]{1,0:T(8,128)S(1)} %get-tuple-element.117), channel_id=1, source_target_pairs={{0,4},{1,5},{2,6},{3,7},{4,0},{5,1},{6,2},{7,3},{8,12},{9,13},{10,... | collective-permute-start | bytes 294920 | tf_op jit(solution)/shard_map/ppermute | solution.py:755
  198.0 5.8 %collective-permute-start.48 = (f32[8,4096]{1,0:T(8,128)S(1)}, f32[8,4096]{1,0:T(8,128)S(1)}, u32[]{:S(2)}, u32[]{:S(2)}) collective-permute-start(f32[8,4096]{1,0:T(8,128)S(1)} %add.100), channel_id=1, source_target_pairs={{0,8},{1,9},{2,10},{3,11},{4,12},{5,13},{6,14},{7,15},{8,0},{9,1},... | collective-permute-start | bytes 393224 | tf_op jit(solution)/shard_map/ppermute | solution.py:755
  202.3 4.7 %collective-permute-start.44 = (f32[24,1024]{1,0:T(8,128)S(1)}, f32[24,1024]{1,0:T(8,128)S(1)}, u32[]{:S(2)}, u32[]{:S(2)}) collective-permute-start(f32[24,1024]{1,0:T(8,128)S(1)} %add.98), channel_id=1, source_target_pairs={{0,8},{1,9},{2,10},{3,11},{4,12},{5,13},{6,14},{7,15},{8,0},{9,1},... | collective-permute-start | bytes 294920 | tf_op jit(solution)/shard_map/ppermute | solution.py:755
  203.8 8.8 %collective-permute-start.49 = (f32[8,4096]{1,0:T(8,128)S(1)}, f32[8,4096]{1,0:T(8,128)S(1)}, u32[]{:S(2)}, u32[]{:S(2)}) collective-permute-start(f32[8,4096]{1,0:T(8,128)S(1)} %add.101.refs_2_), channel_id=1, source_target_pairs={{0,4},{1,5},{2,6},{3,7},{4,0},{5,1},{6,2},{7,3},{8,12},{9,13},{10,... | collective-permute-start | bytes 393224 | tf_op jit(solution)/shard_map/ppermute | solution.py:755
  207.0 5.6 %collective-permute-start.45 = (f32[24,1024]{1,0:T(8,128)S(1)}, f32[24,1024]{1,0:T(8,128)S(1)}, u32[]{:S(2)}, u32[]{:S(2)}) collective-permute-start(f32[24,1024]{1,0:T(8,128)S(1)} %add.99.refs_0_), channel_id=1, source_target_pairs={{0,16},{1,17},{2,18},{3,19},{4,20},{5,21},{6,22},{7,23},{8,24},{9,... | collective-permute-start | bytes 294920 | tf_op jit(solution)/shard_map/ppermute | solution.py:755
  215.6 11.1 %all-to-all-start = ((f32[32,8,128]{2,1,0:T(8,128)}), f32[32,8,128]{2,1,0:T(8,128)S(1)}, u32[]{:S(2)}, u32[]{:S(2)}) async-start(f32[32,8,128]{2,1,0:T(8,128)} %get-tuple-element.125), calls=%async_computation | async-start | bytes 262144 | tf_op jit(solution)/shard_map/all_to_all | solution.py:1021
  (80 other events, 328.7 us)

commit v3 on v2

--- a/solution.py
+++ b/solution.py
@@ -909,10 +909,10 @@
     for b in range(micro):
         a, x, h = call(
             functools.partial(front_kernel, b),
-            [Kept((tokens, width), BF16), Kept((slots, width), F32), Kept((slots, width), BF16)],
+            [shaped((tokens, width), BF16), shaped((slots, width), F32), shaped((slots, width), BF16)],
             [*toks[b], positions, segment_ids, pos_rows, base_gains, bias],
             [pltpu.VMEM((tokens, width), BF16), pltpu.VMEM((tokens, width), BF16)],
-            groups=len(toks[b]), vmem=14, name="front",
+            groups=len(toks[b]), vmem=56, name="front",
         )
         h1.append(a)
         xl.append(x)

time: 230 us -> 228 us (level)
  local copies, waits for them, and re-layouts: 43.9 us -> 37.1 us
  Pallas kernels: 59.1 us -> 62.3 us
    unnamed x185 -> x149, local copies, waits for them, and re-layouts: 19.4 us -> 13.6 us
    pallas_call x20, Pallas kernels: 59.1 us -> 62.3 us  [call(): pl.pallas_call(kernel, out_shape=tuple((jax.ShapeDtypeStruct(o.shape, o.d...]
  transfers between devices with their start and end apart: 51 -> 51, of which waited for: 26 -> 27; matrix products, arithmetic and copies ran while one was open for 13% -> 13% of each run, Pallas kernels for 19% -> 20%
where the time goes in v3:
time: 228 us; the launch traced here: 227 us
  waiting for transfers between devices  82 us (36%)
  Pallas kernels  62.3 us (27%)
  starting transfers between devices  37.5 us (16%)
  local copies, waits for them, and re-layouts  37.1 us (16%)
  other arithmetic  6.72 us (3%)
    ppermute x50, waiting for transfers between devices, send(): return lax.ppermute(x, AXES, perm)  73.8 us
    pallas_call x20, Pallas kernels, call(): pl.pallas_call(kernel, out_shape=tuple((jax.ShapeDtypeStruct(o.shape, o.d...  62.3 us
    ppermute x50, starting transfers between devices, send(): return lax.ppermute(x, AXES, perm)  34.5 us
    gather x1, local copies, waits for them, and re-layouts, lookup(): jnp.take(embed_table, after(jnp.clip(near, 0, held - 1), *start), axis=0)  16.6 us
    unnamed x149, local copies, waits for them, and re-layouts  13.6 us
    all_to_all x1, waiting for transfers between devices, on_device(): notes = lax.all_to_all(note, AXES, 0, 0)  8.17 us
  transfers between devices with their start and end apart: 51, of which 27 were waited for; matrix products, arithmetic and copies ran while one was open for 13% of the time, Pallas kernels for 20%

profile of v3, /device:TPU:0, one launch (start us, length us, event | category | flops | bytes accessed | tf_op | source)
XLA Modules:
  0.0 227.4 jit_solution(5349225443933496132)
XLA Ops:
  2.0 2.8 %split.1 = (bf16[144,1024]{1,0:T(8,128)(2,1)}, bf16[144,1024]{1,0:T(8,128)(2,1)}, bf16[128,2048]{1,0:T(8,128)(2,1)}, bf16[256,1024]{1,0:T(8,128)(2,1)}) custom-call(f32[2,40,128]{2,1,0:T(8,128)} %bitcast.68, f32[16,512]{1,0:T(8,128)} %bitcast.73, f32[1,128]{1,0:T(1,128)} %refs_10_.1, s32[1,16]{1,0:T(1,128)} %reshape_squeeze.3.refs_3_, ...), custom_call_target="tpu_custom_call" | custom-call | tf_op jit(solution)/shard_map/split/pallas_call | solution.py:687
  4.7 3.0 %collective-permute-start = (bf16[144,1024]{1,0:T(8,128)(2,1)}, bf16[144,1024]{1,0:T(8,128)(2,1)S(1)}, u32[]{:S(2)}, u32[]{:S(2)}) collective-permute-start(bf16[144,1024]{1,0:T(8,128)(2,1)} %get-tuple-element.77.refs_1_), channel_id=1, source_target_pairs={{0,4},{1,9},{2,6},{3,11},{4,12},{5,1},{6,14},{7,3},{8,0},{9,17},{1... | collective-permute-start | bytes 884744 | tf_op jit(solution)/shard_map/ppermute | solution.py:755
  7.8 1.6 collective-permute-start.1
  9.3 1.6 collective-permute-start.2
  10.9 1.6 collective-permute-start.3
  14.5 16.6 %gather_fusion = bf16[1024,1024]{1,0:T(8,128)(2,1)S(1)} fusion(bf16[12568,1024]{1,0:T(8,128)(2,1)} %param.27, s32[1024]{0:T(1024)S(1)} %broadcast_clamp_fusion), kind=kCustom, calls=%fused_computation | custom fusion | bytes 4198400 | tf_op jit(solution)/shard_map/jit(_take)/gather | solution.py:812
  31.7 1.2 slice_bitcast_fusion.refs_0_
  36.4 2.4 %slice.31.refs_4_.refs_3_ = bf16[512,1024]{1,0:T(8,128)(2,1)} slice(bf16[2050,1024]{1,0:T(8,128)(2,1)} %param.28), slice={[0:512], [0:1024]} | slice | bytes 2097152 | tf_op jit(solution)/shard_map/slice | solution.py:831
  39.4 2.2 collective-permute-done.7.refs_3_
  42.2 2.7 %collective-permute-done.13.refs_11_.refs_3_ = bf16[144,1024]{1,0:T(8,128)(2,1)S(1)} collective-permute-done((bf16[144,1024]{1,0:T(8,128)(2,1)}, bf16[144,1024]{1,0:T(8,128)(2,1)S(1)}, u32[]{:S(2)}, u32[]{:S(2)}) %collective-permute-start.13) | collective-permute-done | bytes 294944 | tf_op jit(solution)/shard_map/ppermute | solution.py:755
  45.4 1.2 fusion.refs_0_.refs_1_
  46.5 1.9 collective-permute-done.8.refs_0_
  49.6 1.9 collective-permute-done.14.refs_0_
  52.8 1.5 collective-permute-start.5
  54.3 1.8 collective-permute-done.9.refs_5_
  56.6 2.7 %collective-permute-done.15.refs_13_.refs_5_ = bf16[144,1024]{1,0:T(8,128)(2,1)S(1)} collective-permute-done((bf16[144,1024]{1,0:T(8,128)(2,1)}, bf16[144,1024]{1,0:T(8,128)(2,1)S(1)}, u32[]{:S(2)}, u32[]{:S(2)}) %collective-permute-start.15) | collective-permute-done | bytes 294944 | tf_op jit(solution)/shard_map/ppermute | solution.py:755
  59.7 3.2 %collective-permute-done.10.refs_6_.refs_1_ = bf16[144,1024]{1,0:T(8,128)(2,1)} collective-permute-done((bf16[144,1024]{1,0:T(8,128)(2,1)S(1)}, bf16[144,1024]{1,0:T(8,128)(2,1)}, u32[]{:S(2)}, u32[]{:S(2)}) %collective-permute-start.10) | collective-permute-done | bytes 294944 | tf_op jit(solution)/shard_map/ppermute | solution.py:755
  63.4 2.5 %collective-permute-done.16.refs_14_.refs_6_ = bf16[144,1024]{1,0:T(8,128)(2,1)S(1)} collective-permute-done((bf16[144,1024]{1,0:T(8,128)(2,1)S(1)}, bf16[144,1024]{1,0:T(8,128)(2,1)S(1)}, u32[]{:S(2)}, u32[]{:S(2)}) %collective-permute-start.16) | collective-permute-done | bytes 294944 | tf_op jit(solution)/shard_map/ppermute | solution.py:755
  67.4 2.4 %collective-permute-done.11.refs_7_ = bf16[144,1024]{1,0:T(8,128)(2,1)S(1)} collective-permute-done((bf16[144,1024]{1,0:T(8,128)(2,1)}, bf16[144,1024]{1,0:T(8,128)(2,1)S(1)}, u32[]{:S(2)}, u32[]{:S(2)}) %collective-permute-start.11) | collective-permute-done | bytes 294944 | tf_op jit(solution)/shard_map/ppermute | solution.py:755
  70.3 2.8 %collective-permute-done.17.refs_15_.refs_7_ = bf16[144,1024]{1,0:T(8,128)(2,1)} collective-permute-done((bf16[144,1024]{1,0:T(8,128)(2,1)S(1)}, bf16[144,1024]{1,0:T(8,128)(2,1)}, u32[]{:S(2)}, u32[]{:S(2)}) %collective-permute-start.17) | collective-permute-done | bytes 294944 | tf_op jit(solution)/shard_map/ppermute | solution.py:755
  73.6 3.5 %collective-permute-done.5.refs_1_ = bf16[512,1024]{1,0:T(8,128)(2,1)} collective-permute-done((bf16[512,1024]{1,0:T(8,128)(2,1)}, bf16[512,1024]{1,0:T(8,128)(2,1)}, u32[]{:S(2)}, u32[]{:S(2)}) %collective-permute-start.5) | collective-permute-done | bytes 1048608 | tf_op jit(solution)/shard_map/ppermute | solution.py:755
  77.1 2.9 %add.91 = bf16[512,1024]{1,0:T(8,128)(2,1)} add(bf16[512,1024]{1,0:T(8,128)(2,1)} %fusion.refs_0_.refs_1_, bf16[512,1024]{1,0:T(8,128)(2,1)} %collective-permute-done.5.refs_1_) | non-fusion elementwise | flops 524288 | bytes 3145728 | tf_op jit(solution)/shard_map/add | solution.py:864
  80.0 7.4 %collective-permute-done.12.refs_8_ = bf16[144,1024]{1,0:T(8,128)(2,1)S(1)} collective-permute-done((bf16[144,1024]{1,0:T(8,128)(2,1)S(1)}, bf16[144,1024]{1,0:T(8,128)(2,1)S(1)}, u32[]{:S(2)}, u32[]{:S(2)}) %collective-permute-start.12) | collective-permute-done | bytes 294944 | tf_op jit(solution)/shard_map/ppermute | solution.py:755
  87.4 1.9 assemble.5.refs_11_.refs_2_
  89.3 1.0 copy-done
  90.3 1.8 assemble.4.refs_10_.refs_1_
  92.2 0.9 copy-done.2
  95.1 1.0 copy-done.27
  96.1 1.0 copy-done.30
  97.0 1.9 assemble.7.refs_13_.refs_2_
  99.1 5.0 %front.2 = (bf16[512,1024]{1,0:T(8,128)(2,1)}, f32[16,1024]{1,0:T(8,128)}, bf16[16,1024]{1,0:T(8,128)(2,1)}) custom-call(bf16[512,1024]{1,0:T(8,128)(2,1)} %fusion.refs_0_.refs_1_, bf16[512,1024]{1,0:T(8,128)(2,1)} %collective-permute-done.5.refs_1_, s32[2,512]{1,0:T(2,128)} %refs_1_.1, s32[2,512]{1,0:T(2,128)} %refs_0_.8, ...), custom_call_target="tpu_custom_call" | custom-call | tf_op jit(solution)/shard_map/front/pallas_call | solution.py:687
  104.1 2.8 %assemble.6.refs_12_.refs_1_ = bf16[1024,512]{1,0:T(8,128)(2,1)} custom-call(s32[8,2,8]{2,1,0:T(2,128)S(1)} %copy-done.50, bf16[144,1024]{1,0:T(8,128)(2,1)S(1)} %copy-done.20, bf16[144,1024]{1,0:T(8,128)(2,1)S(1)} %copy-done.10, bf16[144,1024]{1,0:T(8,128)(2,1)S(1)} %collective-permute-done.13.refs_11_.refs_3_, bf16[144,1024]{1,0:T(8,128)(2,1)S(1)} %copy-done.12, ...), custom_call_target="tpu_custom_call" | custom-call | tf_op jit(solution)/shard_map/assemble/pallas_call | solution.py:687
  107.5 1.6 collective-permute-done.26.refs_0_
  109.6 1.0 copy-done.25
  110.6 3.1 %unpack.1 = (bf16[2,40,1024]{2,1,0:T(8,128)(2,1)S(1)}, bf16[16,2048]{1,0:T(8,128)(2,1)S(1)}, bf16[16,2048]{1,0:T(8,128)(2,1)S(1)}, f32[1,1024]{1,0:T(1,128)S(1)}, f32[1,128]{1,0:T(1,128)}) custom-call(s32[8,2,8]{2,1,0:T(2,128)S(1)} %copy-done.50, bf16[144,1024]{1,0:T(8,128)(2,1)S(1)} %copy-done.15, bf16[144,1024]{1,0:T(8,128)(2,1)S(1)} %copy-done.8, ...), custom_call_target="tpu_custom_call" | custom-call | tf_op jit(solution)/shard_map/unpack/pallas_call | solution.py:687
  115.6 4.1 %front.3 = (bf16[512,1024]{1,0:T(8,128)(2,1)}, f32[16,1024]{1,0:T(8,128)}, bf16[16,1024]{1,0:T(8,128)(2,1)}) custom-call(bf16[512,1024]{1,0:T(8,128)(2,1)} %collective-permute-done.6.refs_0_, s32[2,512]{1,0:T(2,128)} %refs_1_.1, s32[2,512]{1,0:T(2,128)} %refs_0_.8, bf16[512,1024]{1,0:T(8,128)(2,1)} %slice.31.refs_4_.refs_3_, f32[3,1024]{1,0:T(4,128)} %refs_18_.1, ...), custom_call_target="tpu_custom_call" | custom-call | tf_op jit(solution)/shard_map/front/pallas_call | solution.py:687
  119.9 2.2 collective-permute-done.27.refs_0_
  123.1 8.5 %collective-permute-done.34.refs_14_ = bf16[256,1024]{1,0:T(8,128)(2,1)} collective-permute-done((bf16[256,1024]{1,0:T(8,128)(2,1)}, bf16[256,1024]{1,0:T(8,128)(2,1)}, u32[]{:S(2)}, u32[]{:S(2)}) %collective-permute-start.34) | collective-permute-done | bytes 524320 | tf_op jit(solution)/shard_map/ppermute | solution.py:755
  132.1 5.1 %collective-permute-done.28.refs_7_ = bf16[128,2048]{1,0:T(8,128)(2,1)} collective-permute-done((bf16[128,2048]{1,0:T(8,128)(2,1)}, bf16[128,2048]{1,0:T(8,128)(2,1)}, u32[]{:S(2)}, u32[]{:S(2)}) %collective-permute-start.28) | collective-permute-done | bytes 524320 | tf_op jit(solution)/shard_map/ppermute | solution.py:755
  137.7 14.2 %rows.1 = (bf16[2,512,2048]{2,1,0:T(8,128)(2,1)}, bf16[2,40,512]{2,1,0:T(8,128)(2,1)}, bf16[32,1024]{1,0:T(8,128)(2,1)}, f32[32,1024]{1,0:T(8,128)}, bf16[32,102...) custom-call(s32[2,512]{1,0:T(2,128)} %refs_0_.8, ...), custom_call_target="tpu_custom_call" | custom-call | tf_op jit(solution)/shard_map/rows/pallas_call | solution.py:687
  154.1 1.3 collective-permute-start.30
  156.0 1.0 copy-done.35
  157.0 1.0 copy-done.37
  158.0 3.2 %preload.1 = (bf16[1024,2048]{1,0:T(8,128)(2,1)S(1)}, bf16[2048,1024]{1,0:T(8,128)(2,1)S(1)}) custom-call(s32[8,2,8]{2,1,0:T(2,128)S(1)} %copy-done.50, bf16[32,1024]{1,0:T(8,128)(2,1)S(1)} %copy-done.41, bf16[128,2048]{1,0:T(8,128)(2,1)S(1)} %copy-done.48, bf16[128,2048]{1,0:T(8,128)(2,1)} %after.18.refs_3_, bf16[128,2048]{1,0:T(8,128)(2,1)} %after.19.refs_4_, ...), custom_call_target="tpu_custom_call" | custom-call | tf_op jit(solution)/shard_map/preload/pallas_call | solution.py:687
  161.3 1.0 collective-permute-done.36.refs_7_
  162.2 5.6 %collective-permute-done.30.refs_6_ = bf16[128,2048]{1,0:T(8,128)(2,1)S(1)} collective-permute-done((bf16[128,2048]{1,0:T(8,128)(2,1)}, bf16[128,2048]{1,0:T(8,128)(2,1)S(1)}, u32[]{:S(2)}, u32[]{:S(2)}) %collective-permute-start.30) | collective-permute-done | bytes 524320 | tf_op jit(solution)/shard_map/ppermute | solution.py:755
  167.9 3.1 %ffn.1 = (f32[64,2048]{1,0:T(8,128)S(1)}, bf16[64,2048]{1,0:T(8,128)(2,1)S(1)}, bf16[1024,2048]{1,0:T(8,128)(2,1)S(1)}, bf16[2048,1024]{1,0:T(8,128)(2,1)S(1)}, ...) custom-call(s32[8,2,8]{2,1,0:T(2,128)S(1)} %copy-done.50, ...), custom_call_target="tpu_custom_call", output_to_operand_aliasing={{2}: (8, {}), {3}: (9, {})} | custom-call | tf_op jit(solution)/shard_map/ffn/pallas_call | solution.py:687
  171.1 1.4 collective-permute-done.37.refs_2_
  173.5 1.5 collective-permute-start.39
  175.2 2.0 collective-permute-done.39.refs_2_
  177.2 0.9 collective-permute-done.40.refs_3_
  180.5 3.0 %ffn_back.1 = (f32[32,1152]{1,0:T(8,128)S(1)}, f32[32,1152]{1,0:T(8,128)S(1)}, bf16[64,2048]{1,0:T(8,128)(2,1)S(1)}) custom-call(bf16[32,1152]{1,0:T(8,128)(2,1)S(1)} %get-tuple-element.102.refs_0_, bf16[32,1152]{1,0:T(8,128)(2,1)S(1)} %collective-permute-done.41.refs_1_, f32[64,2048]{1,0:T(8,128)S(1)} %slope.1.refs_2_, ...), custom_call_target="tpu_custom_call" | custom-call | tf_op jit(solution)/shard_map/ffn_back/pallas_call | solution.py:687
  185.8 2.4 %collective-permute-start.47 = (f32[8,4096]{1,0:T(8,128)S(1)}, f32[8,4096]{1,0:T(8,128)S(1)}, u32[]{:S(2)}, u32[]{:S(2)}) collective-permute-start(f32[8,4096]{1,0:T(8,128)S(1)} %get-tuple-element.122), channel_id=1, source_target_pairs={{0,16},{1,17},{2,18},{3,19},{4,20},{5,21},{6,22},{7,23},{8,24},{9,... | collective-permute-start | bytes 393224 | tf_op jit(solution)/shard_map/ppermute | solution.py:755
  188.4 7.1 %rows_back.1 = (f32[2,40,1024]{2,1,0:T(8,128)S(1)}, f32[24,1024]{1,0:T(8,128)S(1)}) custom-call(f32[32,1152]{1,0:T(8,128)S(1)} %get-tuple-element.106.refs_0_, f32[32,1152]{1,0:T(8,128)S(1)} %collective-permute-done.42.refs_1_, f32[32,1024]{1,0:T(8,128)S(1)} %get-tuple-element.108.refs_2_, f32[40,1024]{1,0:T(8,128)S(1)} %get-tuple-element.109.refs_3_, ...), custom_call_target="tpu_custom_call" | custom-call | tf_op jit(solution)/shard_map/rows_back/pallas_call | solution.py:687
  196.0 1.7 collective-permute-start.48
  197.7 2.6 %collective-permute-done.43 = f32[24,1024]{1,0:T(8,128)S(1)} collective-permute-done((f32[24,1024]{1,0:T(8,128)S(1)}, f32[24,1024]{1,0:T(8,128)S(1)}, u32[]{:S(2)}, u32[]{:S(2)}) %collective-permute-start.43) | collective-permute-done | bytes 98336 | tf_op jit(solution)/shard_map/ppermute | solution.py:755
  200.2 1.6 collective-permute-start.44
  201.9 1.7 collective-permute-start.49
  203.5 1.4 collective-permute-done.44
  205.6 5.0 %collective-permute-done.45.refs_1_ = f32[24,1024]{1,0:T(8,128)S(1)} collective-permute-done((f32[24,1024]{1,0:T(8,128)S(1)}, f32[24,1024]{1,0:T(8,128)S(1)}, u32[]{:S(2)}, u32[]{:S(2)}) %collective-permute-start.45) | collective-permute-done | bytes 98336 | tf_op jit(solution)/shard_map/ppermute | solution.py:755
  210.5 3.1 %ortho.1 = (f32[2,8,1024]{2,1,0:T(8,128)S(1)}, f32[8,4096]{1,0:T(8,128)S(1)}, f32[1,1024]{1,0:T(1,128)S(1)}, f32[32,8,128]{2,1,0:T(8,128)}) custom-call(f32[24,1024]{1,0:T(8,128)S(1)} %add.99.refs_0_, f32[24,1024]{1,0:T(8,128)S(1)} %collective-permute-done.45.refs_1_, f32[8,4096]{1,0:T(8,128)S(1)} %add.101.refs_2_, ...), custom_call_target="tpu_custom_call" | custom-call | tf_op jit(solution)/shard_map/ortho/pallas_call | solution.py:687
  213.6 3.0 %all-to-all-start = ((f32[32,8,128]{2,1,0:T(8,128)}), f32[32,8,128]{2,1,0:T(8,128)S(1)}, u32[]{:S(2)}, u32[]{:S(2)}) async-start(f32[32,8,128]{2,1,0:T(8,128)} %get-tuple-element.125), calls=%async_computation | async-start | bytes 262144 | tf_op jit(solution)/shard_map/all_to_all | solution.py:1021
  216.7 8.2 %all-to-all-done.refs_0_ = f32[32,8,128]{2,1,0:T(8,128)S(1)} async-done(((f32[32,8,128]{2,1,0:T(8,128)}), f32[32,8,128]{2,1,0:T(8,128)S(1)}, u32[]{:S(2)}, u32[]{:S(2)}) %all-to-all-start) | async-done | bytes 131104 | tf_op jit(solution)/shard_map/all_to_all | solution.py:1021
  224.9 2.3 %final.1 = (f32[2,40,128]{2,1,0:T(8,128)}, f32[16,512]{1,0:T(8,128)}, f32[1,128]{1,0:T(1,128)}, f32[2,40,128]{2,1,0:T(8,128)}, f32[16,512]{1,0:T(8,128)}, /*inde...) custom-call(f32[32,8,128]{2,1,0:T(8,128)S(1)} %all-to-all-done.refs_, ...), custom_call_target="tpu_custom_call" | custom-call | tf_op jit(solution)/shard_map/final/pallas_call | solution.py:687
  (251 shorter events, 32.3 us)
Async XLA Ops:
  4.7 28.1 %collective-permute-start = (bf16[144,1024]{1,0:T(8,128)(2,1)}, bf16[144,1024]{1,0:T(8,128)(2,1)S(1)}, u32[]{:S(2)}, u32[]{:S(2)}) collective-permute-start(bf16[144,1024]{1,0:T(8,128)(2,1)} %get-tuple-element.77.refs_1_), channel_id=1, source_target_pairs={{0,4},{1,9},{2,6},{3,11},{4,12},{5,1},{6,14},{7,3},{8,0},{9,17},{1... | collective-permute-start | bytes 884744 | tf_op jit(solution)/shard_map/ppermute | solution.py:755
  7.8 25.1 %collective-permute-start.1 = (bf16[144,1024]{1,0:T(8,128)(2,1)}, bf16[144,1024]{1,0:T(8,128)(2,1)S(1)}, u32[]{:S(2)}, u32[]{:S(2)}) collective-permute-start(bf16[144,1024]{1,0:T(8,128)(2,1)} %get-tuple-element.78.refs_9_.refs_1_), channel_id=1, source_target_pairs={{0,4},{1,9},{2,6},{3,11},{4,12},{5,1},{6,14},{7,3},{8,0},{9,17},{1... | collective-permute-start | bytes 884744 | tf_op jit(solution)/shard_map/ppermute | solution.py:755
  9.3 24.0 %collective-permute-start.2 = (bf16[128,2048]{1,0:T(8,128)(2,1)}, bf16[128,2048]{1,0:T(8,128)(2,1)}, u32[]{:S(2)}, u32[]{:S(2)}) collective-permute-start(bf16[128,2048]{1,0:T(8,128)(2,1)} %get-tuple-element.79.refs_2_), channel_id=1, source_target_pairs={{0,4},{1,9},{2,6},{3,11},{4,12},{5,1},{6,14},{7,3},{8,0},{9,17},{1... | collective-permute-start | bytes 1572872 | tf_op jit(solution)/shard_map/ppermute | solution.py:755
  10.9 22.4 %collective-permute-start.3 = (bf16[256,1024]{1,0:T(8,128)(2,1)}, bf16[256,1024]{1,0:T(8,128)(2,1)}, u32[]{:S(2)}, u32[]{:S(2)}) collective-permute-start(bf16[256,1024]{1,0:T(8,128)(2,1)} %get-tuple-element.80.refs_9_), channel_id=1, source_target_pairs={{0,4},{1,9},{2,6},{3,11},{4,12},{5,1},{6,14},{7,3},{8,0},{9,17},{1... | collective-permute-start | bytes 1572872 | tf_op jit(solution)/shard_map/ppermute | solution.py:755
  34.0 11.3 %collective-permute-start.4 = (bf16[512,1024]{1,0:T(8,128)(2,1)}, bf16[512,1024]{1,0:T(8,128)(2,1)S(1)}, u32[]{:S(2)}, u32[]{:S(2)}) collective-permute-start(bf16[512,1024]{1,0:T(8,128)(2,1)} %after.15), channel_id=1, source_target_pairs={{0,1},{1,0},{2,3},{3,2},{4,5},{5,4},{6,7},{7,6},{8,9},{9,8},{10,11... | collective-permute-start | bytes 3145736 | tf_op jit(solution)/shard_map/ppermute | solution.py:755
  34.7 7.0 %collective-permute-start.7 = (bf16[144,1024]{1,0:T(8,128)(2,1)}, bf16[144,1024]{1,0:T(8,128)(2,1)S(1)}, u32[]{:S(2)}, u32[]{:S(2)}) collective-permute-start(bf16[144,1024]{1,0:T(8,128)(2,1)} %copy-done.7), channel_id=1, source_target_pairs={{0,4},{1,9},{2,6},{3,11},{4,12},{5,1},{6,14},{7,3},{8,0},{9,17},{1... | collective-permute-start | bytes 884744 | tf_op jit(solution)/shard_map/ppermute | solution.py:755
  35.2 9.6 %collective-permute-start.13 = (bf16[144,1024]{1,0:T(8,128)(2,1)}, bf16[144,1024]{1,0:T(8,128)(2,1)S(1)}, u32[]{:S(2)}, u32[]{:S(2)}) collective-permute-start(bf16[144,1024]{1,0:T(8,128)(2,1)} %copy-done.9), channel_id=1, source_target_pairs={{0,4},{1,9},{2,6},{3,11},{4,12},{5,1},{6,14},{7,3},{8,0},{9,17},{1... | collective-permute-start | bytes 884744 | tf_op jit(solution)/shard_map/ppermute | solution.py:755
  41.7 47.6 %copy-start.21 = (bf16[144,1024]{1,0:T(8,128)(2,1)}, bf16[144,1024]{1,0:T(8,128)(2,1)S(1)}, u32[]{:S(2)}) copy-start(bf16[144,1024]{1,0:T(8,128)(2,1)S(1)} %collective-permute-done.7.refs_3_) | copy-start | bytes 884740
  41.7 6.7 %collective-permute-start.8 = (bf16[144,1024]{1,0:T(8,128)(2,1)S(1)}, bf16[144,1024]{1,0:T(8,128)(2,1)S(1)}, u32[]{:S(2)}, u32[]{:S(2)}) collective-permute-start(bf16[144,1024]{1,0:T(8,128)(2,1)S(1)} %collective-permute-done.7.refs_3_), channel_id=1, source_target_pairs={{0,4},{1,9},{2,6},{3,11},{4,12},{5,1},{6,14},{7,3},{8,0},{9,17},{1... | collective-permute-start | bytes 884744 | tf_op jit(solution)/shard_map/ppermute | solution.py:755
  44.8 59.2 %copy-start.23 = (bf16[144,1024]{1,0:T(8,128)(2,1)}, bf16[144,1024]{1,0:T(8,128)(2,1)S(1)}, u32[]{:S(2)}) copy-start(bf16[144,1024]{1,0:T(8,128)(2,1)S(1)} %collective-permute-done.13.refs_11_.refs_3_) | copy-start | bytes 884740
  44.8 6.7 %collective-permute-start.14 = (bf16[144,1024]{1,0:T(8,128)(2,1)S(1)}, bf16[144,1024]{1,0:T(8,128)(2,1)S(1)}, u32[]{:S(2)}, u32[]{:S(2)}) collective-permute-start(bf16[144,1024]{1,0:T(8,128)(2,1)S(1)} %collective-permute-done.13.refs_11_.refs_3_), channel_id=1, source_target_pairs={{0,4},{1,9},{2,6},{3,11},{4,12},{5,1},{6,14},{7,3},{8,0},{9,17},{1... | collective-permute-start | bytes 884744 | tf_op jit(solution)/shard_map/ppermute | solution.py:755
  49.1 6.9 %collective-permute-start.9 = (bf16[144,1024]{1,0:T(8,128)(2,1)}, bf16[144,1024]{1,0:T(8,128)(2,1)S(1)}, u32[]{:S(2)}, u32[]{:S(2)}) collective-permute-start(bf16[144,1024]{1,0:T(8,128)(2,1)} %after.16.refs_4_), channel_id=1, source_target_pairs={{0,4},{1,9},{2,6},{3,11},{4,12},{5,1},{6,14},{7,3},{8,0},{9,17},{1... | collective-permute-start | bytes 884744 | tf_op jit(solution)/shard_map/ppermute | solution.py:755
  52.3 7.0 %collective-permute-start.15 = (bf16[144,1024]{1,0:T(8,128)(2,1)}, bf16[144,1024]{1,0:T(8,128)(2,1)S(1)}, u32[]{:S(2)}, u32[]{:S(2)}) collective-permute-start(bf16[144,1024]{1,0:T(8,128)(2,1)} %after.17.refs_12_.refs_4_), channel_id=1, source_target_pairs={{0,4},{1,9},{2,6},{3,11},{4,12},{5,1},{6,14},{7,3},{8,0},{9,17},{1... | collective-permute-start | bytes 884744 | tf_op jit(solution)/shard_map/ppermute | solution.py:755
  52.8 24.3 %collective-permute-start.5 = (bf16[512,1024]{1,0:T(8,128)(2,1)}, bf16[512,1024]{1,0:T(8,128)(2,1)}, u32[]{:S(2)}, u32[]{:S(2)}) collective-permute-start(bf16[512,1024]{1,0:T(8,128)(2,1)} %fusion.refs_0_.refs_1_), channel_id=1, source_target_pairs={{0,2},{1,3},{2,0},{3,1},{4,6},{5,7},{6,4},{7,5},{8,10},{9,11},{10,... | collective-permute-start | bytes 3145736 | tf_op jit(solution)/shard_map/ppermute | solution.py:755
  56.1 33.2 %copy-start.24 = (bf16[144,1024]{1,0:T(8,128)(2,1)}, bf16[144,1024]{1,0:T(8,128)(2,1)S(1)}, u32[]{:S(2)}) copy-start(bf16[144,1024]{1,0:T(8,128)(2,1)S(1)} %collective-permute-done.9.refs_5_) | copy-start | bytes 884740
  56.1 6.8 %collective-permute-start.10 = (bf16[144,1024]{1,0:T(8,128)(2,1)S(1)}, bf16[144,1024]{1,0:T(8,128)(2,1)}, u32[]{:S(2)}, u32[]{:S(2)}) collective-permute-start(bf16[144,1024]{1,0:T(8,128)(2,1)S(1)} %collective-permute-done.9.refs_5_), channel_id=1, source_target_pairs={{0,4},{1,9},{2,6},{3,11},{4,12},{5,1},{6,14},{7,3},{8,0},{9,17},{1... | collective-permute-start | bytes 884744 | tf_op jit(solution)/shard_map/ppermute | solution.py:755
  59.2 6.7 %collective-permute-start.16 = (bf16[144,1024]{1,0:T(8,128)(2,1)S(1)}, bf16[144,1024]{1,0:T(8,128)(2,1)S(1)}, u32[]{:S(2)}, u32[]{:S(2)}) collective-permute-start(bf16[144,1024]{1,0:T(8,128)(2,1)S(1)} %collective-permute-done.15.refs_13_.refs_5_), channel_id=1, source_target_pairs={{0,4},{1,9},{2,6},{3,11},{4,12},{5,1},{6,14},{7,3},{8,0},{9,17},{1... | collective-permute-start | bytes 884744 | tf_op jit(solution)/shard_map/ppermute | solution.py:755
  62.9 6.9 %collective-permute-start.11 = (bf16[144,1024]{1,0:T(8,128)(2,1)}, bf16[144,1024]{1,0:T(8,128)(2,1)S(1)}, u32[]{:S(2)}, u32[]{:S(2)}) collective-permute-start(bf16[144,1024]{1,0:T(8,128)(2,1)} %collective-permute-done.10.refs_6_.refs_1_), channel_id=1, source_target_pairs={{0,4},{1,9},{2,6},{3,11},{4,12},{5,1},{6,14},{7,3},{8,0},{9,17},{1... | collective-permute-start | bytes 884744 | tf_op jit(solution)/shard_map/ppermute | solution.py:755
  66.0 7.1 %collective-permute-start.17 = (bf16[144,1024]{1,0:T(8,128)(2,1)S(1)}, bf16[144,1024]{1,0:T(8,128)(2,1)}, u32[]{:S(2)}, u32[]{:S(2)}) collective-permute-start(bf16[144,1024]{1,0:T(8,128)(2,1)S(1)} %collective-permute-done.16.refs_14_.refs_6_), channel_id=1, source_target_pairs={{0,4},{1,9},{2,6},{3,11},{4,12},{5,1},{6,14},{7,3},{8,0},{9,17},{1... | collective-permute-start | bytes 884744 | tf_op jit(solution)/shard_map/ppermute | solution.py:755
  66.5 20.9 %copy-start.8 = (bf16[144,1024]{1,0:T(8,128)(2,1)S(1)}, bf16[144,1024]{1,0:T(8,128)(2,1)}, u32[]{:S(2)}) copy-start(bf16[144,1024]{1,0:T(8,128)(2,1)} %copy-done.7) | copy-start | bytes 884740
  66.5 20.9 %copy-start.14 = (bf16[144,1024]{1,0:T(8,128)(2,1)S(1)}, bf16[144,1024]{1,0:T(8,128)(2,1)}, u32[]{:S(2)}) copy-start(bf16[144,1024]{1,0:T(8,128)(2,1)} %after.16.refs_4_) | copy-start | bytes 884740
  66.5 20.9 %copy-start.15 = (bf16[144,1024]{1,0:T(8,128)(2,1)S(1)}, bf16[144,1024]{1,0:T(8,128)(2,1)}, u32[]{:S(2)}) copy-start(bf16[144,1024]{1,0:T(8,128)(2,1)} %get-tuple-element.77.refs_1_) | copy-start | bytes 884740
  66.5 20.9 %copy-start.50 = (s32[8,2,8]{2,1,0:T(2,128)S(1)}, s32[8,2,8]{2,1,0:T(2,128)}, u32[]{:S(2)}) copy-start(s32[8,2,8]{2,1,0:T(2,128)} %constant.86.clone.refs_0_) | copy-start | bytes 1540
  66.5 26.6 %collective-permute-start.31 = (bf16[256,1024]{1,0:T(8,128)(2,1)}, bf16[256,1024]{1,0:T(8,128)(2,1)S(1)}, u32[]{:S(2)}, u32[]{:S(2)}) collective-permute-start(bf16[256,1024]{1,0:T(8,128)(2,1)} %after.23.refs_10_), channel_id=1, source_target_pairs={{0,4},{1,9},{2,6},{3,11},{4,12},{5,1},{6,14},{7,3},{8,0},{9,17},{1... | collective-permute-start | bytes 1572872 | tf_op jit(solution)/shard_map/ppermute | solution.py:755
  67.0 27.5 %collective-permute-start.25 = (bf16[128,2048]{1,0:T(8,128)(2,1)}, bf16[128,2048]{1,0:T(8,128)(2,1)}, u32[]{:S(2)}, u32[]{:S(2)}) collective-permute-start(bf16[128,2048]{1,0:T(8,128)(2,1)} %after.18.refs_3_), channel_id=1, source_target_pairs={{0,4},{1,9},{2,6},{3,11},{4,12},{5,1},{6,14},{7,3},{8,0},{9,17},{1... | collective-permute-start | bytes 1572872 | tf_op jit(solution)/shard_map/ppermute | solution.py:755
  69.8 17.6 %collective-permute-start.12 = (bf16[144,1024]{1,0:T(8,128)(2,1)S(1)}, bf16[144,1024]{1,0:T(8,128)(2,1)S(1)}, u32[]{:S(2)}, u32[]{:S(2)}) collective-permute-start(bf16[144,1024]{1,0:T(8,128)(2,1)S(1)} %collective-permute-done.11.refs_7_), channel_id=1, source_target_pairs={{0,4},{1,9},{2,6},{3,11},{4,12},{5,1},{6,14},{7,3},{8,0},{9,17},{1... | collective-permute-start | bytes 884744 | tf_op jit(solution)/shard_map/ppermute | solution.py:755
  73.1 21.8 %collective-permute-start.18 = (bf16[144,1024]{1,0:T(8,128)(2,1)}, bf16[144,1024]{1,0:T(8,128)(2,1)}, u32[]{:S(2)}, u32[]{:S(2)}) collective-permute-start(bf16[144,1024]{1,0:T(8,128)(2,1)} %collective-permute-done.17.refs_15_.refs_7_), channel_id=1, source_target_pairs={{0,4},{1,9},{2,6},{3,11},{4,12},{5,1},{6,14},{7,3},{8,0},{9,17},{1... | collective-permute-start | bytes 884744 | tf_op jit(solution)/shard_map/ppermute | solution.py:755
  80.0 35.0 %collective-permute-start.6 = (bf16[512,1024]{1,0:T(8,128)(2,1)}, bf16[512,1024]{1,0:T(8,128)(2,1)}, u32[]{:S(2)}, u32[]{:S(2)}) collective-permute-start(bf16[512,1024]{1,0:T(8,128)(2,1)} %add.91), channel_id=1, source_target_pairs={{0,1},{1,0},{2,3},{3,2},{4,5},{5,4},{6,7},{7,6},{8,9},{9,8},{10,11... | collective-permute-start | bytes 3145736 | tf_op jit(solution)/shard_map/ppermute | solution.py:755
  94.0 13.0 %collective-permute-start.32 = (bf16[256,1024]{1,0:T(8,128)(2,1)}, bf16[256,1024]{1,0:T(8,128)(2,1)}, u32[]{:S(2)}, u32[]{:S(2)}) collective-permute-start(bf16[256,1024]{1,0:T(8,128)(2,1)} %after.24.refs_11_), channel_id=1, source_target_pairs={{0,4},{1,9},{2,6},{3,11},{4,12},{5,1},{6,14},{7,3},{8,0},{9,17},{1... | collective-permute-start | bytes 1572872 | tf_op jit(solution)/shard_map/ppermute | solution.py:755
  94.5 14.6 %collective-permute-start.26 = (bf16[128,2048]{1,0:T(8,128)(2,1)}, bf16[128,2048]{1,0:T(8,128)(2,1)}, u32[]{:S(2)}, u32[]{:S(2)}) collective-permute-start(bf16[128,2048]{1,0:T(8,128)(2,1)} %after.19.refs_4_), channel_id=1, source_target_pairs={{0,4},{1,9},{2,6},{3,11},{4,12},{5,1},{6,14},{7,3},{8,0},{9,17},{1... | collective-permute-start | bytes 1572872 | tf_op jit(solution)/shard_map/ppermute | solution.py:755
  99.0 23.6 %collective-permute-start.22 = (bf16[1024,512]{1,0:T(8,128)(2,1)S(1)}, bf16[1024,512]{1,0:T(8,128)(2,1)}, u32[]{:S(2)}, u32[]{:S(2)}) collective-permute-start(bf16[1024,512]{1,0:T(8,128)(2,1)S(1)} %assemble.7.refs_13_.refs_2_), channel_id=1, source_target_pairs={{0,1},{1,0},{2,3},{3,2},{4,5},{5,4},{6,7},{7,6},{8,9},{9,8},{10,11... | collective-permute-start | bytes 3145736 | tf_op jit(solution)/shard_map/ppermute | solution.py:755
  107.0 12.8 %collective-permute-start.33 = (bf16[256,1024]{1,0:T(8,128)(2,1)}, bf16[256,1024]{1,0:T(8,128)(2,1)}, u32[]{:S(2)}, u32[]{:S(2)}) collective-permute-start(bf16[256,1024]{1,0:T(8,128)(2,1)} %after.25.refs_12_), channel_id=1, source_target_pairs={{0,4},{1,9},{2,6},{3,11},{4,12},{5,1},{6,14},{7,3},{8,0},{9,17},{1... | collective-permute-start | bytes 1572872 | tf_op jit(solution)/shard_map/ppermute | solution.py:755
  109.1 13.0 %collective-permute-start.27 = (bf16[128,2048]{1,0:T(8,128)(2,1)}, bf16[128,2048]{1,0:T(8,128)(2,1)}, u32[]{:S(2)}, u32[]{:S(2)}) collective-permute-start(bf16[128,2048]{1,0:T(8,128)(2,1)} %after.20.refs_5_), channel_id=1, source_target_pairs={{0,4},{1,9},{2,6},{3,11},{4,12},{5,1},{6,14},{7,3},{8,0},{9,17},{1... | collective-permute-start | bytes 1572872 | tf_op jit(solution)/shard_map/ppermute | solution.py:755
  109.6 28.1 %collective-permute-start.21 = (bf16[1024,512]{1,0:T(8,128)(2,1)}, bf16[1024,512]{1,0:T(8,128)(2,1)}, u32[]{:S(2)}, u32[]{:S(2)}) collective-permute-start(bf16[1024,512]{1,0:T(8,128)(2,1)} %assemble.6.refs_12_.refs_1_), channel_id=1, source_target_pairs={{0,1},{1,0},{2,3},{3,2},{4,5},{5,4},{6,7},{7,6},{8,9},{9,8},{10,11... | collective-permute-start | bytes 3145736 | tf_op jit(solution)/shard_map/ppermute | solution.py:755
  115.0 22.7 %collective-permute-start.20 = (bf16[1024,512]{1,0:T(8,128)(2,1)S(1)}, bf16[1024,512]{1,0:T(8,128)(2,1)}, u32[]{:S(2)}, u32[]{:S(2)}) collective-permute-start(bf16[1024,512]{1,0:T(8,128)(2,1)S(1)} %copy-done.1), channel_id=1, source_target_pairs={{0,1},{1,0},{2,3},{3,2},{4,5},{5,4},{6,7},{7,6},{8,9},{9,8},{10,11... | collective-permute-start | bytes 3145736 | tf_op jit(solution)/shard_map/ppermute | solution.py:755
  119.7 18.0 %collective-permute-start.19 = (bf16[1024,512]{1,0:T(8,128)(2,1)S(1)}, bf16[1024,512]{1,0:T(8,128)(2,1)}, u32[]{:S(2)}, u32[]{:S(2)}) collective-permute-start(bf16[1024,512]{1,0:T(8,128)(2,1)S(1)} %copy-done.3), channel_id=1, source_target_pairs={{0,1},{1,0},{2,3},{3,2},{4,5},{5,4},{6,7},{7,6},{8,9},{9,8},{10,11... | collective-permute-start | bytes 3145736 | tf_op jit(solution)/shard_map/ppermute | solution.py:755
  122.1 9.5 %collective-permute-start.34 = (bf16[256,1024]{1,0:T(8,128)(2,1)}, bf16[256,1024]{1,0:T(8,128)(2,1)}, u32[]{:S(2)}, u32[]{:S(2)}) collective-permute-start(bf16[256,1024]{1,0:T(8,128)(2,1)} %after.26.refs_13_), channel_id=1, source_target_pairs={{0,4},{1,9},{2,6},{3,11},{4,12},{5,1},{6,14},{7,3},{8,0},{9,17},{1... | collective-permute-start | bytes 1572872 | tf_op jit(solution)/shard_map/ppermute | solution.py:755
  122.6 14.6 %collective-permute-start.28 = (bf16[128,2048]{1,0:T(8,128)(2,1)}, bf16[128,2048]{1,0:T(8,128)(2,1)}, u32[]{:S(2)}, u32[]{:S(2)}) collective-permute-start(bf16[128,2048]{1,0:T(8,128)(2,1)} %after.21.refs_6_), channel_id=1, source_target_pairs={{0,4},{1,9},{2,6},{3,11},{4,12},{5,1},{6,14},{7,3},{8,0},{9,17},{1... | collective-permute-start | bytes 1572872 | tf_op jit(solution)/shard_map/ppermute | solution.py:755
  131.6 20.4 %collective-permute-start.35 = (bf16[256,1024]{1,0:T(8,128)(2,1)}, bf16[256,1024]{1,0:T(8,128)(2,1)S(1)}, u32[]{:S(2)}, u32[]{:S(2)}) collective-permute-start(bf16[256,1024]{1,0:T(8,128)(2,1)} %collective-permute-done.34.refs_14_), channel_id=1, source_target_pairs={{0,4},{1,9},{2,6},{3,11},{4,12},{5,1},{6,14},{7,3},{8,0},{9,17},{1... | collective-permute-start | bytes 1572872 | tf_op jit(solution)/shard_map/ppermute | solution.py:755
  137.2 16.1 %collective-permute-start.29 = (bf16[128,2048]{1,0:T(8,128)(2,1)}, bf16[128,2048]{1,0:T(8,128)(2,1)S(1)}, u32[]{:S(2)}, u32[]{:S(2)}) collective-permute-start(bf16[128,2048]{1,0:T(8,128)(2,1)} %collective-permute-done.28.refs_7_), channel_id=1, source_target_pairs={{0,4},{1,9},{2,6},{3,11},{4,12},{5,1},{6,14},{7,3},{8,0},{9,17},{1... | collective-permute-start | bytes 1572872 | tf_op jit(solution)/shard_map/ppermute | solution.py:755
  152.8 9.4 %collective-permute-start.36 = (bf16[256,1024]{1,0:T(8,128)(2,1)}, bf16[256,1024]{1,0:T(8,128)(2,1)S(1)}, u32[]{:S(2)}, u32[]{:S(2)}) collective-permute-start(bf16[256,1024]{1,0:T(8,128)(2,1)} %after.27.refs_15_), channel_id=1, source_target_pairs={{0,4},{1,9},{2,6},{3,11},{4,12},{5,1},{6,14},{7,3},{8,0},{9,17},{1... | collective-permute-start | bytes 1572872 | tf_op jit(solution)/shard_map/ppermute | solution.py:755
  154.1 13.8 %collective-permute-start.30 = (bf16[128,2048]{1,0:T(8,128)(2,1)}, bf16[128,2048]{1,0:T(8,128)(2,1)S(1)}, u32[]{:S(2)}, u32[]{:S(2)}) collective-permute-start(bf16[128,2048]{1,0:T(8,128)(2,1)} %after.22.refs_8_), channel_id=1, source_target_pairs={{0,4},{1,9},{2,6},{3,11},{4,12},{5,1},{6,14},{7,3},{8,0},{9,17},{1... | collective-permute-start | bytes 1572872 | tf_op jit(solution)/shard_map/ppermute | solution.py:755
  155.4 5.8 %collective-permute-start.23 = (bf16[32,1152]{1,0:T(8,128)(2,1)S(1)}, bf16[32,1152]{1,0:T(8,128)(2,1)S(1)}, u32[]{:S(2)}, u32[]{:S(2)}) collective-permute-start(bf16[32,1152]{1,0:T(8,128)(2,1)S(1)} %copy-done.43), channel_id=1, source_target_pairs={{0,1},{1,0},{2,3},{3,2},{4,5},{5,4},{6,7},{7,6},{8,9},{9,8},{10,11... | collective-permute-start | bytes 221192 | tf_op jit(solution)/shard_map/ppermute | solution.py:755
  155.4 5.8 %collective-permute-start.24 = (bf16[16,2048]{1,0:T(8,128)(2,1)S(1)}, bf16[16,2048]{1,0:T(8,128)(2,1)S(1)}, u32[]{:S(2)}, u32[]{:S(2)}) collective-permute-start(bf16[16,2048]{1,0:T(8,128)(2,1)S(1)} %copy-done.68), channel_id=1, source_target_pairs={{0,1},{1,0},{2,3},{3,2},{4,5},{5,4},{6,7},{7,6},{8,9},{9,8},{10,11... | collective-permute-start | bytes 196616 | tf_op jit(solution)/shard_map/ppermute | solution.py:755
  171.0 1.4 collective-permute-start.37
  173.3 1.9 collective-permute-start.38
  173.5 3.8 %collective-permute-start.39 = (f32[32,128]{1,0:T(8,128)S(1)}, f32[32,128]{1,0:T(8,128)S(1)}, u32[]{:S(2)}, u32[]{:S(2)}) collective-permute-start(f32[32,128]{1,0:T(8,128)S(1)} %get-tuple-element.98.refs_0_.refs_1_), channel_id=1, source_target_pairs={{0,2},{1,3},{2,0},{3,1},{4,6},{5,7},{6,4},{7,5},{8,10},{9,11},{10,... | collective-permute-start | bytes 49160 | tf_op jit(solution)/shard_map/ppermute | solution.py:755
  175.0 3.2 %collective-permute-start.40 = (f32[32,128]{1,0:T(8,128)S(1)}, f32[32,128]{1,0:T(8,128)S(1)}, u32[]{:S(2)}, u32[]{:S(2)}) collective-permute-start(f32[32,128]{1,0:T(8,128)S(1)} %get-tuple-element.98.refs_0_.refs_1_), channel_id=1, source_target_pairs={{0,3},{1,2},{2,1},{3,0},{4,7},{5,6},{6,5},{7,4},{8,11},{9,10},{10,... | collective-permute-start | bytes 49160 | tf_op jit(solution)/shard_map/ppermute | solution.py:755
  179.1 1.3 collective-permute-start.41
  184.0 1.4 collective-permute-start.46
  184.2 4.1 %collective-permute-start.42 = (f32[32,1152]{1,0:T(8,128)S(1)}, f32[32,1152]{1,0:T(8,128)S(1)}, u32[]{:S(2)}, u32[]{:S(2)}) collective-permute-start(f32[32,1152]{1,0:T(8,128)S(1)} %get-tuple-element.107), channel_id=1, source_target_pairs={{0,1},{1,0},{2,3},{3,2},{4,5},{5,4},{6,7},{7,6},{8,9},{9,8},{10,11... | collective-permute-start | bytes 442376 | tf_op jit(solution)/shard_map/ppermute | solution.py:755
  185.8 10.2 %collective-permute-start.47 = (f32[8,4096]{1,0:T(8,128)S(1)}, f32[8,4096]{1,0:T(8,128)S(1)}, u32[]{:S(2)}, u32[]{:S(2)}) collective-permute-start(f32[8,4096]{1,0:T(8,128)S(1)} %get-tuple-element.122), channel_id=1, source_target_pairs={{0,16},{1,17},{2,18},{3,19},{4,20},{5,21},{6,22},{7,23},{8,24},{9,... | collective-permute-start | bytes 393224 | tf_op jit(solution)/shard_map/ppermute | solution.py:755
  195.5 29.4 %copy-start.53 = (f32[1,128,2,40]{1,3,2,0:T(8,128)S(1)}, f32[1,128,2,40]{1,3,2,0:T(8,128)}, u32[]{:S(2)}) copy-start(f32[1,128,2,40]{1,3,2,0:T(8,128)} %param.35) | copy-start | bytes 122884
  195.5 29.4 %copy-start.55 = (f32[1,512,16]{1,2,0:T(8,128)S(1)}, f32[1,512,16]{1,2,0:T(8,128)}, u32[]{:S(2)}) copy-start(f32[1,512,16]{1,2,0:T(8,128)} %param.36) | copy-start | bytes 98308
  195.5 29.4 %copy-start.58 = (f32[1,128,2,40]{1,3,2,0:T(8,128)S(1)}, f32[1,128,2,40]{1,3,2,0:T(8,128)}, u32[]{:S(2)}) copy-start(f32[1,128,2,40]{1,3,2,0:T(8,128)} %param.38) | copy-start | bytes 122884
  195.5 29.4 %copy-start.59 = (f32[1,512,16]{1,2,0:T(8,128)S(1)}, f32[1,512,16]{1,2,0:T(8,128)}, u32[]{:S(2)}) copy-start(f32[1,512,16]{1,2,0:T(8,128)} %param.39) | copy-start | bytes 98308
  195.5 29.4 %copy-start.64 = (f32[1,128]{1,0:T(1,128)S(1)}, f32[1,128]{1,0:T(1,128)}, u32[]{:S(2)}) copy-start(f32[1,128]{1,0:T(1,128)} %refs_10_.1) | copy-start | bytes 1540
  195.5 29.4 %copy-start.65 = (f32[1,128]{1,0:T(1,128)S(1)}, f32[1,128]{1,0:T(1,128)}, u32[]{:S(2)}) copy-start(f32[1,128]{1,0:T(1,128)} %refs_13_.1) | copy-start | bytes 1540
  195.5 4.7 %collective-permute-start.43 = (f32[24,1024]{1,0:T(8,128)S(1)}, f32[24,1024]{1,0:T(8,128)S(1)}, u32[]{:S(2)}, u32[]{:S(2)}) collective-permute-start(f32[24,1024]{1,0:T(8,128)S(1)} %get-tuple-element.117), channel_id=1, source_target_pairs={{0,4},{1,5},{2,6},{3,7},{4,0},{5,1},{6,2},{7,3},{8,12},{9,13},{10,... | collective-permute-start | bytes 294920 | tf_op jit(solution)/shard_map/ppermute | solution.py:755
  196.0 5.8 %collective-permute-start.48 = (f32[8,4096]{1,0:T(8,128)S(1)}, f32[8,4096]{1,0:T(8,128)S(1)}, u32[]{:S(2)}, u32[]{:S(2)}) collective-permute-start(f32[8,4096]{1,0:T(8,128)S(1)} %add.100), channel_id=1, source_target_pairs={{0,8},{1,9},{2,10},{3,11},{4,12},{5,13},{6,14},{7,15},{8,0},{9,1},... | collective-permute-start | bytes 393224 | tf_op jit(solution)/shard_map/ppermute | solution.py:755
  200.2 4.7 %collective-permute-start.44 = (f32[24,1024]{1,0:T(8,128)S(1)}, f32[24,1024]{1,0:T(8,128)S(1)}, u32[]{:S(2)}, u32[]{:S(2)}) collective-permute-start(f32[24,1024]{1,0:T(8,128)S(1)} %add.98), channel_id=1, source_target_pairs={{0,8},{1,9},{2,10},{3,11},{4,12},{5,13},{6,14},{7,15},{8,0},{9,1},... | collective-permute-start | bytes 294920 | tf_op jit(solution)/shard_map/ppermute | solution.py:755
  201.9 8.7 %collective-permute-start.49 = (f32[8,4096]{1,0:T(8,128)S(1)}, f32[8,4096]{1,0:T(8,128)S(1)}, u32[]{:S(2)}, u32[]{:S(2)}) collective-permute-start(f32[8,4096]{1,0:T(8,128)S(1)} %add.101.refs_2_), channel_id=1, source_target_pairs={{0,4},{1,5},{2,6},{3,7},{4,0},{5,1},{6,2},{7,3},{8,12},{9,13},{10,... | collective-permute-start | bytes 393224 | tf_op jit(solution)/shard_map/ppermute | solution.py:755
  204.9 5.6 %collective-permute-start.45 = (f32[24,1024]{1,0:T(8,128)S(1)}, f32[24,1024]{1,0:T(8,128)S(1)}, u32[]{:S(2)}, u32[]{:S(2)}) collective-permute-start(f32[24,1024]{1,0:T(8,128)S(1)} %add.99.refs_0_), channel_id=1, source_target_pairs={{0,16},{1,17},{2,18},{3,19},{4,20},{5,21},{6,22},{7,23},{8,24},{9,... | collective-permute-start | bytes 294920 | tf_op jit(solution)/shard_map/ppermute | solution.py:755
  213.6 11.3 %all-to-all-start = ((f32[32,8,128]{2,1,0:T(8,128)}), f32[32,8,128]{2,1,0:T(8,128)S(1)}, u32[]{:S(2)}, u32[]{:S(2)}) async-start(f32[32,8,128]{2,1,0:T(8,128)} %get-tuple-element.125), calls=%async_computation | async-start | bytes 262144 | tf_op jit(solution)/shard_map/all_to_all | solution.py:1021
  (62 other events, 308.5 us)

commit v4 on v3

--- a/solution.py
+++ b/solution.py
@@ -445,7 +445,6 @@
     hl = refs[13 : 13 + micro]
     h1 = refs[13 + micro : 13 + 2 * micro]
     ad, gains, err, start, w_out, mat, left = refs[13 + 2 * micro :]
-    ready(ad, gains)
     rows, width = x1.shape
     slots = rows // micro
     heads = width // HEAD_DIM
@@ -976,7 +975,7 @@
     y_mine, y_send, g_f = call(
         functools.partial(ffn_back_kernel, rank),
         [Kept((rows, width + 128), F32)] * 2 + [Kept((2 * rows, own_hidden), BF16)],
-        [Fresh(e2), Fresh(e2_sib), Fresh(slope), f_own, f_sib,
+        [Fresh(e2), Fresh(e2_sib), Fresh(slope), Fresh(f_own), Fresh(f_sib),
          Fresh(w_up), Fresh(w_down)],
         vmem=14, name="ffn_back",
     )
@@ -998,7 +997,7 @@
         [Kept((2, 5 * rank, width), F32), Kept((2 * rank + 8, width), F32)],
         [Fresh(y_mine), Fresh(y_other), Fresh(g_end), Fresh(g_dn), Fresh(small),
          *[Fresh(x) for x in (x1, e1, u, o, q, p_t, kv, ukv_t, *hl, *h1)],
-         wide_d, base_gains, err_d[0, 0].transpose(1, 2, 0), qstart_d[0].transpose(0, 2, 1), Fresh(w_out)],
+         Fresh(wide_d), Fresh(base_gains), err_d[0, 0].transpose(1, 2, 0), qstart_d[0].transpose(0, 2, 1), Fresh(w_out)],
         vmem=26, name="rows_back",
     )
 

time: 228 us -> 228 us (level)
  no operation moved by 1% of the time
where the time goes in v4:
time: 228 us; the launch traced here: 227 us
  waiting for transfers between devices  82 us (36%)
  Pallas kernels  61.9 us (27%)
  starting transfers between devices  37.5 us (16%)
  local copies, waits for them, and re-layouts  37.1 us (16%)
  other arithmetic  6.72 us (3%)
    ppermute x50, waiting for transfers between devices, send(): return lax.ppermute(x, AXES, perm)  73.8 us
    pallas_call x20, Pallas kernels, call(): pl.pallas_call(kernel, out_shape=tuple((jax.ShapeDtypeStruct(o.shape, o.d...  61.9 us
    ppermute x50, starting transfers between devices, send(): return lax.ppermute(x, AXES, perm)  34.5 us
    gather x1, local copies, waits for them, and re-layouts, lookup(): jnp.take(embed_table, after(jnp.clip(near, 0, held - 1), *start), axis=0)  16.6 us
    unnamed x149, local copies, waits for them, and re-layouts  13.6 us
    all_to_all x1, waiting for transfers between devices, on_device(): notes = lax.all_to_all(note, AXES, 0, 0)  8.17 us
  transfers between devices with their start and end apart: 51, of which 27 were waited for; matrix products, arithmetic and copies ran while one was open for 13% of the time, Pallas kernels for 20%

profile of v4, /device:TPU:0, one launch (start us, length us, event | category | flops | bytes accessed | tf_op | source)
XLA Modules:
  0.0 227.0 jit_solution(3554055436281196546)
XLA Ops:
  2.0 2.8 %split.1 = (bf16[144,1024]{1,0:T(8,128)(2,1)}, bf16[144,1024]{1,0:T(8,128)(2,1)}, bf16[128,2048]{1,0:T(8,128)(2,1)}, bf16[256,1024]{1,0:T(8,128)(2,1)}) custom-call(f32[2,40,128]{2,1,0:T(8,128)} %bitcast.68, f32[16,512]{1,0:T(8,128)} %bitcast.73, f32[1,128]{1,0:T(1,128)} %refs_10_.1, s32[1,16]{1,0:T(1,128)} %reshape_squeeze.3.refs_3_, ...), custom_call_target="tpu_custom_call" | custom-call | tf_op jit(solution)/shard_map/split/pallas_call | solution.py:686
  4.7 3.0 %collective-permute-start = (bf16[144,1024]{1,0:T(8,128)(2,1)}, bf16[144,1024]{1,0:T(8,128)(2,1)S(1)}, u32[]{:S(2)}, u32[]{:S(2)}) collective-permute-start(bf16[144,1024]{1,0:T(8,128)(2,1)} %get-tuple-element.77.refs_1_), channel_id=1, source_target_pairs={{0,4},{1,9},{2,6},{3,11},{4,12},{5,1},{6,14},{7,3},{8,0},{9,17},{1... | collective-permute-start | bytes 884744 | tf_op jit(solution)/shard_map/ppermute | solution.py:754
  7.8 1.6 collective-permute-start.1
  9.3 1.6 collective-permute-start.2
  10.9 1.6 collective-permute-start.3
  14.5 16.6 %gather_fusion = bf16[1024,1024]{1,0:T(8,128)(2,1)S(1)} fusion(bf16[12568,1024]{1,0:T(8,128)(2,1)} %param.27, s32[1024]{0:T(1024)S(1)} %broadcast_clamp_fusion), kind=kCustom, calls=%fused_computation | custom fusion | bytes 4198400 | tf_op jit(solution)/shard_map/jit(_take)/gather | solution.py:811
  31.7 1.2 slice_bitcast_fusion.refs_0_
  36.4 2.4 %slice.31.refs_4_.refs_3_ = bf16[512,1024]{1,0:T(8,128)(2,1)} slice(bf16[2050,1024]{1,0:T(8,128)(2,1)} %param.28), slice={[0:512], [0:1024]} | slice | bytes 2097152 | tf_op jit(solution)/shard_map/slice | solution.py:830
  39.4 2.2 collective-permute-done.7.refs_3_
  42.2 2.7 %collective-permute-done.13.refs_11_.refs_3_ = bf16[144,1024]{1,0:T(8,128)(2,1)S(1)} collective-permute-done((bf16[144,1024]{1,0:T(8,128)(2,1)}, bf16[144,1024]{1,0:T(8,128)(2,1)S(1)}, u32[]{:S(2)}, u32[]{:S(2)}) %collective-permute-start.13) | collective-permute-done | bytes 294944 | tf_op jit(solution)/shard_map/ppermute | solution.py:754
  45.4 1.2 fusion.refs_0_.refs_1_
  46.5 1.9 collective-permute-done.8.refs_0_
  49.6 1.9 collective-permute-done.14.refs_0_
  52.8 1.5 collective-permute-start.5
  54.3 1.8 collective-permute-done.9.refs_5_
  56.6 2.7 %collective-permute-done.15.refs_13_.refs_5_ = bf16[144,1024]{1,0:T(8,128)(2,1)S(1)} collective-permute-done((bf16[144,1024]{1,0:T(8,128)(2,1)}, bf16[144,1024]{1,0:T(8,128)(2,1)S(1)}, u32[]{:S(2)}, u32[]{:S(2)}) %collective-permute-start.15) | collective-permute-done | bytes 294944 | tf_op jit(solution)/shard_map/ppermute | solution.py:754
  59.7 3.2 %collective-permute-done.10.refs_6_.refs_1_ = bf16[144,1024]{1,0:T(8,128)(2,1)} collective-permute-done((bf16[144,1024]{1,0:T(8,128)(2,1)S(1)}, bf16[144,1024]{1,0:T(8,128)(2,1)}, u32[]{:S(2)}, u32[]{:S(2)}) %collective-permute-start.10) | collective-permute-done | bytes 294944 | tf_op jit(solution)/shard_map/ppermute | solution.py:754
  63.4 2.5 %collective-permute-done.16.refs_14_.refs_6_ = bf16[144,1024]{1,0:T(8,128)(2,1)S(1)} collective-permute-done((bf16[144,1024]{1,0:T(8,128)(2,1)S(1)}, bf16[144,1024]{1,0:T(8,128)(2,1)S(1)}, u32[]{:S(2)}, u32[]{:S(2)}) %collective-permute-start.16) | collective-permute-done | bytes 294944 | tf_op jit(solution)/shard_map/ppermute | solution.py:754
  67.4 2.4 %collective-permute-done.11.refs_7_ = bf16[144,1024]{1,0:T(8,128)(2,1)S(1)} collective-permute-done((bf16[144,1024]{1,0:T(8,128)(2,1)}, bf16[144,1024]{1,0:T(8,128)(2,1)S(1)}, u32[]{:S(2)}, u32[]{:S(2)}) %collective-permute-start.11) | collective-permute-done | bytes 294944 | tf_op jit(solution)/shard_map/ppermute | solution.py:754
  70.3 2.8 %collective-permute-done.17.refs_15_.refs_7_ = bf16[144,1024]{1,0:T(8,128)(2,1)} collective-permute-done((bf16[144,1024]{1,0:T(8,128)(2,1)S(1)}, bf16[144,1024]{1,0:T(8,128)(2,1)}, u32[]{:S(2)}, u32[]{:S(2)}) %collective-permute-start.17) | collective-permute-done | bytes 294944 | tf_op jit(solution)/shard_map/ppermute | solution.py:754
  73.6 3.5 %collective-permute-done.5.refs_1_ = bf16[512,1024]{1,0:T(8,128)(2,1)} collective-permute-done((bf16[512,1024]{1,0:T(8,128)(2,1)}, bf16[512,1024]{1,0:T(8,128)(2,1)}, u32[]{:S(2)}, u32[]{:S(2)}) %collective-permute-start.5) | collective-permute-done | bytes 1048608 | tf_op jit(solution)/shard_map/ppermute | solution.py:754
  77.1 2.9 %add.91 = bf16[512,1024]{1,0:T(8,128)(2,1)} add(bf16[512,1024]{1,0:T(8,128)(2,1)} %fusion.refs_0_.refs_1_, bf16[512,1024]{1,0:T(8,128)(2,1)} %collective-permute-done.5.refs_1_) | non-fusion elementwise | flops 524288 | bytes 3145728 | tf_op jit(solution)/shard_map/add | solution.py:863
  80.0 7.4 %collective-permute-done.12.refs_8_ = bf16[144,1024]{1,0:T(8,128)(2,1)S(1)} collective-permute-done((bf16[144,1024]{1,0:T(8,128)(2,1)S(1)}, bf16[144,1024]{1,0:T(8,128)(2,1)S(1)}, u32[]{:S(2)}, u32[]{:S(2)}) %collective-permute-start.12) | collective-permute-done | bytes 294944 | tf_op jit(solution)/shard_map/ppermute | solution.py:754
  87.4 1.9 assemble.5.refs_11_.refs_2_
  89.3 1.0 copy-done
  90.3 1.8 assemble.4.refs_10_.refs_1_
  92.2 0.9 copy-done.2
  95.1 1.0 copy-done.27
  96.1 1.0 copy-done.30
  97.0 1.9 assemble.7.refs_13_.refs_2_
  99.1 5.0 %front.2 = (bf16[512,1024]{1,0:T(8,128)(2,1)}, f32[16,1024]{1,0:T(8,128)}, bf16[16,1024]{1,0:T(8,128)(2,1)}) custom-call(bf16[512,1024]{1,0:T(8,128)(2,1)} %fusion.refs_0_.refs_1_, bf16[512,1024]{1,0:T(8,128)(2,1)} %collective-permute-done.5.refs_1_, s32[2,512]{1,0:T(2,128)} %refs_1_.1, s32[2,512]{1,0:T(2,128)} %refs_0_.8, ...), custom_call_target="tpu_custom_call" | custom-call | tf_op jit(solution)/shard_map/front/pallas_call | solution.py:686
  104.1 2.8 %assemble.6.refs_12_.refs_1_ = bf16[1024,512]{1,0:T(8,128)(2,1)} custom-call(s32[8,2,8]{2,1,0:T(2,128)S(1)} %copy-done.50, bf16[144,1024]{1,0:T(8,128)(2,1)S(1)} %copy-done.20, bf16[144,1024]{1,0:T(8,128)(2,1)S(1)} %copy-done.10, bf16[144,1024]{1,0:T(8,128)(2,1)S(1)} %collective-permute-done.13.refs_11_.refs_3_, bf16[144,1024]{1,0:T(8,128)(2,1)S(1)} %copy-done.12, ...), custom_call_target="tpu_custom_call" | custom-call | tf_op jit(solution)/shard_map/assemble/pallas_call | solution.py:686
  107.5 1.6 collective-permute-done.26.refs_0_
  109.6 1.0 copy-done.25
  110.6 3.1 %unpack.1 = (bf16[2,40,1024]{2,1,0:T(8,128)(2,1)S(1)}, bf16[16,2048]{1,0:T(8,128)(2,1)S(1)}, bf16[16,2048]{1,0:T(8,128)(2,1)S(1)}, f32[1,1024]{1,0:T(1,128)S(1)}, f32[1,128]{1,0:T(1,128)}) custom-call(s32[8,2,8]{2,1,0:T(2,128)S(1)} %copy-done.50, bf16[144,1024]{1,0:T(8,128)(2,1)S(1)} %copy-done.15, bf16[144,1024]{1,0:T(8,128)(2,1)S(1)} %copy-done.8, ...), custom_call_target="tpu_custom_call" | custom-call | tf_op jit(solution)/shard_map/unpack/pallas_call | solution.py:686
  115.6 4.1 %front.3 = (bf16[512,1024]{1,0:T(8,128)(2,1)}, f32[16,1024]{1,0:T(8,128)}, bf16[16,1024]{1,0:T(8,128)(2,1)}) custom-call(bf16[512,1024]{1,0:T(8,128)(2,1)} %collective-permute-done.6.refs_0_, s32[2,512]{1,0:T(2,128)} %refs_1_.1, s32[2,512]{1,0:T(2,128)} %refs_0_.8, bf16[512,1024]{1,0:T(8,128)(2,1)} %slice.31.refs_4_.refs_3_, f32[3,1024]{1,0:T(4,128)} %refs_18_.1, ...), custom_call_target="tpu_custom_call" | custom-call | tf_op jit(solution)/shard_map/front/pallas_call | solution.py:686
  119.9 2.2 collective-permute-done.27.refs_0_
  123.1 8.5 %collective-permute-done.34.refs_14_ = bf16[256,1024]{1,0:T(8,128)(2,1)} collective-permute-done((bf16[256,1024]{1,0:T(8,128)(2,1)}, bf16[256,1024]{1,0:T(8,128)(2,1)}, u32[]{:S(2)}, u32[]{:S(2)}) %collective-permute-start.34) | collective-permute-done | bytes 524320 | tf_op jit(solution)/shard_map/ppermute | solution.py:754
  132.1 5.1 %collective-permute-done.28.refs_7_ = bf16[128,2048]{1,0:T(8,128)(2,1)} collective-permute-done((bf16[128,2048]{1,0:T(8,128)(2,1)}, bf16[128,2048]{1,0:T(8,128)(2,1)}, u32[]{:S(2)}, u32[]{:S(2)}) %collective-permute-start.28) | collective-permute-done | bytes 524320 | tf_op jit(solution)/shard_map/ppermute | solution.py:754
  137.7 14.2 %rows.1 = (bf16[2,512,2048]{2,1,0:T(8,128)(2,1)}, bf16[2,40,512]{2,1,0:T(8,128)(2,1)}, bf16[32,1024]{1,0:T(8,128)(2,1)}, f32[32,1024]{1,0:T(8,128)}, bf16[32,102...) custom-call(s32[2,512]{1,0:T(2,128)} %refs_0_.8, ...), custom_call_target="tpu_custom_call" | custom-call | tf_op jit(solution)/shard_map/rows/pallas_call | solution.py:686
  154.1 1.3 collective-permute-start.30
  156.0 1.0 copy-done.35
  157.0 1.0 copy-done.37
  158.0 3.2 %preload.1 = (bf16[1024,2048]{1,0:T(8,128)(2,1)S(1)}, bf16[2048,1024]{1,0:T(8,128)(2,1)S(1)}) custom-call(s32[8,2,8]{2,1,0:T(2,128)S(1)} %copy-done.50, bf16[32,1024]{1,0:T(8,128)(2,1)S(1)} %copy-done.41, bf16[128,2048]{1,0:T(8,128)(2,1)S(1)} %copy-done.48, bf16[128,2048]{1,0:T(8,128)(2,1)} %after.18.refs_3_, bf16[128,2048]{1,0:T(8,128)(2,1)} %after.19.refs_4_, ...), custom_call_target="tpu_custom_call" | custom-call | tf_op jit(solution)/shard_map/preload/pallas_call | solution.py:686
  161.3 1.0 collective-permute-done.36.refs_7_
  162.2 5.6 %collective-permute-done.30.refs_6_ = bf16[128,2048]{1,0:T(8,128)(2,1)S(1)} collective-permute-done((bf16[128,2048]{1,0:T(8,128)(2,1)}, bf16[128,2048]{1,0:T(8,128)(2,1)S(1)}, u32[]{:S(2)}, u32[]{:S(2)}) %collective-permute-start.30) | collective-permute-done | bytes 524320 | tf_op jit(solution)/shard_map/ppermute | solution.py:754
  167.9 3.1 %ffn.1 = (f32[64,2048]{1,0:T(8,128)S(1)}, bf16[64,2048]{1,0:T(8,128)(2,1)S(1)}, bf16[1024,2048]{1,0:T(8,128)(2,1)S(1)}, bf16[2048,1024]{1,0:T(8,128)(2,1)S(1)}, ...) custom-call(s32[8,2,8]{2,1,0:T(2,128)S(1)} %copy-done.50, ...), custom_call_target="tpu_custom_call", output_to_operand_aliasing={{2}: (8, {}), {3}: (9, {})} | custom-call | tf_op jit(solution)/shard_map/ffn/pallas_call | solution.py:686
  171.1 1.4 collective-permute-done.37.refs_2_
  173.5 1.5 collective-permute-start.39
  175.2 2.0 collective-permute-done.39.refs_2_
  177.2 0.9 collective-permute-done.40.refs_3_
  180.5 2.9 %ffn_back.1 = (f32[32,1152]{1,0:T(8,128)S(1)}, f32[32,1152]{1,0:T(8,128)S(1)}, bf16[64,2048]{1,0:T(8,128)(2,1)S(1)}) custom-call(bf16[32,1152]{1,0:T(8,128)(2,1)S(1)} %get-tuple-element.102.refs_0_, bf16[32,1152]{1,0:T(8,128)(2,1)S(1)} %collective-permute-done.41.refs_1_, f32[64,2048]{1,0:T(8,128)S(1)} %slope.1.refs_2_, ...), custom_call_target="tpu_custom_call" | custom-call | tf_op jit(solution)/shard_map/ffn_back/pallas_call | solution.py:686
  185.7 2.4 %collective-permute-start.47 = (f32[8,4096]{1,0:T(8,128)S(1)}, f32[8,4096]{1,0:T(8,128)S(1)}, u32[]{:S(2)}, u32[]{:S(2)}) collective-permute-start(f32[8,4096]{1,0:T(8,128)S(1)} %get-tuple-element.122), channel_id=1, source_target_pairs={{0,16},{1,17},{2,18},{3,19},{4,20},{5,21},{6,22},{7,23},{8,24},{9,... | collective-permute-start | bytes 393224 | tf_op jit(solution)/shard_map/ppermute | solution.py:754
  188.2 6.8 %rows_back.1 = (f32[2,40,1024]{2,1,0:T(8,128)S(1)}, f32[24,1024]{1,0:T(8,128)S(1)}) custom-call(f32[32,1152]{1,0:T(8,128)S(1)} %get-tuple-element.106.refs_0_, f32[32,1152]{1,0:T(8,128)S(1)} %collective-permute-done.42.refs_1_, f32[32,1024]{1,0:T(8,128)S(1)} %get-tuple-element.108.refs_2_, f32[40,1024]{1,0:T(8,128)S(1)} %get-tuple-element.109.refs_3_, ...), custom_call_target="tpu_custom_call" | custom-call | tf_op jit(solution)/shard_map/rows_back/pallas_call | solution.py:686
  195.6 1.7 collective-permute-start.48
  197.2 2.6 %collective-permute-done.43 = f32[24,1024]{1,0:T(8,128)S(1)} collective-permute-done((f32[24,1024]{1,0:T(8,128)S(1)}, f32[24,1024]{1,0:T(8,128)S(1)}, u32[]{:S(2)}, u32[]{:S(2)}) %collective-permute-start.43) | collective-permute-done | bytes 98336 | tf_op jit(solution)/shard_map/ppermute | solution.py:754
  199.8 1.6 collective-permute-start.44
  201.4 1.7 collective-permute-start.49
  203.1 1.4 collective-permute-done.44
  205.1 5.0 %collective-permute-done.45.refs_1_ = f32[24,1024]{1,0:T(8,128)S(1)} collective-permute-done((f32[24,1024]{1,0:T(8,128)S(1)}, f32[24,1024]{1,0:T(8,128)S(1)}, u32[]{:S(2)}, u32[]{:S(2)}) %collective-permute-start.45) | collective-permute-done | bytes 98336 | tf_op jit(solution)/shard_map/ppermute | solution.py:754
  210.1 3.1 %ortho.1 = (f32[2,8,1024]{2,1,0:T(8,128)S(1)}, f32[8,4096]{1,0:T(8,128)S(1)}, f32[1,1024]{1,0:T(1,128)S(1)}, f32[32,8,128]{2,1,0:T(8,128)}) custom-call(f32[24,1024]{1,0:T(8,128)S(1)} %add.99.refs_0_, f32[24,1024]{1,0:T(8,128)S(1)} %collective-permute-done.45.refs_1_, f32[8,4096]{1,0:T(8,128)S(1)} %add.101.refs_2_, ...), custom_call_target="tpu_custom_call" | custom-call | tf_op jit(solution)/shard_map/ortho/pallas_call | solution.py:686
  213.2 3.0 %all-to-all-start = ((f32[32,8,128]{2,1,0:T(8,128)}), f32[32,8,128]{2,1,0:T(8,128)S(1)}, u32[]{:S(2)}, u32[]{:S(2)}) async-start(f32[32,8,128]{2,1,0:T(8,128)} %get-tuple-element.125), calls=%async_computation | async-start | bytes 262144 | tf_op jit(solution)/shard_map/all_to_all | solution.py:1020
  216.3 8.2 %all-to-all-done.refs_0_ = f32[32,8,128]{2,1,0:T(8,128)S(1)} async-done(((f32[32,8,128]{2,1,0:T(8,128)}), f32[32,8,128]{2,1,0:T(8,128)S(1)}, u32[]{:S(2)}, u32[]{:S(2)}) %all-to-all-start) | async-done | bytes 131104 | tf_op jit(solution)/shard_map/all_to_all | solution.py:1020
  224.5 2.3 %final.1 = (f32[2,40,128]{2,1,0:T(8,128)}, f32[16,512]{1,0:T(8,128)}, f32[1,128]{1,0:T(1,128)}, f32[2,40,128]{2,1,0:T(8,128)}, f32[16,512]{1,0:T(8,128)}, /*inde...) custom-call(f32[32,8,128]{2,1,0:T(8,128)S(1)} %all-to-all-done.refs_, ...), custom_call_target="tpu_custom_call" | custom-call | tf_op jit(solution)/shard_map/final/pallas_call | solution.py:686
  (251 shorter events, 32.3 us)
Async XLA Ops:
  4.7 28.1 %collective-permute-start = (bf16[144,1024]{1,0:T(8,128)(2,1)}, bf16[144,1024]{1,0:T(8,128)(2,1)S(1)}, u32[]{:S(2)}, u32[]{:S(2)}) collective-permute-start(bf16[144,1024]{1,0:T(8,128)(2,1)} %get-tuple-element.77.refs_1_), channel_id=1, source_target_pairs={{0,4},{1,9},{2,6},{3,11},{4,12},{5,1},{6,14},{7,3},{8,0},{9,17},{1... | collective-permute-start | bytes 884744 | tf_op jit(solution)/shard_map/ppermute | solution.py:754
  7.8 25.1 %collective-permute-start.1 = (bf16[144,1024]{1,0:T(8,128)(2,1)}, bf16[144,1024]{1,0:T(8,128)(2,1)S(1)}, u32[]{:S(2)}, u32[]{:S(2)}) collective-permute-start(bf16[144,1024]{1,0:T(8,128)(2,1)} %get-tuple-element.78.refs_9_.refs_1_), channel_id=1, source_target_pairs={{0,4},{1,9},{2,6},{3,11},{4,12},{5,1},{6,14},{7,3},{8,0},{9,17},{1... | collective-permute-start | bytes 884744 | tf_op jit(solution)/shard_map/ppermute | solution.py:754
  9.3 24.0 %collective-permute-start.2 = (bf16[128,2048]{1,0:T(8,128)(2,1)}, bf16[128,2048]{1,0:T(8,128)(2,1)}, u32[]{:S(2)}, u32[]{:S(2)}) collective-permute-start(bf16[128,2048]{1,0:T(8,128)(2,1)} %get-tuple-element.79.refs_2_), channel_id=1, source_target_pairs={{0,4},{1,9},{2,6},{3,11},{4,12},{5,1},{6,14},{7,3},{8,0},{9,17},{1... | collective-permute-start | bytes 1572872 | tf_op jit(solution)/shard_map/ppermute | solution.py:754
  10.9 22.4 %collective-permute-start.3 = (bf16[256,1024]{1,0:T(8,128)(2,1)}, bf16[256,1024]{1,0:T(8,128)(2,1)}, u32[]{:S(2)}, u32[]{:S(2)}) collective-permute-start(bf16[256,1024]{1,0:T(8,128)(2,1)} %get-tuple-element.80.refs_9_), channel_id=1, source_target_pairs={{0,4},{1,9},{2,6},{3,11},{4,12},{5,1},{6,14},{7,3},{8,0},{9,17},{1... | collective-permute-start | bytes 1572872 | tf_op jit(solution)/shard_map/ppermute | solution.py:754
  34.0 11.3 %collective-permute-start.4 = (bf16[512,1024]{1,0:T(8,128)(2,1)}, bf16[512,1024]{1,0:T(8,128)(2,1)S(1)}, u32[]{:S(2)}, u32[]{:S(2)}) collective-permute-start(bf16[512,1024]{1,0:T(8,128)(2,1)} %after.15), channel_id=1, source_target_pairs={{0,1},{1,0},{2,3},{3,2},{4,5},{5,4},{6,7},{7,6},{8,9},{9,8},{10,11... | collective-permute-start | bytes 3145736 | tf_op jit(solution)/shard_map/ppermute | solution.py:754
  34.7 7.0 %collective-permute-start.7 = (bf16[144,1024]{1,0:T(8,128)(2,1)}, bf16[144,1024]{1,0:T(8,128)(2,1)S(1)}, u32[]{:S(2)}, u32[]{:S(2)}) collective-permute-start(bf16[144,1024]{1,0:T(8,128)(2,1)} %copy-done.7), channel_id=1, source_target_pairs={{0,4},{1,9},{2,6},{3,11},{4,12},{5,1},{6,14},{7,3},{8,0},{9,17},{1... | collective-permute-start | bytes 884744 | tf_op jit(solution)/shard_map/ppermute | solution.py:754
  35.2 9.6 %collective-permute-start.13 = (bf16[144,1024]{1,0:T(8,128)(2,1)}, bf16[144,1024]{1,0:T(8,128)(2,1)S(1)}, u32[]{:S(2)}, u32[]{:S(2)}) collective-permute-start(bf16[144,1024]{1,0:T(8,128)(2,1)} %copy-done.9), channel_id=1, source_target_pairs={{0,4},{1,9},{2,6},{3,11},{4,12},{5,1},{6,14},{7,3},{8,0},{9,17},{1... | collective-permute-start | bytes 884744 | tf_op jit(solution)/shard_map/ppermute | solution.py:754
  41.7 47.6 %copy-start.21 = (bf16[144,1024]{1,0:T(8,128)(2,1)}, bf16[144,1024]{1,0:T(8,128)(2,1)S(1)}, u32[]{:S(2)}) copy-start(bf16[144,1024]{1,0:T(8,128)(2,1)S(1)} %collective-permute-done.7.refs_3_) | copy-start | bytes 884740
  41.7 6.7 %collective-permute-start.8 = (bf16[144,1024]{1,0:T(8,128)(2,1)S(1)}, bf16[144,1024]{1,0:T(8,128)(2,1)S(1)}, u32[]{:S(2)}, u32[]{:S(2)}) collective-permute-start(bf16[144,1024]{1,0:T(8,128)(2,1)S(1)} %collective-permute-done.7.refs_3_), channel_id=1, source_target_pairs={{0,4},{1,9},{2,6},{3,11},{4,12},{5,1},{6,14},{7,3},{8,0},{9,17},{1... | collective-permute-start | bytes 884744 | tf_op jit(solution)/shard_map/ppermute | solution.py:754
  44.8 59.2 %copy-start.23 = (bf16[144,1024]{1,0:T(8,128)(2,1)}, bf16[144,1024]{1,0:T(8,128)(2,1)S(1)}, u32[]{:S(2)}) copy-start(bf16[144,1024]{1,0:T(8,128)(2,1)S(1)} %collective-permute-done.13.refs_11_.refs_3_) | copy-start | bytes 884740
  44.8 6.7 %collective-permute-start.14 = (bf16[144,1024]{1,0:T(8,128)(2,1)S(1)}, bf16[144,1024]{1,0:T(8,128)(2,1)S(1)}, u32[]{:S(2)}, u32[]{:S(2)}) collective-permute-start(bf16[144,1024]{1,0:T(8,128)(2,1)S(1)} %collective-permute-done.13.refs_11_.refs_3_), channel_id=1, source_target_pairs={{0,4},{1,9},{2,6},{3,11},{4,12},{5,1},{6,14},{7,3},{8,0},{9,17},{1... | collective-permute-start | bytes 884744 | tf_op jit(solution)/shard_map/ppermute | solution.py:754
  49.1 6.9 %collective-permute-start.9 = (bf16[144,1024]{1,0:T(8,128)(2,1)}, bf16[144,1024]{1,0:T(8,128)(2,1)S(1)}, u32[]{:S(2)}, u32[]{:S(2)}) collective-permute-start(bf16[144,1024]{1,0:T(8,128)(2,1)} %after.16.refs_4_), channel_id=1, source_target_pairs={{0,4},{1,9},{2,6},{3,11},{4,12},{5,1},{6,14},{7,3},{8,0},{9,17},{1... | collective-permute-start | bytes 884744 | tf_op jit(solution)/shard_map/ppermute | solution.py:754
  52.3 7.0 %collective-permute-start.15 = (bf16[144,1024]{1,0:T(8,128)(2,1)}, bf16[144,1024]{1,0:T(8,128)(2,1)S(1)}, u32[]{:S(2)}, u32[]{:S(2)}) collective-permute-start(bf16[144,1024]{1,0:T(8,128)(2,1)} %after.17.refs_12_.refs_4_), channel_id=1, source_target_pairs={{0,4},{1,9},{2,6},{3,11},{4,12},{5,1},{6,14},{7,3},{8,0},{9,17},{1... | collective-permute-start | bytes 884744 | tf_op jit(solution)/shard_map/ppermute | solution.py:754
  52.8 24.3 %collective-permute-start.5 = (bf16[512,1024]{1,0:T(8,128)(2,1)}, bf16[512,1024]{1,0:T(8,128)(2,1)}, u32[]{:S(2)}, u32[]{:S(2)}) collective-permute-start(bf16[512,1024]{1,0:T(8,128)(2,1)} %fusion.refs_0_.refs_1_), channel_id=1, source_target_pairs={{0,2},{1,3},{2,0},{3,1},{4,6},{5,7},{6,4},{7,5},{8,10},{9,11},{10,... | collective-permute-start | bytes 3145736 | tf_op jit(solution)/shard_map/ppermute | solution.py:754
  56.1 33.2 %copy-start.24 = (bf16[144,1024]{1,0:T(8,128)(2,1)}, bf16[144,1024]{1,0:T(8,128)(2,1)S(1)}, u32[]{:S(2)}) copy-start(bf16[144,1024]{1,0:T(8,128)(2,1)S(1)} %collective-permute-done.9.refs_5_) | copy-start | bytes 884740
  56.1 6.8 %collective-permute-start.10 = (bf16[144,1024]{1,0:T(8,128)(2,1)S(1)}, bf16[144,1024]{1,0:T(8,128)(2,1)}, u32[]{:S(2)}, u32[]{:S(2)}) collective-permute-start(bf16[144,1024]{1,0:T(8,128)(2,1)S(1)} %collective-permute-done.9.refs_5_), channel_id=1, source_target_pairs={{0,4},{1,9},{2,6},{3,11},{4,12},{5,1},{6,14},{7,3},{8,0},{9,17},{1... | collective-permute-start | bytes 884744 | tf_op jit(solution)/shard_map/ppermute | solution.py:754
  59.2 6.7 %collective-permute-start.16 = (bf16[144,1024]{1,0:T(8,128)(2,1)S(1)}, bf16[144,1024]{1,0:T(8,128)(2,1)S(1)}, u32[]{:S(2)}, u32[]{:S(2)}) collective-permute-start(bf16[144,1024]{1,0:T(8,128)(2,1)S(1)} %collective-permute-done.15.refs_13_.refs_5_), channel_id=1, source_target_pairs={{0,4},{1,9},{2,6},{3,11},{4,12},{5,1},{6,14},{7,3},{8,0},{9,17},{1... | collective-permute-start | bytes 884744 | tf_op jit(solution)/shard_map/ppermute | solution.py:754
  62.9 6.9 %collective-permute-start.11 = (bf16[144,1024]{1,0:T(8,128)(2,1)}, bf16[144,1024]{1,0:T(8,128)(2,1)S(1)}, u32[]{:S(2)}, u32[]{:S(2)}) collective-permute-start(bf16[144,1024]{1,0:T(8,128)(2,1)} %collective-permute-done.10.refs_6_.refs_1_), channel_id=1, source_target_pairs={{0,4},{1,9},{2,6},{3,11},{4,12},{5,1},{6,14},{7,3},{8,0},{9,17},{1... | collective-permute-start | bytes 884744 | tf_op jit(solution)/shard_map/ppermute | solution.py:754
  66.0 7.1 %collective-permute-start.17 = (bf16[144,1024]{1,0:T(8,128)(2,1)S(1)}, bf16[144,1024]{1,0:T(8,128)(2,1)}, u32[]{:S(2)}, u32[]{:S(2)}) collective-permute-start(bf16[144,1024]{1,0:T(8,128)(2,1)S(1)} %collective-permute-done.16.refs_14_.refs_6_), channel_id=1, source_target_pairs={{0,4},{1,9},{2,6},{3,11},{4,12},{5,1},{6,14},{7,3},{8,0},{9,17},{1... | collective-permute-start | bytes 884744 | tf_op jit(solution)/shard_map/ppermute | solution.py:754
  66.5 20.9 %copy-start.8 = (bf16[144,1024]{1,0:T(8,128)(2,1)S(1)}, bf16[144,1024]{1,0:T(8,128)(2,1)}, u32[]{:S(2)}) copy-start(bf16[144,1024]{1,0:T(8,128)(2,1)} %copy-done.7) | copy-start | bytes 884740
  66.5 20.9 %copy-start.14 = (bf16[144,1024]{1,0:T(8,128)(2,1)S(1)}, bf16[144,1024]{1,0:T(8,128)(2,1)}, u32[]{:S(2)}) copy-start(bf16[144,1024]{1,0:T(8,128)(2,1)} %after.16.refs_4_) | copy-start | bytes 884740
  66.5 20.9 %copy-start.15 = (bf16[144,1024]{1,0:T(8,128)(2,1)S(1)}, bf16[144,1024]{1,0:T(8,128)(2,1)}, u32[]{:S(2)}) copy-start(bf16[144,1024]{1,0:T(8,128)(2,1)} %get-tuple-element.77.refs_1_) | copy-start | bytes 884740
  66.5 20.9 %copy-start.50 = (s32[8,2,8]{2,1,0:T(2,128)S(1)}, s32[8,2,8]{2,1,0:T(2,128)}, u32[]{:S(2)}) copy-start(s32[8,2,8]{2,1,0:T(2,128)} %constant.86.clone.refs_0_) | copy-start | bytes 1540
  66.5 26.6 %collective-permute-start.31 = (bf16[256,1024]{1,0:T(8,128)(2,1)}, bf16[256,1024]{1,0:T(8,128)(2,1)S(1)}, u32[]{:S(2)}, u32[]{:S(2)}) collective-permute-start(bf16[256,1024]{1,0:T(8,128)(2,1)} %after.23.refs_10_), channel_id=1, source_target_pairs={{0,4},{1,9},{2,6},{3,11},{4,12},{5,1},{6,14},{7,3},{8,0},{9,17},{1... | collective-permute-start | bytes 1572872 | tf_op jit(solution)/shard_map/ppermute | solution.py:754
  67.0 27.5 %collective-permute-start.25 = (bf16[128,2048]{1,0:T(8,128)(2,1)}, bf16[128,2048]{1,0:T(8,128)(2,1)}, u32[]{:S(2)}, u32[]{:S(2)}) collective-permute-start(bf16[128,2048]{1,0:T(8,128)(2,1)} %after.18.refs_3_), channel_id=1, source_target_pairs={{0,4},{1,9},{2,6},{3,11},{4,12},{5,1},{6,14},{7,3},{8,0},{9,17},{1... | collective-permute-start | bytes 1572872 | tf_op jit(solution)/shard_map/ppermute | solution.py:754
  69.8 17.6 %collective-permute-start.12 = (bf16[144,1024]{1,0:T(8,128)(2,1)S(1)}, bf16[144,1024]{1,0:T(8,128)(2,1)S(1)}, u32[]{:S(2)}, u32[]{:S(2)}) collective-permute-start(bf16[144,1024]{1,0:T(8,128)(2,1)S(1)} %collective-permute-done.11.refs_7_), channel_id=1, source_target_pairs={{0,4},{1,9},{2,6},{3,11},{4,12},{5,1},{6,14},{7,3},{8,0},{9,17},{1... | collective-permute-start | bytes 884744 | tf_op jit(solution)/shard_map/ppermute | solution.py:754
  73.1 21.8 %collective-permute-start.18 = (bf16[144,1024]{1,0:T(8,128)(2,1)}, bf16[144,1024]{1,0:T(8,128)(2,1)}, u32[]{:S(2)}, u32[]{:S(2)}) collective-permute-start(bf16[144,1024]{1,0:T(8,128)(2,1)} %collective-permute-done.17.refs_15_.refs_7_), channel_id=1, source_target_pairs={{0,4},{1,9},{2,6},{3,11},{4,12},{5,1},{6,14},{7,3},{8,0},{9,17},{1... | collective-permute-start | bytes 884744 | tf_op jit(solution)/shard_map/ppermute | solution.py:754
  80.0 35.0 %collective-permute-start.6 = (bf16[512,1024]{1,0:T(8,128)(2,1)}, bf16[512,1024]{1,0:T(8,128)(2,1)}, u32[]{:S(2)}, u32[]{:S(2)}) collective-permute-start(bf16[512,1024]{1,0:T(8,128)(2,1)} %add.91), channel_id=1, source_target_pairs={{0,1},{1,0},{2,3},{3,2},{4,5},{5,4},{6,7},{7,6},{8,9},{9,8},{10,11... | collective-permute-start | bytes 3145736 | tf_op jit(solution)/shard_map/ppermute | solution.py:754
  94.0 13.0 %collective-permute-start.32 = (bf16[256,1024]{1,0:T(8,128)(2,1)}, bf16[256,1024]{1,0:T(8,128)(2,1)}, u32[]{:S(2)}, u32[]{:S(2)}) collective-permute-start(bf16[256,1024]{1,0:T(8,128)(2,1)} %after.24.refs_11_), channel_id=1, source_target_pairs={{0,4},{1,9},{2,6},{3,11},{4,12},{5,1},{6,14},{7,3},{8,0},{9,17},{1... | collective-permute-start | bytes 1572872 | tf_op jit(solution)/shard_map/ppermute | solution.py:754
  94.5 14.6 %collective-permute-start.26 = (bf16[128,2048]{1,0:T(8,128)(2,1)}, bf16[128,2048]{1,0:T(8,128)(2,1)}, u32[]{:S(2)}, u32[]{:S(2)}) collective-permute-start(bf16[128,2048]{1,0:T(8,128)(2,1)} %after.19.refs_4_), channel_id=1, source_target_pairs={{0,4},{1,9},{2,6},{3,11},{4,12},{5,1},{6,14},{7,3},{8,0},{9,17},{1... | collective-permute-start | bytes 1572872 | tf_op jit(solution)/shard_map/ppermute | solution.py:754
  99.0 23.6 %collective-permute-start.22 = (bf16[1024,512]{1,0:T(8,128)(2,1)S(1)}, bf16[1024,512]{1,0:T(8,128)(2,1)}, u32[]{:S(2)}, u32[]{:S(2)}) collective-permute-start(bf16[1024,512]{1,0:T(8,128)(2,1)S(1)} %assemble.7.refs_13_.refs_2_), channel_id=1, source_target_pairs={{0,1},{1,0},{2,3},{3,2},{4,5},{5,4},{6,7},{7,6},{8,9},{9,8},{10,11... | collective-permute-start | bytes 3145736 | tf_op jit(solution)/shard_map/ppermute | solution.py:754
  107.0 12.8 %collective-permute-start.33 = (bf16[256,1024]{1,0:T(8,128)(2,1)}, bf16[256,1024]{1,0:T(8,128)(2,1)}, u32[]{:S(2)}, u32[]{:S(2)}) collective-permute-start(bf16[256,1024]{1,0:T(8,128)(2,1)} %after.25.refs_12_), channel_id=1, source_target_pairs={{0,4},{1,9},{2,6},{3,11},{4,12},{5,1},{6,14},{7,3},{8,0},{9,17},{1... | collective-permute-start | bytes 1572872 | tf_op jit(solution)/shard_map/ppermute | solution.py:754
  109.1 13.0 %collective-permute-start.27 = (bf16[128,2048]{1,0:T(8,128)(2,1)}, bf16[128,2048]{1,0:T(8,128)(2,1)}, u32[]{:S(2)}, u32[]{:S(2)}) collective-permute-start(bf16[128,2048]{1,0:T(8,128)(2,1)} %after.20.refs_5_), channel_id=1, source_target_pairs={{0,4},{1,9},{2,6},{3,11},{4,12},{5,1},{6,14},{7,3},{8,0},{9,17},{1... | collective-permute-start | bytes 1572872 | tf_op jit(solution)/shard_map/ppermute | solution.py:754
  109.6 28.1 %collective-permute-start.21 = (bf16[1024,512]{1,0:T(8,128)(2,1)}, bf16[1024,512]{1,0:T(8,128)(2,1)}, u32[]{:S(2)}, u32[]{:S(2)}) collective-permute-start(bf16[1024,512]{1,0:T(8,128)(2,1)} %assemble.6.refs_12_.refs_1_), channel_id=1, source_target_pairs={{0,1},{1,0},{2,3},{3,2},{4,5},{5,4},{6,7},{7,6},{8,9},{9,8},{10,11... | collective-permute-start | bytes 3145736 | tf_op jit(solution)/shard_map/ppermute | solution.py:754
  115.0 22.7 %collective-permute-start.20 = (bf16[1024,512]{1,0:T(8,128)(2,1)S(1)}, bf16[1024,512]{1,0:T(8,128)(2,1)}, u32[]{:S(2)}, u32[]{:S(2)}) collective-permute-start(bf16[1024,512]{1,0:T(8,128)(2,1)S(1)} %copy-done.1), channel_id=1, source_target_pairs={{0,1},{1,0},{2,3},{3,2},{4,5},{5,4},{6,7},{7,6},{8,9},{9,8},{10,11... | collective-permute-start | bytes 3145736 | tf_op jit(solution)/shard_map/ppermute | solution.py:754
  119.7 18.0 %collective-permute-start.19 = (bf16[1024,512]{1,0:T(8,128)(2,1)S(1)}, bf16[1024,512]{1,0:T(8,128)(2,1)}, u32[]{:S(2)}, u32[]{:S(2)}) collective-permute-start(bf16[1024,512]{1,0:T(8,128)(2,1)S(1)} %copy-done.3), channel_id=1, source_target_pairs={{0,1},{1,0},{2,3},{3,2},{4,5},{5,4},{6,7},{7,6},{8,9},{9,8},{10,11... | collective-permute-start | bytes 3145736 | tf_op jit(solution)/shard_map/ppermute | solution.py:754
  122.1 9.5 %collective-permute-start.34 = (bf16[256,1024]{1,0:T(8,128)(2,1)}, bf16[256,1024]{1,0:T(8,128)(2,1)}, u32[]{:S(2)}, u32[]{:S(2)}) collective-permute-start(bf16[256,1024]{1,0:T(8,128)(2,1)} %after.26.refs_13_), channel_id=1, source_target_pairs={{0,4},{1,9},{2,6},{3,11},{4,12},{5,1},{6,14},{7,3},{8,0},{9,17},{1... | collective-permute-start | bytes 1572872 | tf_op jit(solution)/shard_map/ppermute | solution.py:754
  122.6 14.6 %collective-permute-start.28 = (bf16[128,2048]{1,0:T(8,128)(2,1)}, bf16[128,2048]{1,0:T(8,128)(2,1)}, u32[]{:S(2)}, u32[]{:S(2)}) collective-permute-start(bf16[128,2048]{1,0:T(8,128)(2,1)} %after.21.refs_6_), channel_id=1, source_target_pairs={{0,4},{1,9},{2,6},{3,11},{4,12},{5,1},{6,14},{7,3},{8,0},{9,17},{1... | collective-permute-start | bytes 1572872 | tf_op jit(solution)/shard_map/ppermute | solution.py:754
  131.6 20.4 %collective-permute-start.35 = (bf16[256,1024]{1,0:T(8,128)(2,1)}, bf16[256,1024]{1,0:T(8,128)(2,1)S(1)}, u32[]{:S(2)}, u32[]{:S(2)}) collective-permute-start(bf16[256,1024]{1,0:T(8,128)(2,1)} %collective-permute-done.34.refs_14_), channel_id=1, source_target_pairs={{0,4},{1,9},{2,6},{3,11},{4,12},{5,1},{6,14},{7,3},{8,0},{9,17},{1... | collective-permute-start | bytes 1572872 | tf_op jit(solution)/shard_map/ppermute | solution.py:754
  137.2 16.1 %collective-permute-start.29 = (bf16[128,2048]{1,0:T(8,128)(2,1)}, bf16[128,2048]{1,0:T(8,128)(2,1)S(1)}, u32[]{:S(2)}, u32[]{:S(2)}) collective-permute-start(bf16[128,2048]{1,0:T(8,128)(2,1)} %collective-permute-done.28.refs_7_), channel_id=1, source_target_pairs={{0,4},{1,9},{2,6},{3,11},{4,12},{5,1},{6,14},{7,3},{8,0},{9,17},{1... | collective-permute-start | bytes 1572872 | tf_op jit(solution)/shard_map/ppermute | solution.py:754
  152.8 9.4 %collective-permute-start.36 = (bf16[256,1024]{1,0:T(8,128)(2,1)}, bf16[256,1024]{1,0:T(8,128)(2,1)S(1)}, u32[]{:S(2)}, u32[]{:S(2)}) collective-permute-start(bf16[256,1024]{1,0:T(8,128)(2,1)} %after.27.refs_15_), channel_id=1, source_target_pairs={{0,4},{1,9},{2,6},{3,11},{4,12},{5,1},{6,14},{7,3},{8,0},{9,17},{1... | collective-permute-start | bytes 1572872 | tf_op jit(solution)/shard_map/ppermute | solution.py:754
  154.1 13.8 %collective-permute-start.30 = (bf16[128,2048]{1,0:T(8,128)(2,1)}, bf16[128,2048]{1,0:T(8,128)(2,1)S(1)}, u32[]{:S(2)}, u32[]{:S(2)}) collective-permute-start(bf16[128,2048]{1,0:T(8,128)(2,1)} %after.22.refs_8_), channel_id=1, source_target_pairs={{0,4},{1,9},{2,6},{3,11},{4,12},{5,1},{6,14},{7,3},{8,0},{9,17},{1... | collective-permute-start | bytes 1572872 | tf_op jit(solution)/shard_map/ppermute | solution.py:754
  155.4 5.8 %collective-permute-start.23 = (bf16[32,1152]{1,0:T(8,128)(2,1)S(1)}, bf16[32,1152]{1,0:T(8,128)(2,1)S(1)}, u32[]{:S(2)}, u32[]{:S(2)}) collective-permute-start(bf16[32,1152]{1,0:T(8,128)(2,1)S(1)} %copy-done.43), channel_id=1, source_target_pairs={{0,1},{1,0},{2,3},{3,2},{4,5},{5,4},{6,7},{7,6},{8,9},{9,8},{10,11... | collective-permute-start | bytes 221192 | tf_op jit(solution)/shard_map/ppermute | solution.py:754
  155.4 5.8 %collective-permute-start.24 = (bf16[16,2048]{1,0:T(8,128)(2,1)S(1)}, bf16[16,2048]{1,0:T(8,128)(2,1)S(1)}, u32[]{:S(2)}, u32[]{:S(2)}) collective-permute-start(bf16[16,2048]{1,0:T(8,128)(2,1)S(1)} %copy-done.68), channel_id=1, source_target_pairs={{0,1},{1,0},{2,3},{3,2},{4,5},{5,4},{6,7},{7,6},{8,9},{9,8},{10,11... | collective-permute-start | bytes 196616 | tf_op jit(solution)/shard_map/ppermute | solution.py:754
  171.0 1.4 collective-permute-start.37
  173.3 1.9 collective-permute-start.38
  173.5 3.8 %collective-permute-start.39 = (f32[32,128]{1,0:T(8,128)S(1)}, f32[32,128]{1,0:T(8,128)S(1)}, u32[]{:S(2)}, u32[]{:S(2)}) collective-permute-start(f32[32,128]{1,0:T(8,128)S(1)} %get-tuple-element.98.refs_0_.refs_1_), channel_id=1, source_target_pairs={{0,2},{1,3},{2,0},{3,1},{4,6},{5,7},{6,4},{7,5},{8,10},{9,11},{10,... | collective-permute-start | bytes 49160 | tf_op jit(solution)/shard_map/ppermute | solution.py:754
  175.0 3.2 %collective-permute-start.40 = (f32[32,128]{1,0:T(8,128)S(1)}, f32[32,128]{1,0:T(8,128)S(1)}, u32[]{:S(2)}, u32[]{:S(2)}) collective-permute-start(f32[32,128]{1,0:T(8,128)S(1)} %get-tuple-element.98.refs_0_.refs_1_), channel_id=1, source_target_pairs={{0,3},{1,2},{2,1},{3,0},{4,7},{5,6},{6,5},{7,4},{8,11},{9,10},{10,... | collective-permute-start | bytes 49160 | tf_op jit(solution)/shard_map/ppermute | solution.py:754
  179.1 1.3 collective-permute-start.41
  183.8 1.4 collective-permute-start.46
  184.0 4.1 %collective-permute-start.42 = (f32[32,1152]{1,0:T(8,128)S(1)}, f32[32,1152]{1,0:T(8,128)S(1)}, u32[]{:S(2)}, u32[]{:S(2)}) collective-permute-start(f32[32,1152]{1,0:T(8,128)S(1)} %get-tuple-element.107), channel_id=1, source_target_pairs={{0,1},{1,0},{2,3},{3,2},{4,5},{5,4},{6,7},{7,6},{8,9},{9,8},{10,11... | collective-permute-start | bytes 442376 | tf_op jit(solution)/shard_map/ppermute | solution.py:754
  185.7 9.9 %collective-permute-start.47 = (f32[8,4096]{1,0:T(8,128)S(1)}, f32[8,4096]{1,0:T(8,128)S(1)}, u32[]{:S(2)}, u32[]{:S(2)}) collective-permute-start(f32[8,4096]{1,0:T(8,128)S(1)} %get-tuple-element.122), channel_id=1, source_target_pairs={{0,16},{1,17},{2,18},{3,19},{4,20},{5,21},{6,22},{7,23},{8,24},{9,... | collective-permute-start | bytes 393224 | tf_op jit(solution)/shard_map/ppermute | solution.py:754
  195.0 29.4 %copy-start.53 = (f32[1,128,2,40]{1,3,2,0:T(8,128)S(1)}, f32[1,128,2,40]{1,3,2,0:T(8,128)}, u32[]{:S(2)}) copy-start(f32[1,128,2,40]{1,3,2,0:T(8,128)} %param.35) | copy-start | bytes 122884
  195.0 29.4 %copy-start.55 = (f32[1,512,16]{1,2,0:T(8,128)S(1)}, f32[1,512,16]{1,2,0:T(8,128)}, u32[]{:S(2)}) copy-start(f32[1,512,16]{1,2,0:T(8,128)} %param.36) | copy-start | bytes 98308
  195.1 29.4 %copy-start.58 = (f32[1,128,2,40]{1,3,2,0:T(8,128)S(1)}, f32[1,128,2,40]{1,3,2,0:T(8,128)}, u32[]{:S(2)}) copy-start(f32[1,128,2,40]{1,3,2,0:T(8,128)} %param.38) | copy-start | bytes 122884
  195.1 29.4 %copy-start.59 = (f32[1,512,16]{1,2,0:T(8,128)S(1)}, f32[1,512,16]{1,2,0:T(8,128)}, u32[]{:S(2)}) copy-start(f32[1,512,16]{1,2,0:T(8,128)} %param.39) | copy-start | bytes 98308
  195.1 29.4 %copy-start.64 = (f32[1,128]{1,0:T(1,128)S(1)}, f32[1,128]{1,0:T(1,128)}, u32[]{:S(2)}) copy-start(f32[1,128]{1,0:T(1,128)} %refs_10_.1) | copy-start | bytes 1540
  195.1 29.4 %copy-start.65 = (f32[1,128]{1,0:T(1,128)S(1)}, f32[1,128]{1,0:T(1,128)}, u32[]{:S(2)}) copy-start(f32[1,128]{1,0:T(1,128)} %refs_13_.1) | copy-start | bytes 1540
  195.1 4.7 %collective-permute-start.43 = (f32[24,1024]{1,0:T(8,128)S(1)}, f32[24,1024]{1,0:T(8,128)S(1)}, u32[]{:S(2)}, u32[]{:S(2)}) collective-permute-start(f32[24,1024]{1,0:T(8,128)S(1)} %get-tuple-element.117), channel_id=1, source_target_pairs={{0,4},{1,5},{2,6},{3,7},{4,0},{5,1},{6,2},{7,3},{8,12},{9,13},{10,... | collective-permute-start | bytes 294920 | tf_op jit(solution)/shard_map/ppermute | solution.py:754
  195.6 5.8 %collective-permute-start.48 = (f32[8,4096]{1,0:T(8,128)S(1)}, f32[8,4096]{1,0:T(8,128)S(1)}, u32[]{:S(2)}, u32[]{:S(2)}) collective-permute-start(f32[8,4096]{1,0:T(8,128)S(1)} %add.100), channel_id=1, source_target_pairs={{0,8},{1,9},{2,10},{3,11},{4,12},{5,13},{6,14},{7,15},{8,0},{9,1},... | collective-permute-start | bytes 393224 | tf_op jit(solution)/shard_map/ppermute | solution.py:754
  199.8 4.7 %collective-permute-start.44 = (f32[24,1024]{1,0:T(8,128)S(1)}, f32[24,1024]{1,0:T(8,128)S(1)}, u32[]{:S(2)}, u32[]{:S(2)}) collective-permute-start(f32[24,1024]{1,0:T(8,128)S(1)} %add.98), channel_id=1, source_target_pairs={{0,8},{1,9},{2,10},{3,11},{4,12},{5,13},{6,14},{7,15},{8,0},{9,1},... | collective-permute-start | bytes 294920 | tf_op jit(solution)/shard_map/ppermute | solution.py:754
  201.4 8.7 %collective-permute-start.49 = (f32[8,4096]{1,0:T(8,128)S(1)}, f32[8,4096]{1,0:T(8,128)S(1)}, u32[]{:S(2)}, u32[]{:S(2)}) collective-permute-start(f32[8,4096]{1,0:T(8,128)S(1)} %add.101.refs_2_), channel_id=1, source_target_pairs={{0,4},{1,5},{2,6},{3,7},{4,0},{5,1},{6,2},{7,3},{8,12},{9,13},{10,... | collective-permute-start | bytes 393224 | tf_op jit(solution)/shard_map/ppermute | solution.py:754
  204.5 5.6 %collective-permute-start.45 = (f32[24,1024]{1,0:T(8,128)S(1)}, f32[24,1024]{1,0:T(8,128)S(1)}, u32[]{:S(2)}, u32[]{:S(2)}) collective-permute-start(f32[24,1024]{1,0:T(8,128)S(1)} %add.99.refs_0_), channel_id=1, source_target_pairs={{0,16},{1,17},{2,18},{3,19},{4,20},{5,21},{6,22},{7,23},{8,24},{9,... | collective-permute-start | bytes 294920 | tf_op jit(solution)/shard_map/ppermute | solution.py:754
  213.2 11.3 %all-to-all-start = ((f32[32,8,128]{2,1,0:T(8,128)}), f32[32,8,128]{2,1,0:T(8,128)S(1)}, u32[]{:S(2)}, u32[]{:S(2)}) async-start(f32[32,8,128]{2,1,0:T(8,128)} %get-tuple-element.125), calls=%async_computation | async-start | bytes 262144 | tf_op jit(solution)/shard_map/all_to_all | solution.py:1020
  (62 other events, 306.2 us)
